TPU v7x, 32 devices: a whole 2x2x4 slice. The times are simulated.
32 devices in a mesh: row: 4 (over y, x), col: 8 (over z, core).
Axes of the slice: x: 2, y: 2, z: 4, core: 2. Of those that a mesh axis runs over, the one named last changes fastest.
Arguments:
- costs: bfloat16 [128, 1024, 128], P('row', 'col'), may hold values from 0 to 63, as said below
- p_small: int32 [1], replicated, may hold values from 4 to 16
- p_large: int32 [1], replicated, may hold values from 32 to 96
Outputs:
- left_view: bfloat16 [128, 1024, 128], P('row', 'col')
- right_view: bfloat16 [128, 1024, 128], P('row', 'col')
Inputs may be any that keep to these rules, and one draw needn't show every extreme that they name: `costs`: whole numbers.
All inputs are finite; a program needn't handle non-finite values.
Results may differ from a plain program's by a relative error of at most 0.001.
Values may be sent and summed in bfloat16 or wider, within the bound.
No kernel may reach another device: no remote copies, remote signals or barrier semaphores. Data moves between devices by JAX's collectives and lax.ppermute only.
A program may use at most 64 MiB of HBM per device.

v0:
```python
import jax
import jax.numpy as jnp
from jax import lax
from jax.sharding import PartitionSpec as P


def shifted(block, axis, distance):
    devices = range(lax.axis_size(axis))
    route = [(i - distance, i) for i in devices if i - distance in devices]
    return lax.ppermute(block, axis, route)


def advance(before, here_cost, p_one, p_two):
    lowest = jnp.min(before, axis=-1, keepdims=True)
    barrier = jnp.full(before.shape[:-1] + (1,), jnp.inf, before.dtype)
    lower_side = jnp.concatenate([barrier, before[..., :-1]], axis=-1)
    upper_side = jnp.concatenate([before[..., 1:], barrier], axis=-1)
    smallest = jnp.minimum(
        jnp.minimum(before, jnp.minimum(lower_side, upper_side) + p_one), lowest + p_two
    )
    return here_cost + smallest - lowest


def run_strip(strip_costs, incoming, p_one, p_two, forward):

    def advance_one(before, here_cost):
        after = advance(before, here_cost, p_one, p_two)
        return (after, after)

    _, values = lax.scan(advance_one, incoming, strip_costs, reverse=not forward)
    final = values[-1] if forward else values[0]
    return (values, final)


def chain_step(k, state, sender, position, horizontal, forward, pieces, cost_grid, p_one, p_two):
    carry, volume = state
    incoming = sender(carry)
    strip_no = k - position
    active = jnp.logical_and(strip_no >= 0, strip_no < pieces)
    strip_at = jnp.clip(strip_no, 0, pieces - 1)
    axis_dim = 0 if horizontal else 1
    strip_size = cost_grid.shape[axis_dim] // pieces

    def active_work(operands):
        arrived, current = operands
        strip_costs = lax.dynamic_slice_in_dim(
            cost_grid, strip_at * strip_size, strip_size, axis_dim
        )
        if horizontal:
            strip_costs = jnp.transpose(strip_costs, (1, 0, 2))
        values, final = run_strip(strip_costs, arrived, p_one, p_two, forward)
        if horizontal:
            values = jnp.transpose(values, (1, 0, 2))
        return (
            final,
            lax.dynamic_update_slice_in_dim(current, values, strip_at * strip_size, axis_dim),
        )

    def passive(operands):
        return (jnp.zeros_like(operands[0]), operands[1])

    return lax.cond(active, active_work, passive, (incoming, volume))


def diagonal_view(joined, out_width):
    row_count, span_count, depth = joined.shape
    turned = jnp.transpose(joined, (0, 2, 1)).reshape(row_count, depth * span_count)
    padded = jnp.pad(turned, ((0, 0), (0, depth)))
    sheared = padded.reshape(row_count, depth, span_count + 1)[:, :, :out_width]
    return jnp.transpose(sheared, (0, 2, 1))


def send_east(carry):
    return shifted(carry, "col", 1)


def send_west(carry):
    return shifted(carry, "col", -1)


def send_south(carry):
    return shifted(carry, "row", 1)


def send_north(carry):
    return shifted(carry, "row", -1)


def shards(costs, p_small, p_large):
    cost_grid = costs.astype(jnp.float32)
    p_one = p_small[0].astype(jnp.float32)
    p_two = p_large[0].astype(jnp.float32)
    tile_rows, tile_cols, depth = cost_grid.shape
    col_count = lax.axis_size("col")
    row_count = lax.axis_size("row")
    col_here = lax.axis_index("col")
    row_here = lax.axis_index("row")
    pieces = 4
    carry_rows = jnp.zeros((tile_rows // pieces, depth), jnp.float32)
    carry_cols = jnp.zeros((tile_cols // pieces, depth), jnp.float32)
    blank_volume = jnp.zeros_like(cost_grid)
    chains = [
        (send_east, col_here, True, True, col_count + pieces - 1),
        (send_west, col_count - 1 - col_here, True, False, col_count + pieces - 1),
        (send_south, row_here, False, True, row_count + pieces - 1),
        (send_north, row_count - 1 - row_here, False, False, row_count + pieces - 1),
    ]
    starts = [
        (carry_rows, blank_volume),
        (carry_rows, blank_volume),
        (carry_cols, blank_volume),
        (carry_cols, blank_volume),
    ]
    longest = max(col_count, row_count) + pieces - 1

    def all_paths(k, states):
        return tuple(
            (
                chain_step(
                    k,
                    state,
                    chain[0],
                    chain[1],
                    chain[2],
                    chain[3],
                    pieces,
                    cost_grid,
                    p_one,
                    p_two,
                )
                for state, chain in zip(states, chains)
            )
        )

    finals = lax.fori_loop(0, longest, all_paths, tuple(starts))
    results = [final[1] for final in finals]
    summed = results[0] + results[1] + results[2] + results[3]
    left_view = (summed * (1.0 / 64.0)).astype(jnp.bfloat16)
    next_view = shifted(left_view, "col", -1)
    joined = jnp.concatenate([left_view, next_view], axis=1)
    right_view = diagonal_view(joined, tile_cols)
    return (left_view, right_view)


def solution(mesh):
    placed = (P("row", "col", None), P(), P())
    return jax.shard_map(
        shards,
        mesh=mesh,
        in_specs=placed,
        out_specs=(P("row", "col", None), P("row", "col", None)),
        check_vma=False,
    )
```

profile of v0, /device:TPU:1, one launch (start us, length us, event | category | flops | bytes accessed | tf_op | source)
XLA Modules:
  0.0 838.5 jit_solution(13696004202516994049)
XLA Ops:
  11.5 763.4 %while.95 = (s32[]{:T(128)}, f32[8,128]{1,0:T(8,128)S(1)}, f32[32,128,128]{2,0,1:T(8,128)}, f32[8,128]{1,0:T(8,128)}, f32[32,128,128]{2,0,1:T(8,128)}, /*index=5...) while((s32[]{:T(128)}, f32[8,128]{1,0:T(8,128)S(1)}, ...), condition=%wide.region_21.22_spmd, body=%wide.region_0.21_spmd.sunk | while | flops 79864 | bytes 18592032 | solution.py:135
  43.5 34.4 %collective-permute-start.1 = (f32[8,128]{1,0:T(8,128)}, f32[8,128]{1,0:T(8,128)S(1)}, u32[]{:S(2)}, u32[]{:S(2)}) collective-permute-start(f32[8,128]{1,0:T(8,128)} %get-tuple-element.1357), channel_id=1, source_target_pairs={{1,0},{2,1},{3,2},{4,3},{5,4},{6,5},{7,6},{9,8},{10,9},{11,10},{12... | collective-permute-start | bytes 12296 | tf_op jit(solution)/shard_map/while/body/eval_jaxpr/ppermute | solution.py:10
  78.0 38.0 %conditional.8 = (f32[8,128]{1,0:T(8,128)S(1)}, f32[32,128,128]{2,0,1:T(8,128)}) conditional(s32[]{:T(128)} %convert_element_type.59, f32[32,128,128]{2,0,1:T(8,128)} %get-tuple-element.1356, (s32[]{:T(128)}, f32[32,128,128]{2,1,0:T(8,128)S(1)}, f32[]{:T(128)}, f32[]{:T(128)}, f32[8,128]{1,0:T(8,128)S(1)}, /*index=5*/f32[32,128,128]{2,0,1:T(8,128)}) %tuple.193), branch_computations={%region_1.1_spmd, %region_2.5_spmd} | conditional | flops 7176 | bytes 6345971 | solution.py:62
  79.3 35.8 %while.91 = (s32[]{:T(128)}, f32[8,128]{1,0:T(8,128)S(1)}, f32[128,8,128]{2,1,0:T(8,128)S(1)}, f32[128,8,128]{2,1,0:T(8,128)S(1)}, f32[]{:T(128)}, /*index=5*/f32[]{:T(128)}, s32[]{:T(128)}, f32[]{:T(128)}) while((s32[]{:T(128)}, f32[8,128]{1,0:T(8,128)S(1)}, f32[128,8,128]{2,1,0:T(8,128)S(1)}, f32[128,8,128]{2,1,0:T(8,128)S(1)}, f32[]{:T(128)}, ...), condition=%wide.region_5.4_spmd, body=%wide.region_3.3_spmd.sunk | while | flops 7170 | bytes 46157 | solution.py:30
  139.5 38.0 %conditional.8 = (f32[8,128]{1,0:T(8,128)S(1)}, f32[32,128,128]{2,0,1:T(8,128)}) conditional(s32[]{:T(128)} %convert_element_type.59, f32[32,128,128]{2,0,1:T(8,128)} %get-tuple-element.1356, (s32[]{:T(128)}, f32[32,128,128]{2,1,0:T(8,128)S(1)}, f32[]{:T(128)}, f32[]{:T(128)}, f32[8,128]{1,0:T(8,128)S(1)}, /*index=5*/f32[32,128,128]{2,0,1:T(8,128)}) %tuple.193), branch_computations={%region_1.1_spmd, %region_2.5_spmd} | conditional | flops 7176 | bytes 6345971 | solution.py:62
  140.9 35.8 %while.91 = (s32[]{:T(128)}, f32[8,128]{1,0:T(8,128)S(1)}, f32[128,8,128]{2,1,0:T(8,128)S(1)}, f32[128,8,128]{2,1,0:T(8,128)S(1)}, f32[]{:T(128)}, /*index=5*/f32[]{:T(128)}, s32[]{:T(128)}, f32[]{:T(128)}) while((s32[]{:T(128)}, f32[8,128]{1,0:T(8,128)S(1)}, f32[128,8,128]{2,1,0:T(8,128)S(1)}, f32[128,8,128]{2,1,0:T(8,128)S(1)}, f32[]{:T(128)}, ...), condition=%wide.region_5.4_spmd, body=%wide.region_3.3_spmd.sunk | while | flops 7170 | bytes 46157 | solution.py:30
  191.1 17.7 %collective-permute-start.2 = (f32[32,128]{1,0:T(8,128)}, f32[32,128]{1,0:T(8,128)S(1)}, u32[]{:S(2)}, u32[]{:S(2)}) collective-permute-start(f32[32,128]{1,0:T(8,128)} %get-tuple-element.1359), channel_id=1, source_target_pairs={{0,8},{8,16},{16,24},{1,9},{9,17},{17,25},{2,10},{10,18},{18,26},{... | collective-permute-start | bytes 49160 | tf_op jit(solution)/shard_map/while/body/eval_jaxpr/ppermute | solution.py:10
  215.5 38.0 %conditional.8 = (f32[8,128]{1,0:T(8,128)S(1)}, f32[32,128,128]{2,0,1:T(8,128)}) conditional(s32[]{:T(128)} %convert_element_type.59, f32[32,128,128]{2,0,1:T(8,128)} %get-tuple-element.1356, (s32[]{:T(128)}, f32[32,128,128]{2,1,0:T(8,128)S(1)}, f32[]{:T(128)}, f32[]{:T(128)}, f32[8,128]{1,0:T(8,128)S(1)}, /*index=5*/f32[32,128,128]{2,0,1:T(8,128)}) %tuple.193), branch_computations={%region_1.1_spmd, %region_2.5_spmd} | conditional | flops 7176 | bytes 6345971 | solution.py:62
  216.9 35.8 %while.91 = (s32[]{:T(128)}, f32[8,128]{1,0:T(8,128)S(1)}, f32[128,8,128]{2,1,0:T(8,128)S(1)}, f32[128,8,128]{2,1,0:T(8,128)S(1)}, f32[]{:T(128)}, /*index=5*/f32[]{:T(128)}, s32[]{:T(128)}, f32[]{:T(128)}) while((s32[]{:T(128)}, f32[8,128]{1,0:T(8,128)S(1)}, f32[128,8,128]{2,1,0:T(8,128)S(1)}, f32[128,8,128]{2,1,0:T(8,128)S(1)}, f32[]{:T(128)}, ...), condition=%wide.region_5.4_spmd, body=%wide.region_3.3_spmd.sunk | while | flops 7170 | bytes 46157 | solution.py:30
  290.3 38.0 %conditional.8 = (f32[8,128]{1,0:T(8,128)S(1)}, f32[32,128,128]{2,0,1:T(8,128)}) conditional(s32[]{:T(128)} %convert_element_type.59, f32[32,128,128]{2,0,1:T(8,128)} %get-tuple-element.1356, (s32[]{:T(128)}, f32[32,128,128]{2,1,0:T(8,128)S(1)}, f32[]{:T(128)}, f32[]{:T(128)}, f32[8,128]{1,0:T(8,128)S(1)}, /*index=5*/f32[32,128,128]{2,0,1:T(8,128)}) %tuple.193), branch_computations={%region_1.1_spmd, %region_2.5_spmd} | conditional | flops 7176 | bytes 6345971 | solution.py:62
  291.6 35.8 %while.91 = (s32[]{:T(128)}, f32[8,128]{1,0:T(8,128)S(1)}, f32[128,8,128]{2,1,0:T(8,128)S(1)}, f32[128,8,128]{2,1,0:T(8,128)S(1)}, f32[]{:T(128)}, /*index=5*/f32[]{:T(128)}, s32[]{:T(128)}, f32[]{:T(128)}) while((s32[]{:T(128)}, f32[8,128]{1,0:T(8,128)S(1)}, f32[128,8,128]{2,1,0:T(8,128)S(1)}, f32[128,8,128]{2,1,0:T(8,128)S(1)}, f32[]{:T(128)}, ...), condition=%wide.region_5.4_spmd, body=%wide.region_3.3_spmd.sunk | while | flops 7170 | bytes 46157 | solution.py:30
  341.9 16.4 %collective-permute-start.2 = (f32[32,128]{1,0:T(8,128)}, f32[32,128]{1,0:T(8,128)S(1)}, u32[]{:S(2)}, u32[]{:S(2)}) collective-permute-start(f32[32,128]{1,0:T(8,128)} %get-tuple-element.1359), channel_id=1, source_target_pairs={{0,8},{8,16},{16,24},{1,9},{9,17},{17,25},{2,10},{10,18},{18,26},{... | collective-permute-start | bytes 49160 | tf_op jit(solution)/shard_map/while/body/eval_jaxpr/ppermute | solution.py:10
  365.5 45.1 %collective-permute-done.1 = f32[8,128]{1,0:T(8,128)S(1)} collective-permute-done((f32[8,128]{1,0:T(8,128)}, f32[8,128]{1,0:T(8,128)S(1)}, u32[]{:S(2)}, u32[]{:S(2)}) %collective-permute-start.1) | collective-permute-done | bytes 4128 | tf_op jit(solution)/shard_map/while/body/eval_jaxpr/ppermute | solution.py:10
  430.2 77.3 %collective-permute-start = (f32[8,128]{1,0:T(8,128)S(1)}, f32[8,128]{1,0:T(8,128)S(1)}, u32[]{:S(2)}, u32[]{:S(2)}) collective-permute-start(f32[8,128]{1,0:T(8,128)S(1)} %get-tuple-element.1355), channel_id=1, source_target_pairs={{0,1},{1,2},{2,3},{3,4},{4,5},{5,6},{6,7},{8,9},{9,10},{10,11},{11... | collective-permute-start | bytes 12296 | tf_op jit(solution)/shard_map/while/body/eval_jaxpr/ppermute | solution.py:10
  512.8 38.6 %conditional.9 = (f32[8,128]{1,0:T(8,128)}, f32[32,128,128]{2,0,1:T(8,128)}) conditional(s32[]{:T(128)} %convert_element_type.60, f32[32,128,128]{2,0,1:T(8,128)} %get-tuple-element.1358, (s32[]{:T(128)}, f32[32,128,128]{2,1,0:T(8,128)S(1)}, f32[]{:T(128)}, f32[]{:T(128)}, f32[8,128]{1,0:T(8,128)S(1)}, /*index=5*/f32[32,128,128]{2,0,1:T(8,128)}) %tuple.194), branch_computations={%region_6.6_spmd, %region_7.10_spmd} | conditional | flops 7177 | bytes 6870283 | solution.py:62
  514.1 35.8 %while.92 = (s32[]{:T(128)}, f32[8,128]{1,0:T(8,128)S(1)}, f32[128,8,128]{2,1,0:T(8,128)S(1)}, f32[128,8,128]{2,1,0:T(8,128)S(1)}, f32[]{:T(128)}, /*index=5*/f32[]{:T(128)}, s32[]{:T(128)}, s32[]{:T(128)}, f32[]{:T(128)}) while((s32[]{:T(128)}, f32[8,128]{1,0:T(8,128)S(1)}, f32[128,8,128]{2,1,0:T(8,128)S(1)}, f32[128,8,128]{2,1,0:T(8,128)S(1)}, ...), condition=%wide.region_10.9_spmd, body=%wide.region_8.8_spmd.sunk | while | flops 7171 | bytes 46169 | solution.py:30
  571.7 39.2 %collective-permute-done.1 = f32[8,128]{1,0:T(8,128)S(1)} collective-permute-done((f32[8,128]{1,0:T(8,128)}, f32[8,128]{1,0:T(8,128)S(1)}, u32[]{:S(2)}, u32[]{:S(2)}) %collective-permute-start.1) | collective-permute-done | bytes 4128 | tf_op jit(solution)/shard_map/while/body/eval_jaxpr/ppermute | solution.py:10
  610.9 38.6 %conditional.9 = (f32[8,128]{1,0:T(8,128)}, f32[32,128,128]{2,0,1:T(8,128)}) conditional(s32[]{:T(128)} %convert_element_type.60, f32[32,128,128]{2,0,1:T(8,128)} %get-tuple-element.1358, (s32[]{:T(128)}, f32[32,128,128]{2,1,0:T(8,128)S(1)}, f32[]{:T(128)}, f32[]{:T(128)}, f32[8,128]{1,0:T(8,128)S(1)}, /*index=5*/f32[32,128,128]{2,0,1:T(8,128)}) %tuple.194), branch_computations={%region_6.6_spmd, %region_7.10_spmd} | conditional | flops 7177 | bytes 6870283 | solution.py:62
  612.2 35.8 %while.92 = (s32[]{:T(128)}, f32[8,128]{1,0:T(8,128)S(1)}, f32[128,8,128]{2,1,0:T(8,128)S(1)}, f32[128,8,128]{2,1,0:T(8,128)S(1)}, f32[]{:T(128)}, /*index=5*/f32[]{:T(128)}, s32[]{:T(128)}, s32[]{:T(128)}, f32[]{:T(128)}) while((s32[]{:T(128)}, f32[8,128]{1,0:T(8,128)S(1)}, f32[128,8,128]{2,1,0:T(8,128)S(1)}, f32[128,8,128]{2,1,0:T(8,128)S(1)}, ...), condition=%wide.region_10.9_spmd, body=%wide.region_8.8_spmd.sunk | while | flops 7171 | bytes 46169 | solution.py:30
  665.1 38.6 %conditional.9 = (f32[8,128]{1,0:T(8,128)}, f32[32,128,128]{2,0,1:T(8,128)}) conditional(s32[]{:T(128)} %convert_element_type.60, f32[32,128,128]{2,0,1:T(8,128)} %get-tuple-element.1358, (s32[]{:T(128)}, f32[32,128,128]{2,1,0:T(8,128)S(1)}, f32[]{:T(128)}, f32[]{:T(128)}, f32[8,128]{1,0:T(8,128)S(1)}, /*index=5*/f32[32,128,128]{2,0,1:T(8,128)}) %tuple.194), branch_computations={%region_6.6_spmd, %region_7.10_spmd} | conditional | flops 7177 | bytes 6870283 | solution.py:62
  666.5 35.8 %while.92 = (s32[]{:T(128)}, f32[8,128]{1,0:T(8,128)S(1)}, f32[128,8,128]{2,1,0:T(8,128)S(1)}, f32[128,8,128]{2,1,0:T(8,128)S(1)}, f32[]{:T(128)}, /*index=5*/f32[]{:T(128)}, s32[]{:T(128)}, s32[]{:T(128)}, f32[]{:T(128)}) while((s32[]{:T(128)}, f32[8,128]{1,0:T(8,128)S(1)}, f32[128,8,128]{2,1,0:T(8,128)S(1)}, f32[128,8,128]{2,1,0:T(8,128)S(1)}, ...), condition=%wide.region_10.9_spmd, body=%wide.region_8.8_spmd.sunk | while | flops 7171 | bytes 46169 | solution.py:30
  719.9 38.6 %conditional.9 = (f32[8,128]{1,0:T(8,128)}, f32[32,128,128]{2,0,1:T(8,128)}) conditional(s32[]{:T(128)} %convert_element_type.60, f32[32,128,128]{2,0,1:T(8,128)} %get-tuple-element.1358, (s32[]{:T(128)}, f32[32,128,128]{2,1,0:T(8,128)S(1)}, f32[]{:T(128)}, f32[]{:T(128)}, f32[8,128]{1,0:T(8,128)S(1)}, /*index=5*/f32[32,128,128]{2,0,1:T(8,128)}) %tuple.194), branch_computations={%region_6.6_spmd, %region_7.10_spmd} | conditional | flops 7177 | bytes 6870283 | solution.py:62
  721.3 35.8 %while.92 = (s32[]{:T(128)}, f32[8,128]{1,0:T(8,128)S(1)}, f32[128,8,128]{2,1,0:T(8,128)S(1)}, f32[128,8,128]{2,1,0:T(8,128)S(1)}, f32[]{:T(128)}, /*index=5*/f32[]{:T(128)}, s32[]{:T(128)}, s32[]{:T(128)}, f32[]{:T(128)}) while((s32[]{:T(128)}, f32[8,128]{1,0:T(8,128)S(1)}, f32[128,8,128]{2,1,0:T(8,128)S(1)}, f32[128,8,128]{2,1,0:T(8,128)S(1)}, ...), condition=%wide.region_10.9_spmd, body=%wide.region_8.8_spmd.sunk | while | flops 7171 | bytes 46169 | solution.py:30
  780.9 38.5 %collective-permute-start.4 = (bf16[32,128,128]{2,1,0:T(8,128)(2,1)S(1)}, bf16[32,128,128]{2,1,0:T(8,128)(2,1)S(1)}, u32[]{:S(2)}, u32[]{:S(2)}) collective-permute-start(bf16[32,128,128]{2,1,0:T(8,128)(2,1)S(1)} %fusion.7), channel_id=1, source_target_pairs={{1,0},{2,1},{3,2},{4,3},{5,4},{6,5},{7,6},{9,8},{10,9},{11,10},{12... | collective-permute-start | bytes 3145736 | tf_op jit(solution)/shard_map/ppermute | solution.py:10
  (5673 shorter events, 729.4 us)
Async XLA Ops:
  38.9 78.3 %collective-permute-start.2 = (f32[32,128]{1,0:T(8,128)}, f32[32,128]{1,0:T(8,128)S(1)}, u32[]{:S(2)}, u32[]{:S(2)}) collective-permute-start(f32[32,128]{1,0:T(8,128)} %get-tuple-element.1359), channel_id=1, source_target_pairs={{0,8},{8,16},{16,24},{1,9},{9,17},{17,25},{2,10},{10,18},{18,26},{... | collective-permute-start | bytes 49160 | tf_op jit(solution)/shard_map/while/body/eval_jaxpr/ppermute | solution.py:10
  40.2 88.7 %collective-permute-start.3 = (f32[32,128]{1,0:T(8,128)}, f32[32,128]{1,0:T(8,128)S(1)}, u32[]{:S(2)}, u32[]{:S(2)}) collective-permute-start(f32[32,128]{1,0:T(8,128)} %get-tuple-element.1361), channel_id=1, source_target_pairs={{8,0},{16,8},{24,16},{9,1},{17,9},{25,17},{10,2},{18,10},{26,18},{... | collective-permute-start | bytes 49160 | tf_op jit(solution)/shard_map/while/body/eval_jaxpr/ppermute | solution.py:10
  43.5 72.5 %collective-permute-start.1 = (f32[8,128]{1,0:T(8,128)}, f32[8,128]{1,0:T(8,128)S(1)}, u32[]{:S(2)}, u32[]{:S(2)}) collective-permute-start(f32[8,128]{1,0:T(8,128)} %get-tuple-element.1357), channel_id=1, source_target_pairs={{1,0},{2,1},{3,2},{4,3},{5,4},{6,5},{7,6},{9,8},{10,9},{11,10},{12... | collective-permute-start | bytes 12296 | tf_op jit(solution)/shard_map/while/body/eval_jaxpr/ppermute | solution.py:10
  129.6 49.1 %collective-permute-start.2 = (f32[32,128]{1,0:T(8,128)}, f32[32,128]{1,0:T(8,128)S(1)}, u32[]{:S(2)}, u32[]{:S(2)}) collective-permute-start(f32[32,128]{1,0:T(8,128)} %get-tuple-element.1359), channel_id=1, source_target_pairs={{0,8},{8,16},{16,24},{1,9},{9,17},{17,25},{2,10},{10,18},{18,26},{... | collective-permute-start | bytes 49160 | tf_op jit(solution)/shard_map/while/body/eval_jaxpr/ppermute | solution.py:10
  133.8 56.6 %collective-permute-start.3 = (f32[32,128]{1,0:T(8,128)}, f32[32,128]{1,0:T(8,128)S(1)}, u32[]{:S(2)}, u32[]{:S(2)}) collective-permute-start(f32[32,128]{1,0:T(8,128)} %get-tuple-element.1361), channel_id=1, source_target_pairs={{8,0},{16,8},{24,16},{9,1},{17,9},{25,17},{10,2},{18,10},{26,18},{... | collective-permute-start | bytes 49160 | tf_op jit(solution)/shard_map/while/body/eval_jaxpr/ppermute | solution.py:10
  137.1 40.5 %collective-permute-start.1 = (f32[8,128]{1,0:T(8,128)}, f32[8,128]{1,0:T(8,128)S(1)}, u32[]{:S(2)}, u32[]{:S(2)}) collective-permute-start(f32[8,128]{1,0:T(8,128)} %get-tuple-element.1357), channel_id=1, source_target_pairs={{1,0},{2,1},{3,2},{4,3},{5,4},{6,5},{7,6},{9,8},{10,9},{11,10},{12... | collective-permute-start | bytes 12296 | tf_op jit(solution)/shard_map/while/body/eval_jaxpr/ppermute | solution.py:10
  191.1 63.7 %collective-permute-start.2 = (f32[32,128]{1,0:T(8,128)}, f32[32,128]{1,0:T(8,128)S(1)}, u32[]{:S(2)}, u32[]{:S(2)}) collective-permute-start(f32[32,128]{1,0:T(8,128)} %get-tuple-element.1359), channel_id=1, source_target_pairs={{0,8},{8,16},{16,24},{1,9},{9,17},{17,25},{2,10},{10,18},{18,26},{... | collective-permute-start | bytes 49160 | tf_op jit(solution)/shard_map/while/body/eval_jaxpr/ppermute | solution.py:10
  208.8 57.7 %collective-permute-start.3 = (f32[32,128]{1,0:T(8,128)}, f32[32,128]{1,0:T(8,128)S(1)}, u32[]{:S(2)}, u32[]{:S(2)}) collective-permute-start(f32[32,128]{1,0:T(8,128)} %get-tuple-element.1361), channel_id=1, source_target_pairs={{8,0},{16,8},{24,16},{9,1},{17,9},{25,17},{10,2},{18,10},{26,18},{... | collective-permute-start | bytes 49160 | tf_op jit(solution)/shard_map/while/body/eval_jaxpr/ppermute | solution.py:10
  278.3 51.1 %collective-permute-start.2 = (f32[32,128]{1,0:T(8,128)}, f32[32,128]{1,0:T(8,128)S(1)}, u32[]{:S(2)}, u32[]{:S(2)}) collective-permute-start(f32[32,128]{1,0:T(8,128)} %get-tuple-element.1359), channel_id=1, source_target_pairs={{0,8},{8,16},{16,24},{1,9},{9,17},{17,25},{2,10},{10,18},{18,26},{... | collective-permute-start | bytes 49160 | tf_op jit(solution)/shard_map/while/body/eval_jaxpr/ppermute | solution.py:10
  283.1 47.0 %collective-permute-start.3 = (f32[32,128]{1,0:T(8,128)}, f32[32,128]{1,0:T(8,128)S(1)}, u32[]{:S(2)}, u32[]{:S(2)}) collective-permute-start(f32[32,128]{1,0:T(8,128)} %get-tuple-element.1361), channel_id=1, source_target_pairs={{8,0},{16,8},{24,16},{9,1},{17,9},{25,17},{10,2},{18,10},{26,18},{... | collective-permute-start | bytes 49160 | tf_op jit(solution)/shard_map/while/body/eval_jaxpr/ppermute | solution.py:10
  341.9 69.3 %collective-permute-start.2 = (f32[32,128]{1,0:T(8,128)}, f32[32,128]{1,0:T(8,128)S(1)}, u32[]{:S(2)}, u32[]{:S(2)}) collective-permute-start(f32[32,128]{1,0:T(8,128)} %get-tuple-element.1359), channel_id=1, source_target_pairs={{0,8},{8,16},{16,24},{1,9},{9,17},{17,25},{2,10},{10,18},{18,26},{... | collective-permute-start | bytes 49160 | tf_op jit(solution)/shard_map/while/body/eval_jaxpr/ppermute | solution.py:10
  358.3 53.6 %collective-permute-start.3 = (f32[32,128]{1,0:T(8,128)}, f32[32,128]{1,0:T(8,128)S(1)}, u32[]{:S(2)}, u32[]{:S(2)}) collective-permute-start(f32[32,128]{1,0:T(8,128)} %get-tuple-element.1361), channel_id=1, source_target_pairs={{8,0},{16,8},{24,16},{9,1},{17,9},{25,17},{10,2},{18,10},{26,18},{... | collective-permute-start | bytes 49160 | tf_op jit(solution)/shard_map/while/body/eval_jaxpr/ppermute | solution.py:10
  363.5 47.1 %collective-permute-start.1 = (f32[8,128]{1,0:T(8,128)}, f32[8,128]{1,0:T(8,128)S(1)}, u32[]{:S(2)}, u32[]{:S(2)}) collective-permute-start(f32[8,128]{1,0:T(8,128)} %get-tuple-element.1357), channel_id=1, source_target_pairs={{1,0},{2,1},{3,2},{4,3},{5,4},{6,5},{7,6},{9,8},{10,9},{11,10},{12... | collective-permute-start | bytes 12296 | tf_op jit(solution)/shard_map/while/body/eval_jaxpr/ppermute | solution.py:10
  423.7 127.7 %collective-permute-start.2 = (f32[32,128]{1,0:T(8,128)}, f32[32,128]{1,0:T(8,128)S(1)}, u32[]{:S(2)}, u32[]{:S(2)}) collective-permute-start(f32[32,128]{1,0:T(8,128)} %get-tuple-element.1359), channel_id=1, source_target_pairs={{0,8},{8,16},{16,24},{1,9},{9,17},{17,25},{2,10},{10,18},{18,26},{... | collective-permute-start | bytes 49160 | tf_op jit(solution)/shard_map/while/body/eval_jaxpr/ppermute | solution.py:10
  428.9 123.1 %collective-permute-start.3 = (f32[32,128]{1,0:T(8,128)}, f32[32,128]{1,0:T(8,128)S(1)}, u32[]{:S(2)}, u32[]{:S(2)}) collective-permute-start(f32[32,128]{1,0:T(8,128)} %get-tuple-element.1361), channel_id=1, source_target_pairs={{8,0},{16,8},{24,16},{9,1},{17,9},{25,17},{10,2},{18,10},{26,18},{... | collective-permute-start | bytes 49160 | tf_op jit(solution)/shard_map/while/body/eval_jaxpr/ppermute | solution.py:10
  430.2 79.3 %collective-permute-start = (f32[8,128]{1,0:T(8,128)S(1)}, f32[8,128]{1,0:T(8,128)S(1)}, u32[]{:S(2)}, u32[]{:S(2)}) collective-permute-start(f32[8,128]{1,0:T(8,128)S(1)} %get-tuple-element.1355), channel_id=1, source_target_pairs={{0,1},{1,2},{2,3},{3,4},{4,5},{5,6},{6,7},{8,9},{9,10},{10,11},{11... | collective-permute-start | bytes 12296 | tf_op jit(solution)/shard_map/while/body/eval_jaxpr/ppermute | solution.py:10
  563.8 85.6 %collective-permute-start.2 = (f32[32,128]{1,0:T(8,128)}, f32[32,128]{1,0:T(8,128)S(1)}, u32[]{:S(2)}, u32[]{:S(2)}) collective-permute-start(f32[32,128]{1,0:T(8,128)} %get-tuple-element.1359), channel_id=1, source_target_pairs={{0,8},{8,16},{16,24},{1,9},{9,17},{17,25},{2,10},{10,18},{18,26},{... | collective-permute-start | bytes 49160 | tf_op jit(solution)/shard_map/while/body/eval_jaxpr/ppermute | solution.py:10
  565.1 85.0 %collective-permute-start.3 = (f32[32,128]{1,0:T(8,128)}, f32[32,128]{1,0:T(8,128)S(1)}, u32[]{:S(2)}, u32[]{:S(2)}) collective-permute-start(f32[32,128]{1,0:T(8,128)} %get-tuple-element.1361), channel_id=1, source_target_pairs={{8,0},{16,8},{24,16},{9,1},{17,9},{25,17},{10,2},{18,10},{26,18},{... | collective-permute-start | bytes 49160 | tf_op jit(solution)/shard_map/while/body/eval_jaxpr/ppermute | solution.py:10
  569.7 41.2 %collective-permute-start.1 = (f32[8,128]{1,0:T(8,128)}, f32[8,128]{1,0:T(8,128)S(1)}, u32[]{:S(2)}, u32[]{:S(2)}) collective-permute-start(f32[8,128]{1,0:T(8,128)} %get-tuple-element.1357), channel_id=1, source_target_pairs={{1,0},{2,1},{3,2},{4,3},{5,4},{6,5},{7,6},{9,8},{10,9},{11,10},{12... | collective-permute-start | bytes 12296 | tf_op jit(solution)/shard_map/while/body/eval_jaxpr/ppermute | solution.py:10
  650.8 52.9 %collective-permute-start.2 = (f32[32,128]{1,0:T(8,128)}, f32[32,128]{1,0:T(8,128)S(1)}, u32[]{:S(2)}, u32[]{:S(2)}) collective-permute-start(f32[32,128]{1,0:T(8,128)} %get-tuple-element.1359), channel_id=1, source_target_pairs={{0,8},{8,16},{16,24},{1,9},{9,17},{17,25},{2,10},{10,18},{18,26},{... | collective-permute-start | bytes 49160 | tf_op jit(solution)/shard_map/while/body/eval_jaxpr/ppermute | solution.py:10
  654.8 49.6 %collective-permute-start.3 = (f32[32,128]{1,0:T(8,128)}, f32[32,128]{1,0:T(8,128)S(1)}, u32[]{:S(2)}, u32[]{:S(2)}) collective-permute-start(f32[32,128]{1,0:T(8,128)} %get-tuple-element.1361), channel_id=1, source_target_pairs={{8,0},{16,8},{24,16},{9,1},{17,9},{25,17},{10,2},{18,10},{26,18},{... | collective-permute-start | bytes 49160 | tf_op jit(solution)/shard_map/while/body/eval_jaxpr/ppermute | solution.py:10
  705.0 53.5 %collective-permute-start.2 = (f32[32,128]{1,0:T(8,128)}, f32[32,128]{1,0:T(8,128)S(1)}, u32[]{:S(2)}, u32[]{:S(2)}) collective-permute-start(f32[32,128]{1,0:T(8,128)} %get-tuple-element.1359), channel_id=1, source_target_pairs={{0,8},{8,16},{16,24},{1,9},{9,17},{17,25},{2,10},{10,18},{18,26},{... | collective-permute-start | bytes 49160 | tf_op jit(solution)/shard_map/while/body/eval_jaxpr/ppermute | solution.py:10
  711.3 47.8 %collective-permute-start.3 = (f32[32,128]{1,0:T(8,128)}, f32[32,128]{1,0:T(8,128)S(1)}, u32[]{:S(2)}, u32[]{:S(2)}) collective-permute-start(f32[32,128]{1,0:T(8,128)} %get-tuple-element.1361), channel_id=1, source_target_pairs={{8,0},{16,8},{24,16},{9,1},{17,9},{25,17},{10,2},{18,10},{26,18},{... | collective-permute-start | bytes 49160 | tf_op jit(solution)/shard_map/while/body/eval_jaxpr/ppermute | solution.py:10
  780.9 40.8 %collective-permute-start.4 = (bf16[32,128,128]{2,1,0:T(8,128)(2,1)S(1)}, bf16[32,128,128]{2,1,0:T(8,128)(2,1)S(1)}, u32[]{:S(2)}, u32[]{:S(2)}) collective-permute-start(bf16[32,128,128]{2,1,0:T(8,128)(2,1)S(1)} %fusion.7), channel_id=1, source_target_pairs={{1,0},{2,1},{3,2},{4,3},{5,4},{6,5},{7,6},{9,8},{10,9},{11,10},{12... | collective-permute-start | bytes 3145736 | tf_op jit(solution)/shard_map/ppermute | solution.py:10
  (44 other events, 447.6 us)
where the time goes:
time: 843 us; the launch traced here: 838 us
  starting transfers between devices  285 us (34%)
  other arithmetic  256 us (30%)
  local copies, waits for them, and re-layouts  167 us (20%)
  waiting for transfers between devices  102 us (12%)
  loops' own time  26.2 us (3%)
    ppermute x45, starting transfers between devices, shifted(): return lax.ppermute(block, axis, route)  285 us
    reduce_min x1288, other arithmetic, advance(): lowest = jnp.min(before, axis=-1, keepdims=True)  171 us
    ppermute x45, waiting for transfers between devices, shifted(): return lax.ppermute(block, axis, route)  102 us
    slice x1280, local copies, waits for them, and re-layouts, advance(): lower_side = jnp.concatenate([barrier, before[..., :-1]], axis=-1)  93.1 us
    dynamic_update_slice x1024, other arithmetic, run_strip(): lax.scan(advance_one, incoming, strip_costs, reverse=not forward)  71.1 us
    another operation x48, local copies, waits for them, and re-layouts  24.5 us
    another operation x16, loops' own time, run_strip(): lax.scan(advance_one, incoming, strip_costs, reverse=not forward)  24.5 us

commit v1 on v0

v1 whole, which is shorter than its diff:
```python
import functools

import jax
import jax.numpy as jnp
from jax import lax
from jax.experimental import pallas as pl
from jax.experimental.pallas import tpu as pltpu
from jax.sharding import PartitionSpec as P

SUB = 8
BIG = 1e30
TRANSPOSED = (((1,), (1,)), ((), ()))
PLAIN = (((1,), (0,)), ((), ()))
LIMIT = 40 * 1024 * 1024


def one_hot(rule, size):
    row = lax.broadcasted_iota(jnp.int32, (size, size), 0)
    col = lax.broadcasted_iota(jnp.int32, (size, size), 1)
    return jnp.where(rule(row, col), 1.0, 0.0).astype(jnp.bfloat16)


def interleave(size):
    return one_hot(lambda r, c: c == (r % SUB) * (size // SUB) + r // SUB, size)


def identity(size):
    return one_hot(lambda r, c: r == c, size)


def reversal(size):
    return one_hot(lambda r, c: r + c == size - 1, size)


def dot(a, b, dims):
    return lax.dot_general(a, b, dims, preferred_element_type=jnp.float32)


def split(block):
    wide = block.astype(jnp.float32)
    return [wide[i : i + SUB] for i in range(0, wide.shape[0], SUB)]


def join(parts):
    return jnp.concatenate(parts, axis=0).astype(jnp.bfloat16)


def fold_min(parts):
    parts = list(parts)
    while len(parts) > 1:
        parts = [jnp.minimum(a, b) for a, b in zip(parts[::2], parts[1::2])]
    low = parts[0]
    for shift in (4, 2, 1):
        low = jnp.minimum(low, pltpu.roll(low, shift, 0))
    return low


def relax(v, q1, q2):
    sub = lax.broadcasted_iota(jnp.int32, v[0].shape, 0)
    under = jnp.where(sub == 0, BIG, pltpu.roll(v[-1], 1, 0))
    over = jnp.where(sub == SUB - 1, BIG, pltpu.roll(v[0], SUB - 1, 0))
    low = fold_min(v)
    jump = low + q2
    below = [under] + v[:-1]
    above = v[1:] + [over]
    best = [
        jnp.minimum(jnp.minimum(x, jump), jnp.minimum(a, b) + q1)
        for x, a, b in zip(v, below, above)
    ]
    return best, low


def penalties(small_ref, large_ref, lanes):
    shape = (SUB, lanes)
    q1 = jnp.full(shape, small_ref[0], jnp.int32).astype(jnp.float32)
    q2 = jnp.full(shape, large_ref[0], jnp.int32).astype(jnp.float32)
    return q1, q2


def lanes_from(v, fresh, first):
    lane = lax.broadcasted_iota(jnp.int32, v[0].shape, 1)
    return [jnp.where(lane < first, a, b) for a, b in zip(v, fresh)]


def prepare_kernel(costs_ref, turned_ref, out_ref):
    rows, cols, depth = costs_ref.shape
    mix = interleave(depth)
    for g in range(cols // rows):
        span = pl.ds(g * rows, rows)

        def body(y, carry):
            t = g * rows + y
            block = jnp.concatenate(
                [
                    turned_ref[t],
                    turned_ref[cols - 1 - t],
                    costs_ref[y, span, :],
                    costs_ref[rows - 1 - y, span, :],
                ],
                axis=0,
            )
            out_ref[t] = dot(mix, block, TRANSPOSED).astype(jnp.bfloat16)
            return carry

        lax.fori_loop(0, rows, body, 0, unroll=4)


def stage_kernel(rows, small_ref, large_ref, c_ref, h_ref, v_ref, h_out, v_out):
    cols, depth, lanes = c_ref.shape
    q1, q2 = penalties(small_ref, large_ref, lanes)
    v = split(h_ref[...])
    for g in range(cols // rows):
        v = lanes_from(v, split(v_ref[g]), 2 * rows)

        def body(y, v):
            best, _ = relax(list(v), q1, q2)
            return tuple(a + b for a, b in zip(best, split(c_ref[g * rows + y])))

        v = list(lax.fori_loop(0, rows, body, tuple(v), unroll=4))
        low = fold_min(v)
        v = [x - low for x in v]
        v_out[g] = join(v)
    h_out[...] = join(v)


def final_kernel(hops, v_hops, *refs):
    small_ref, large_ref, place_ref, c_ref, costs_ref = refs[:5]
    h_refs = refs[5 : 5 + hops]
    v_refs = refs[5 + hops : 5 + hops + v_hops]
    left_ref, skew_ref, h_sum, v_sum = refs[5 + hops + v_hops :]
    rows, cols, depth = costs_ref.shape
    lanes = c_ref.shape[2]
    q1, q2 = penalties(small_ref, large_ref, lanes)
    col_here, row_here = place_ref[0], place_ref[1]
    lane = lax.broadcasted_iota(jnp.int32, (depth, lanes), 1)
    ident = identity(lanes)

    def pick(arrivals, here, first, second):
        total = jnp.zeros((depth, lanes), jnp.float32)
        count = len(arrivals)
        for s, block in enumerate(arrivals):
            early = jnp.where(here == s + 1, 1.0, 0.0)
            late = jnp.where(here == count - 1 - s, 1.0, 0.0)
            share = jnp.where(lane < first, 0.0, jnp.where(lane < second, early, late))
            total = total + block.astype(jnp.float32) * share
        return split(total)

    v = pick([ref[...] for ref in h_refs], col_here, 0, rows)
    half = rows // 2
    for g in range(cols // rows):
        fresh = pick([ref[g] for ref in v_refs], row_here, 2 * rows, 3 * rows)
        v = lanes_from(v, fresh, 2 * rows)
        for second in (False, True):

            def body(i, v):
                y = i + half if second else i
                t = g * rows + y
                best, low = relax(list(v), q1, q2)
                flat = dot(ident, join([x - low for x in best]), TRANSPOSED)
                spans = [
                    (h_sum, t * rows),
                    (h_sum, (cols - 1 - t) * rows),
                    (v_sum, y * cols + g * rows),
                    (v_sum, (rows - 1 - y) * cols + g * rows),
                ]
                for n, (ref, start) in enumerate(spans):
                    where = pl.ds(pl.multiple_of(start, rows), rows)
                    part = flat[n * rows : (n + 1) * rows]
                    again = 2 * g >= cols // rows if n < 2 else second
                    ref[where, :] = ref[where, :] + part if again else part
                return tuple(a + b for a, b in zip(best, split(c_ref[t])))

            v = list(lax.fori_loop(0, half, body, tuple(v), unroll=2))

    mix = interleave(depth)
    back = reversal(depth)

    def finish(y, carry):
        h_rows = h_sum[pl.ds(y, cols, stride=rows), :].astype(jnp.bfloat16)
        v_rows = v_sum[pl.ds(pl.multiple_of(y * cols, cols), cols), :].astype(jnp.bfloat16)
        extra = dot(h_rows, mix, PLAIN) + dot(v_rows, mix, PLAIN)
        summed = extra + 4.0 * costs_ref[y].astype(jnp.float32)
        left = (summed * (1.0 / 64.0)).astype(jnp.bfloat16)
        left_ref[y] = left
        turned = dot(back, left, TRANSPOSED)
        skewed = pltpu.roll(turned, 1, 1, stride=1, stride_axis=0)
        skewed = dot(ident, skewed.astype(jnp.bfloat16), TRANSPOSED).astype(jnp.bfloat16)
        skew_ref[y] = dot(skewed, back, PLAIN).astype(jnp.bfloat16)
        return carry

    lax.fori_loop(0, rows, finish, 0, unroll=2)


def in_vmem(count):
    return [pl.BlockSpec(memory_space=pltpu.VMEM)] * count


def in_smem(count):
    return [pl.BlockSpec(memory_space=pltpu.SMEM)] * count


def both_ways(block, axis, hop):
    size = lax.axis_size(axis)
    route = [(hop, hop + 1), (size - 1 - hop, size - 2 - hop)]
    return lax.ppermute(block, axis, route)


def shards(costs, p_small, p_large):
    rows, cols, depth = costs.shape
    lanes = 4 * rows
    groups = cols // rows
    col_count, row_count = lax.axis_size("col"), lax.axis_size("row")
    params = pltpu.CompilerParams(vmem_limit_bytes=LIMIT)
    turned = jnp.transpose(costs, (1, 0, 2))
    layered = pl.pallas_call(
        prepare_kernel,
        out_shape=jax.ShapeDtypeStruct((cols, depth, lanes), jnp.bfloat16),
        in_specs=in_vmem(2),
        out_specs=pl.BlockSpec(memory_space=pltpu.VMEM),
        compiler_params=params,
        name="prepare",
    )(costs, turned)

    stage = pl.pallas_call(
        functools.partial(stage_kernel, rows),
        out_shape=(
            jax.ShapeDtypeStruct((depth, lanes), jnp.bfloat16),
            jax.ShapeDtypeStruct((groups, depth, lanes), jnp.bfloat16),
        ),
        in_specs=in_smem(2) + in_vmem(3),
        out_specs=tuple(in_vmem(2)),
        compiler_params=params,
        name="stage",
    )
    h_hops, v_hops = col_count - 1, row_count - 1
    spacing = 2 if 2 * (v_hops - 1) < h_hops else 1
    h_now = jnp.zeros((depth, lanes), jnp.bfloat16)
    v_now = jnp.zeros((groups, depth, lanes), jnp.bfloat16)
    h_got, v_got = [], []
    for s in range(max(h_hops, spacing * (v_hops - 1) + 1)):
        h_end, v_end = stage(p_small, p_large, layered, h_now, v_now)
        if s < h_hops:
            h_now = both_ways(h_end, "col", s)
            h_got.append(h_now)
        if s % spacing == 0 and len(v_got) < v_hops:
            v_next = both_ways(v_end, "row", len(v_got))
            v_got.append(v_next)
        if (s + 1) % spacing == 0:
            v_now = v_next

    place = jnp.stack([lax.axis_index("col"), lax.axis_index("row")]).astype(jnp.int32)
    tile = jax.ShapeDtypeStruct((rows, cols, depth), jnp.bfloat16)
    left_view, skewed = pl.pallas_call(
        functools.partial(final_kernel, h_hops, v_hops),
        out_shape=(tile, tile),
        in_specs=in_smem(3) + in_vmem(2 + h_hops + v_hops),
        out_specs=tuple(in_vmem(2)),
        scratch_shapes=[pltpu.VMEM((rows * cols, depth), jnp.float32)] * 2,
        compiler_params=params,
        name="final",
    )(p_small, p_large, place, layered, costs, *h_got, *v_got)

    arrived = lax.ppermute(skewed, "col", [(i, i - 1) for i in range(1, col_count)])
    x = lax.broadcasted_iota(jnp.int32, (cols, depth), 0)
    d = lax.broadcasted_iota(jnp.int32, (cols, depth), 1)
    right_view = jnp.where((x + d < cols)[None], skewed, arrived)
    return left_view, right_view


def solution(mesh):
    placed = (P("row", "col", None), P(), P())
    return jax.shard_map(
        shards,
        mesh=mesh,
        in_specs=placed,
        out_specs=(P("row", "col", None), P("row", "col", None)),
        check_vma=False,
    )
```

time: 843 us -> 117 us (0.14)
  starting transfers between devices: 285 us -> 15.7 us
  other arithmetic: 256 us -> 1.21 us
  local copies, waits for them, and re-layouts: 167 us -> 5.36 us
  waiting for transfers between devices: 102 us -> 30.1 us
  Pallas kernels: 0 us -> 61.9 us
  loops' own time: 26.2 us -> 0 us
    ppermute x45 -> x11, starting transfers between devices: 285 us -> 15.7 us  [the longest x10 13.5 us: both_ways(): return lax.ppermute(block, axis, route)]
    reduce_min x1288 -> x0, other arithmetic: 171 us -> none  [advance(): lowest = jnp.min(before, axis=-1, keepdims=True)]
    slice x1280 -> x0, local copies, waits for them, and re-layouts: 93.1 us -> none  [advance(): lower_side = jnp.concatenate([barrier, before[..., :-1]], axis=-1)]
    ppermute x45 -> x11, waiting for transfers between devices: 102 us -> 30.1 us  [the longest x10 16.3 us: both_ways(): return lax.ppermute(block, axis, route)]
    dynamic_update_slice x1024 -> x0, other arithmetic: 71.1 us -> none  [run_strip(): lax.scan(advance_one, incoming, strip_costs, reverse=not forward)]
    pallas_call x0 -> x9, Pallas kernels: none -> 61.9 us  [the longest x1 33.5 us: shards(): pl.pallas_call(functools.partial(final_kernel, h_hops, v_hops), out_shape...]
    another operation x61 -> x0, loops' own time: 26.2 us -> none  [the longest x16 24.5 us: run_strip(): lax.scan(advance_one, incoming, strip_costs, reverse=not forward)]
    another operation x48 -> x0, local copies, waits for them, and re-layouts: 24.5 us -> none
where the time goes in v1:
time: 117 us; the launch traced here: 116 us
  Pallas kernels  61.9 us (53%)
  waiting for transfers between devices  30.1 us (26%)
  starting transfers between devices  15.7 us (13%)
  local copies, waits for them, and re-layouts  5.36 us (5%)
  between operations  2.16 us (2%)
  other arithmetic  1.21 us (1%)
    pallas_call x1, Pallas kernels, shards(): pl.pallas_call(functools.partial(final_kernel, h_hops, v_hops), out_shape...  33.5 us
    pallas_call x7, Pallas kernels, shards(): h_end, v_end = stage(p_small, p_large, layered, h_now, v_now)  21.7 us
    ppermute x10, waiting for transfers between devices, both_ways(): return lax.ppermute(block, axis, route)  16.3 us
    ppermute x1, waiting for transfers between devices, shards(): lax.ppermute(skewed, 'col', [(i, i - 1) for i in range(1, col_count)])  13.8 us
    ppermute x10, starting transfers between devices, both_ways(): return lax.ppermute(block, axis, route)  13.5 us
    pallas_call x1, Pallas kernels, shards(): pl.pallas_call(prepare_kernel, out_shape=jax.ShapeDtypeStruct((cols, dept...  6.75 us
    unnamed x11, local copies, waits for them, and re-layouts  5.33 us
  transfers between devices with their start and end apart: 11, of which 5 were waited for; matrix products, arithmetic and copies ran while one was open for 0% of the time, Pallas kernels for 9%

profile of v1, /device:TPU:1, one launch (start us, length us, event | category | flops | bytes accessed | tf_op | source)
XLA Modules:
  0.0 116.5 jit_solution(1483345074738791328)
XLA Ops:
  0.6 1.9 %copy.7 = bf16[32,128,128]{2,0,1:T(8,128)(2,1)S(1)} copy(bf16[32,128,128]{2,1,0:T(8,128)(2,1)} %refs_4_.1) | data formatting | bytes 2097152 | tf_op args[0]
  2.5 1.2 %copy-done.3 = bf16[32,128,128]{2,1,0:T(8,128)(2,1)S(1)} copy-done((bf16[32,128,128]{2,1,0:T(8,128)(2,1)S(1)}, bf16[32,128,128]{2,1,0:T(8,128)(2,1)}, u32[]{:S(2)}) %copy-start.3) | copy-done | bytes 1048600
  3.8 6.7 %prepare.1.c_ref.refs_3_ = bf16[128,128,128]{2,1,0:T(8,128)(2,1)S(1)} custom-call(bf16[32,128,128]{2,1,0:T(8,128)(2,1)S(1)} %copy-done.3, bf16[128,32,128]{2,1,0:T(8,128)(2,1)S(1)} %bitcast.5), custom_call_target="tpu_custom_call" | custom-call | tf_op jit(solution)/shard_map/prepare/pallas_call | solution.py:215
  11.9 2.7 %stage.7 = (bf16[128,128]{1,0:T(8,128)(2,1)S(1)}, bf16[4,128,128]{2,1,0:T(8,128)(2,1)S(1)}) custom-call(s32[1]{0:T(128)S(6)} %copy.8.small_ref.refs_0_, s32[1]{0:T(128)S(6)} %copy.9.large_ref.refs_1_, bf16[128,128,128]{2,1,0:T(8,128)(2,1)S(1)} %prepare.1.c_ref.refs_3_, bf16[128,128]{1,0:T(8,128)(2,1)S(1)} %broadcast_in_dim.15.h_ref, ...), custom_call_target="tpu_custom_call" | custom-call | tf_op jit(solution)/shard_map/stage/pallas_call | solution.py:241
  14.6 4.0 %collective-permute-start.2 = (bf16[4,128,128]{2,1,0:T(8,128)(2,1)S(1)}, bf16[4,128,128]{2,1,0:T(8,128)(2,1)S(1)}, u32[]{:S(2)}, u32[]{:S(2)}) collective-permute-start(bf16[4,128,128]{2,1,0:T(8,128)(2,1)S(1)} %get-tuple-element.16), channel_id=1, source_target_pairs={{0,8},{24,16},{1,9},{25,17},{2,10},{26,18},{3,11},{27,19},{4,12},{... | collective-permute-start | bytes 393224 | tf_op jit(solution)/shard_map/ppermute | solution.py:205
  18.6 1.3 %collective-permute-start = (bf16[128,128]{1,0:T(8,128)(2,1)S(1)}, bf16[128,128]{1,0:T(8,128)(2,1)S(1)}, u32[]{:S(2)}, u32[]{:S(2)}) collective-permute-start(bf16[128,128]{1,0:T(8,128)(2,1)S(1)} %get-tuple-element.14), channel_id=1, source_target_pairs={{0,1},{7,6},{8,9},{15,14},{16,17},{23,22},{24,25},{31,30}} | collective-permute-start | bytes 98312 | tf_op jit(solution)/shard_map/ppermute | solution.py:205
  19.9 1.8 %collective-permute-done.h_ref.refs_5_ = bf16[128,128]{1,0:T(8,128)(2,1)S(1)} collective-permute-done((bf16[128,128]{1,0:T(8,128)(2,1)S(1)}, bf16[128,128]{1,0:T(8,128)(2,1)S(1)}, u32[]{:S(2)}, u32[]{:S(2)}) %collective-permute-start) | collective-permute-done | bytes 32800 | tf_op jit(solution)/shard_map/ppermute | solution.py:205
  21.7 3.4 %stage.8 = (bf16[128,128]{1,0:T(8,128)(2,1)S(1)}, bf16[4,128,128]{2,1,0:T(8,128)(2,1)}) custom-call(s32[1]{0:T(128)S(6)} %copy.8.small_ref.refs_0_, s32[1]{0:T(128)S(6)} %copy.9.large_ref.refs_1_, bf16[128,128,128]{2,1,0:T(8,128)(2,1)S(1)} %prepare.1.c_ref.refs_3_, bf16[128,128]{1,0:T(8,128)(2,1)S(1)} %collective-permute-done.h_ref.refs_5_, ...), custom_call_target="tpu_custom_call" | custom-call | tf_op jit(solution)/shard_map/stage/pallas_call | solution.py:241
  25.1 1.6 %collective-permute-start.1 = (bf16[128,128]{1,0:T(8,128)(2,1)S(1)}, bf16[128,128]{1,0:T(8,128)(2,1)S(1)}, u32[]{:S(2)}, u32[]{:S(2)}) collective-permute-start(bf16[128,128]{1,0:T(8,128)(2,1)S(1)} %get-tuple-element.15), channel_id=1, source_target_pairs={{1,2},{6,5},{9,10},{14,13},{17,18},{22,21},{25,26},{30,29}} | collective-permute-start | bytes 98312 | tf_op jit(solution)/shard_map/ppermute | solution.py:205
  26.7 1.0 collective-permute-done.1.h_ref.refs_6_
  27.7 2.7 %stage.9 = (bf16[128,128]{1,0:T(8,128)(2,1)S(1)}, bf16[4,128,128]{2,1,0:T(8,128)(2,1)S(1)}) custom-call(s32[1]{0:T(128)S(6)} %copy.8.small_ref.refs_0_, s32[1]{0:T(128)S(6)} %copy.9.large_ref.refs_1_, bf16[128,128,128]{2,1,0:T(8,128)(2,1)S(1)} %prepare.1.c_ref.refs_3_, bf16[128,128]{1,0:T(8,128)(2,1)S(1)} %collective-permute-done.1.h_ref.refs_6_, ...), custom_call_target="tpu_custom_call" | custom-call | tf_op jit(solution)/shard_map/stage/pallas_call | solution.py:241
  31.8 3.4 %stage.10 = (bf16[128,128]{1,0:T(8,128)(2,1)S(1)}, bf16[4,128,128]{2,1,0:T(8,128)(2,1)}) custom-call(s32[1]{0:T(128)S(6)} %copy.8.small_ref.refs_0_, s32[1]{0:T(128)S(6)} %copy.9.large_ref.refs_1_, bf16[128,128,128]{2,1,0:T(8,128)(2,1)S(1)} %prepare.1.c_ref.refs_3_, bf16[128,128]{1,0:T(8,128)(2,1)S(1)} %collective-permute-done.3.h_ref.refs_7_, ...), custom_call_target="tpu_custom_call" | custom-call | tf_op jit(solution)/shard_map/stage/pallas_call | solution.py:241
  35.8 2.7 %stage.11 = (bf16[128,128]{1,0:T(8,128)(2,1)S(1)}, bf16[4,128,128]{2,1,0:T(8,128)(2,1)S(1)}) custom-call(s32[1]{0:T(128)S(6)} %copy.8.small_ref.refs_0_, s32[1]{0:T(128)S(6)} %copy.9.large_ref.refs_1_, bf16[128,128,128]{2,1,0:T(8,128)(2,1)S(1)} %prepare.1.c_ref.refs_3_, bf16[128,128]{1,0:T(8,128)(2,1)S(1)} %collective-permute-done.4.h_ref.refs_8_, ...), custom_call_target="tpu_custom_call" | custom-call | tf_op jit(solution)/shard_map/stage/pallas_call | solution.py:241
  38.6 1.3 %collective-permute-start.8 = (bf16[4,128,128]{2,1,0:T(8,128)(2,1)S(1)}, bf16[4,128,128]{2,1,0:T(8,128)(2,1)S(1)}, u32[]{:S(2)}, u32[]{:S(2)}) collective-permute-start(bf16[4,128,128]{2,1,0:T(8,128)(2,1)S(1)} %get-tuple-element.22), channel_id=1, source_target_pairs={{16,24},{8,0},{17,25},{9,1},{18,26},{10,2},{19,27},{11,3},{20,28},... | collective-permute-start | bytes 393224 | tf_op jit(solution)/shard_map/ppermute | solution.py:205
  40.7 3.4 %stage.12 = (bf16[128,128]{1,0:T(8,128)(2,1)S(1)}, bf16[4,128,128]{2,1,0:T(8,128)(2,1)}) custom-call(s32[1]{0:T(128)S(6)} %copy.8.small_ref.refs_0_, s32[1]{0:T(128)S(6)} %copy.9.large_ref.refs_1_, bf16[128,128,128]{2,1,0:T(8,128)(2,1)S(1)} %prepare.1.c_ref.refs_3_, bf16[128,128]{1,0:T(8,128)(2,1)S(1)} %collective-permute-done.6.h_ref.refs_9_, ...), custom_call_target="tpu_custom_call" | custom-call | tf_op jit(solution)/shard_map/stage/pallas_call | solution.py:241
  44.1 1.3 %collective-permute-start.7 = (bf16[128,128]{1,0:T(8,128)(2,1)S(1)}, bf16[128,128]{1,0:T(8,128)(2,1)S(1)}, u32[]{:S(2)}, u32[]{:S(2)}) collective-permute-start(bf16[128,128]{1,0:T(8,128)(2,1)S(1)} %get-tuple-element.21), channel_id=1, source_target_pairs={{5,6},{2,1},{13,14},{10,9},{21,22},{18,17},{29,30},{26,25}} | collective-permute-start | bytes 98312 | tf_op jit(solution)/shard_map/ppermute | solution.py:205
  45.4 12.7 %collective-permute-done.7.h_ref.refs_10_ = bf16[128,128]{1,0:T(8,128)(2,1)S(1)} collective-permute-done((bf16[128,128]{1,0:T(8,128)(2,1)S(1)}, bf16[128,128]{1,0:T(8,128)(2,1)S(1)}, u32[]{:S(2)}, u32[]{:S(2)}) %collective-permute-start.7) | collective-permute-done | bytes 32800 | tf_op jit(solution)/shard_map/ppermute | solution.py:205
  58.1 2.2 %copy-done.1 = bf16[128,128,128]{2,1,0:T(8,128)(2,1)S(1)} copy-done((bf16[128,128,128]{2,1,0:T(8,128)(2,1)S(1)}, bf16[128,128,128]{2,1,0:T(8,128)(2,1)}, u32[]{:S(2)}) %copy-start.1) | copy-done | bytes 4194328
  60.3 3.4 %stage.13 = (bf16[128,128]{1,0:T(8,128)(2,1)S(1)}, bf16[4,128,128]{2,1,0:T(8,128)(2,1)}) custom-call(s32[1]{0:T(128)S(6)} %copy.8.small_ref.refs_0_, s32[1]{0:T(128)S(6)} %copy.9.large_ref.refs_1_, bf16[128,128,128]{2,1,0:T(8,128)(2,1)S(1)} %copy-done.1, bf16[128,128]{1,0:T(8,128)(2,1)S(1)} %collective-permute-done.7.h_ref.refs_10_, ...), custom_call_target="tpu_custom_call" | custom-call | tf_op jit(solution)/shard_map/stage/pallas_call | solution.py:241
  63.7 1.3 %collective-permute-start.9 = (bf16[128,128]{1,0:T(8,128)(2,1)S(1)}, bf16[128,128]{1,0:T(8,128)(2,1)S(1)}, u32[]{:S(2)}, u32[]{:S(2)}) collective-permute-start(bf16[128,128]{1,0:T(8,128)(2,1)S(1)} %get-tuple-element.23), channel_id=1, source_target_pairs={{6,7},{1,0},{14,15},{9,8},{22,23},{17,16},{30,31},{25,24}} | collective-permute-start | bytes 98312 | tf_op jit(solution)/shard_map/ppermute | solution.py:205
  65.8 33.5 %final.1 = (bf16[32,128,128]{2,1,0:T(8,128)(2,1)}, bf16[32,128,128]{2,1,0:T(8,128)(2,1)S(1)}) custom-call(s32[1]{0:T(128)S(6)} %copy.8.small_ref.refs_0_, s32[1]{0:T(128)S(6)} %copy.9.large_ref.refs_1_, s32[2]{0:T(128)S(1)} %pad_add_fusion.refs_2_, bf16[128,128,128]{2,1,0:T(8,128)(2,1)S(1)} %copy-done.2, bf16[32,128,128]{2,1,0:T(8,128)(2,1)S(1)} %copy-done.4, ...), custom_call_target="tpu_custom_call" | custom-call | tf_op jit(solution)/shard_map/final/pallas_call | solution.py:253
  99.3 2.2 %collective-permute-start.10 = (bf16[32,128,128]{2,1,0:T(8,128)(2,1)S(1)}, bf16[32,128,128]{2,1,0:T(8,128)(2,1)S(1)}, u32[]{:S(2)}, u32[]{:S(2)}) collective-permute-start(bf16[32,128,128]{2,1,0:T(8,128)(2,1)S(1)} %get-tuple-element.25), channel_id=1, source_target_pairs={{1,0},{2,1},{3,2},{4,3},{5,4},{6,5},{7,6},{9,8},{10,9},{11,10},{12... | collective-permute-start | bytes 3145736 | tf_op jit(solution)/shard_map/ppermute | solution.py:263
  101.5 13.8 %collective-permute-done.10 = bf16[32,128,128]{2,1,0:T(8,128)(2,1)S(1)} collective-permute-done((bf16[32,128,128]{2,1,0:T(8,128)(2,1)S(1)}, bf16[32,128,128]{2,1,0:T(8,128)(2,1)S(1)}, u32[]{:S(2)}, u32[]{:S(2)}) %collective-permute-start.10) | collective-permute-done | bytes 1048608 | tf_op jit(solution)/shard_map/ppermute | solution.py:263
  115.4 1.1 broadcast_select_fusion
  (23 shorter events, 3.7 us)
Async XLA Ops:
  2.5 1.2 %copy-start.3 = (bf16[32,128,128]{2,1,0:T(8,128)(2,1)S(1)}, bf16[32,128,128]{2,1,0:T(8,128)(2,1)}, u32[]{:S(2)}) copy-start(bf16[32,128,128]{2,1,0:T(8,128)(2,1)} %refs_4_.1) | copy-start | bytes 3145732
  10.5 30.2 %copy-start = (bf16[128,128,128]{2,1,0:T(8,128)(2,1)}, bf16[128,128,128]{2,1,0:T(8,128)(2,1)S(1)}, u32[]{:S(2)}) copy-start(bf16[128,128,128]{2,1,0:T(8,128)(2,1)S(1)} %prepare.1.c_ref.refs_3_) | copy-start | bytes 12582916
  14.6 13.1 %collective-permute-start.2 = (bf16[4,128,128]{2,1,0:T(8,128)(2,1)S(1)}, bf16[4,128,128]{2,1,0:T(8,128)(2,1)S(1)}, u32[]{:S(2)}, u32[]{:S(2)}) collective-permute-start(bf16[4,128,128]{2,1,0:T(8,128)(2,1)S(1)} %get-tuple-element.16), channel_id=1, source_target_pairs={{0,8},{24,16},{1,9},{25,17},{2,10},{26,18},{3,11},{27,19},{4,12},{... | collective-permute-start | bytes 393224 | tf_op jit(solution)/shard_map/ppermute | solution.py:205
  18.6 3.1 %collective-permute-start = (bf16[128,128]{1,0:T(8,128)(2,1)S(1)}, bf16[128,128]{1,0:T(8,128)(2,1)S(1)}, u32[]{:S(2)}, u32[]{:S(2)}) collective-permute-start(bf16[128,128]{1,0:T(8,128)(2,1)S(1)} %get-tuple-element.14), channel_id=1, source_target_pairs={{0,1},{7,6},{8,9},{15,14},{16,17},{23,22},{24,25},{31,30}} | collective-permute-start | bytes 98312 | tf_op jit(solution)/shard_map/ppermute | solution.py:205
  25.1 2.6 %collective-permute-start.1 = (bf16[128,128]{1,0:T(8,128)(2,1)S(1)}, bf16[128,128]{1,0:T(8,128)(2,1)S(1)}, u32[]{:S(2)}, u32[]{:S(2)}) collective-permute-start(bf16[128,128]{1,0:T(8,128)(2,1)S(1)} %get-tuple-element.15), channel_id=1, source_target_pairs={{1,2},{6,5},{9,10},{14,13},{17,18},{22,21},{25,26},{30,29}} | collective-permute-start | bytes 98312 | tf_op jit(solution)/shard_map/ppermute | solution.py:205
  30.4 5.4 %collective-permute-start.5 = (bf16[4,128,128]{2,1,0:T(8,128)(2,1)S(1)}, bf16[4,128,128]{2,1,0:T(8,128)(2,1)S(1)}, u32[]{:S(2)}, u32[]{:S(2)}) collective-permute-start(bf16[4,128,128]{2,1,0:T(8,128)(2,1)S(1)} %get-tuple-element.19), channel_id=1, source_target_pairs={{8,16},{16,8},{9,17},{17,9},{10,18},{18,10},{11,19},{19,11},{12,20... | collective-permute-start | bytes 393224 | tf_op jit(solution)/shard_map/ppermute | solution.py:205
  31.1 0.7 collective-permute-start.3
  35.2 0.7 collective-permute-start.4
  38.6 19.5 %collective-permute-start.8 = (bf16[4,128,128]{2,1,0:T(8,128)(2,1)S(1)}, bf16[4,128,128]{2,1,0:T(8,128)(2,1)S(1)}, u32[]{:S(2)}, u32[]{:S(2)}) collective-permute-start(bf16[4,128,128]{2,1,0:T(8,128)(2,1)S(1)} %get-tuple-element.22), channel_id=1, source_target_pairs={{16,24},{8,0},{17,25},{9,1},{18,26},{10,2},{19,27},{11,3},{20,28},... | collective-permute-start | bytes 393224 | tf_op jit(solution)/shard_map/ppermute | solution.py:205
  39.9 25.9 %copy-start.4 = (bf16[32,128,128]{2,1,0:T(8,128)(2,1)S(1)}, bf16[32,128,128]{2,1,0:T(8,128)(2,1)}, u32[]{:S(2)}) copy-start(bf16[32,128,128]{2,1,0:T(8,128)(2,1)} %refs_4_.1) | copy-start | bytes 3145732
  39.9 0.8 collective-permute-start.6
  44.1 14.0 %collective-permute-start.7 = (bf16[128,128]{1,0:T(8,128)(2,1)S(1)}, bf16[128,128]{1,0:T(8,128)(2,1)S(1)}, u32[]{:S(2)}, u32[]{:S(2)}) collective-permute-start(bf16[128,128]{1,0:T(8,128)(2,1)S(1)} %get-tuple-element.21), channel_id=1, source_target_pairs={{5,6},{2,1},{13,14},{10,9},{21,22},{18,17},{29,30},{26,25}} | collective-permute-start | bytes 98312 | tf_op jit(solution)/shard_map/ppermute | solution.py:205
  58.1 2.2 %copy-start.1 = (bf16[128,128,128]{2,1,0:T(8,128)(2,1)S(1)}, bf16[128,128,128]{2,1,0:T(8,128)(2,1)}, u32[]{:S(2)}) copy-start(bf16[128,128,128]{2,1,0:T(8,128)(2,1)} %copy-done) | copy-start | bytes 12582916
  60.3 5.5 %copy-start.2 = (bf16[128,128,128]{2,1,0:T(8,128)(2,1)S(1)}, bf16[128,128,128]{2,1,0:T(8,128)(2,1)}, u32[]{:S(2)}) copy-start(bf16[128,128,128]{2,1,0:T(8,128)(2,1)} %copy-done) | copy-start | bytes 12582916
  63.7 2.1 %collective-permute-start.9 = (bf16[128,128]{1,0:T(8,128)(2,1)S(1)}, bf16[128,128]{1,0:T(8,128)(2,1)S(1)}, u32[]{:S(2)}, u32[]{:S(2)}) collective-permute-start(bf16[128,128]{1,0:T(8,128)(2,1)S(1)} %get-tuple-element.23), channel_id=1, source_target_pairs={{6,7},{1,0},{14,15},{9,8},{22,23},{17,16},{30,31},{25,24}} | collective-permute-start | bytes 98312 | tf_op jit(solution)/shard_map/ppermute | solution.py:205
  99.3 16.1 %collective-permute-start.10 = (bf16[32,128,128]{2,1,0:T(8,128)(2,1)S(1)}, bf16[32,128,128]{2,1,0:T(8,128)(2,1)S(1)}, u32[]{:S(2)}, u32[]{:S(2)}) collective-permute-start(bf16[32,128,128]{2,1,0:T(8,128)(2,1)S(1)} %get-tuple-element.25), channel_id=1, source_target_pairs={{1,0},{2,1},{3,2},{4,3},{5,4},{6,5},{7,6},{9,8},{10,9},{11,10},{12... | collective-permute-start | bytes 3145736 | tf_op jit(solution)/shard_map/ppermute | solution.py:263

commit v2 on v1

v2 whole, which is shorter than its diff:
```python
import functools

import jax
import jax.numpy as jnp
from jax import lax
from jax.experimental import pallas as pl
from jax.experimental.pallas import tpu as pltpu
from jax.sharding import PartitionSpec as P

SUB = 8
BIG = 1e30
TRANSPOSED = (((1,), (1,)), ((), ()))
PLAIN = (((1,), (0,)), ((), ()))
LIMIT = 40 * 1024 * 1024


def one_hot(rule, size):
    row = lax.broadcasted_iota(jnp.int32, (size, size), 0)
    col = lax.broadcasted_iota(jnp.int32, (size, size), 1)
    return jnp.where(rule(row, col), 1.0, 0.0).astype(jnp.bfloat16)


def interleave(size):
    return one_hot(lambda r, c: c == (r % SUB) * (size // SUB) + r // SUB, size)


def identity(size):
    return one_hot(lambda r, c: r == c, size)


def dot(a, b, dims):
    return lax.dot_general(a, b, dims, preferred_element_type=jnp.float32)


def split(block):
    wide = block.astype(jnp.float32)
    return [wide[i : i + SUB] for i in range(0, wide.shape[0], SUB)]


def join(parts):
    return jnp.concatenate(parts, axis=0).astype(jnp.bfloat16)


def fold_min(parts):
    parts = list(parts)
    while len(parts) > 1:
        parts = [jnp.minimum(a, b) for a, b in zip(parts[::2], parts[1::2])]
    low = parts[0]
    for shift in (4, 2, 1):
        low = jnp.minimum(low, pltpu.roll(low, shift, 0))
    return low


def relax(v, q1, q2):
    sub = lax.broadcasted_iota(jnp.int32, v[0].shape, 0)
    under = jnp.where(sub == 0, BIG, pltpu.roll(v[-1], 1, 0))
    over = jnp.where(sub == SUB - 1, BIG, pltpu.roll(v[0], SUB - 1, 0))
    low = fold_min(v)
    jump = low + q2
    below = [under] + v[:-1]
    above = v[1:] + [over]
    best = [
        jnp.minimum(jnp.minimum(x, jump), jnp.minimum(a, b) + q1)
        for x, a, b in zip(v, below, above)
    ]
    return best, low


def penalties(small_ref, large_ref, lanes):
    shape = (SUB, lanes)
    q1 = jnp.full(shape, small_ref[0], jnp.int32).astype(jnp.float32)
    q2 = jnp.full(shape, large_ref[0], jnp.int32).astype(jnp.float32)
    return q1, q2


def prepare_kernel(costs_ref, out_ref, wide_ref):
    rows, cols, depth = costs_ref.shape
    mix = interleave(depth)
    batch = 4

    def widen(y, carry):
        where = pl.ds(pl.multiple_of(y * cols, cols), cols)
        wide_ref[where, :] = costs_ref[y].astype(jnp.float32)
        return carry

    lax.fori_loop(0, rows, widen, 0, unroll=4)

    def column(x):
        return wide_ref[pl.ds(x, rows, stride=cols), :].astype(jnp.bfloat16)

    for g in range(cols // rows):
        span = pl.ds(g * rows, rows)

        def body(i, carry):
            parts = []
            for n in range(batch):
                y = i * batch + n
                t = g * rows + y
                parts += [
                    column(t),
                    column(cols - 1 - t),
                    costs_ref[y, span, :],
                    costs_ref[rows - 1 - y, span, :],
                ]
            block = jnp.concatenate(parts, axis=0)
            flat = dot(mix, block, TRANSPOSED).astype(jnp.bfloat16)
            lanes = 4 * rows
            for n in range(batch):
                out_ref[g * rows + i * batch + n] = flat[:, n * lanes : (n + 1) * lanes]
            return carry

        lax.fori_loop(0, rows // batch, body, 0, unroll=2)


def scan(v, c_ref, start, steps, q1, q2, unroll):
    def body(t, v):
        best, _ = relax(list(v), q1, q2)
        return tuple(a + b for a, b in zip(best, split(c_ref[start + t])))

    return list(lax.fori_loop(0, steps, body, tuple(v), unroll=unroll))


def lowered(v):
    low = fold_min(v)
    return [x - low for x in v]


def choose(table, here):
    found = jnp.int32(-1)
    for n, value in enumerate(table):
        found = jnp.where(here == n, jnp.int32(value), found)
    return found


def load_arrival(index, arrivals, held_ref):
    @pl.when(index < 0)
    def _():
        held_ref[...] = jnp.zeros(held_ref.shape, held_ref.dtype)

    for n, ref in enumerate(arrivals):

        @pl.when(index == n)
        def _():
            held_ref[...] = ref[...]


def stage_kernel(plan, s, rows, place_ref, small_ref, large_ref, c_ref, *refs):
    arrivals, out_ref, held_ref = refs[:s], refs[s], refs[s + 1]
    cols, depth, lanes = c_ref.shape
    groups = cols // rows
    col_here, row_here = place_ref[0], place_ref[1]
    q1, q2 = penalties(small_ref, large_ref, lanes)
    across = s < plan.cols - 1
    along = any(s in slots for slots in plan.slots)

    if across:

        @pl.when((col_here == s) | (col_here == plan.cols - 1 - s))
        def _():
            if s:
                v = split(arrivals[s - 1][...])
            else:
                v = [jnp.zeros((SUB, lanes), jnp.float32)] * (depth // SUB)
            v = scan(v, c_ref, 0, cols, q1, q2, 8)
            out_ref[...] = join(lowered(v))

    if along:
        hops = [slots.index(s) if s in slots else -1 for slots in plan.slots]
        source = [slots[j - 1] if j > 0 else -1 for slots, j in zip(plan.slots, hops)]
        hop = choose(hops, col_here)
        south = row_here == hop
        north = row_here == plan.rows - 1 - hop

        @pl.when((hop >= 0) & (south | north))
        def _():
            load_arrival(choose(source, col_here), arrivals, held_ref)
            base = 2 * rows + jnp.where(north, rows, 0)
            lane = lax.broadcasted_iota(jnp.int32, (SUB, lanes), 1)
            packed = None
            for g in range(groups):
                turn = lax.rem(base + lanes - g * rows, lanes)
                v = [pltpu.roll(x, turn, 1) for x in split(held_ref[...])]
                v = lowered(scan(v, c_ref, g * rows, rows, q1, q2, 8))
                turn = lax.rem(lanes - base + g * rows, lanes)
                v = [pltpu.roll(x, turn, 1) for x in v]
                mine = (lane >= g * rows) & (lane < (g + 1) * rows)
                packed = v if packed is None else [jnp.where(mine, a, b) for a, b in zip(v, packed)]
            out_ref[...] = join(packed)


def skew(v, lane, sub):
    count = len(v)
    bit = 1
    while bit < SUB:
        taken = (lane & bit) != 0
        inner = sub < SUB - bit
        up = [pltpu.roll(a, SUB - bit, 0) for a in v]
        v = [
            jnp.where(taken, jnp.where(inner, up[k], up[(k + 1) % count]), v[k])
            for k in range(count)
        ]
        bit *= 2
    while bit < SUB * count:
        taken = (lane & bit) != 0
        v = [jnp.where(taken, v[(k + bit // SUB) % count], v[k]) for k in range(count)]
        bit *= 2
    return v


def final_kernel(plan, stages, *refs):
    place_ref, small_ref, large_ref, c_ref, costs_ref = refs[:5]
    arrivals = refs[5 : 5 + stages]
    left_ref, skew_ref = refs[5 + stages : 7 + stages]
    held_ref, path_ref, east_ref, west_ref, v_ref = refs[7 + stages :]
    rows, cols, depth = costs_ref.shape
    lanes = c_ref.shape[2]
    q1, q2 = penalties(small_ref, large_ref, lanes)
    col_here, row_here = place_ref[0], place_ref[1]
    lane = lax.broadcasted_iota(jnp.int32, (SUB, lanes), 1)
    sub = lax.broadcasted_iota(jnp.int32, (SUB, lanes), 0)

    load_arrival(col_here - 1, arrivals, held_ref.at[0])
    load_arrival(plan.cols - 2 - col_here, arrivals, held_ref.at[1])
    for n in range(2):
        hop = row_here - 1 if n == 0 else plan.rows - 2 - row_here
        source = jnp.int32(-1)
        for j in range(plan.rows - 1):
            found = choose([slots[j] for slots in plan.slots], col_here)
            source = jnp.where(hop == j, found, source)
        load_arrival(source, arrivals, held_ref.at[2 + n])

    east, west = split(held_ref[0]), split(held_ref[1])
    v = [jnp.where(lane < rows, a, b) for a, b in zip(east, west)]
    for g in range(cols // rows):
        south = [pltpu.roll(x, (2 * rows - g * rows) % lanes, 1) for x in split(held_ref[2])]
        north = [pltpu.roll(x, (3 * rows - g * rows) % lanes, 1) for x in split(held_ref[3])]
        fresh = [jnp.where(lane < 3 * rows, a, b) for a, b in zip(south, north)]
        v = [jnp.where(lane < 2 * rows, a, b) for a, b in zip(v, fresh)]

        def body(y, v):
            t = g * rows + y
            best, low = relax(list(v), q1, q2)
            path_ref[t] = join([x - low for x in best])
            return tuple(a + b for a, b in zip(best, split(c_ref[t])))

        v = list(lax.fori_loop(0, rows, body, tuple(v), unroll=8))

    ident = identity(lanes)
    batch = 4
    for g in range(cols // rows):

        def turn(i, carry):
            t = g * rows + i * batch
            block = path_ref[pl.ds(t, batch)].reshape(batch * depth, lanes)
            flat = dot(ident, block, TRANSPOSED)
            for n in range(batch):
                y = i * batch + n
                part = flat[:, n * depth : (n + 1) * depth]
                x = g * rows + y
                east_ref[pl.ds(pl.multiple_of(x * rows, rows), rows), :] = part[:rows]
                x = cols - 1 - x
                west_ref[pl.ds(pl.multiple_of(x * rows, rows), rows), :] = part[rows : 2 * rows]
                v_ref[0, y, g * rows : (g + 1) * rows] = part[2 * rows : 3 * rows]
                v_ref[1, rows - 1 - y, g * rows : (g + 1) * rows] = part[3 * rows :]
            return carry

        lax.fori_loop(0, rows // batch, turn, 0, unroll=2)

    mix = interleave(depth)

    def finish(y, carry):
        crossing = pl.ds(y, cols, stride=rows)
        h_rows = east_ref[crossing, :] + west_ref[crossing, :]
        v_rows = v_ref[0, y] + v_ref[1, y]
        both = jnp.concatenate([h_rows, v_rows], axis=0).astype(jnp.bfloat16)
        extra = dot(both, mix, PLAIN)
        summed = extra[:cols] + extra[cols:] + 4.0 * costs_ref[y].astype(jnp.float32)
        left = (summed * (1.0 / 64.0)).astype(jnp.bfloat16)
        left_ref[y] = left
        skew_ref[y] = join(skew(split(left), lane, sub))
        return carry

    lax.fori_loop(0, rows, finish, 0, unroll=4)


class Plan:
    def __init__(self, rows, cols):
        self.rows, self.cols = rows, cols
        self.slots = []
        for c in range(cols):
            busy = {c - 1, c, cols - 2 - c, cols - 1 - c}
            free = [s for s in range(cols + 4 + rows) if s not in busy or s >= cols - 1]
            self.slots.append(free[: rows - 1])
        last = [slots[-1] + 1 for slots in self.slots if slots]
        self.stages = max([cols - 1] + last)

    def route(self, s):
        pairs = []
        if s < self.cols - 1:
            for r in range(self.rows):
                pairs += [
                    ((r, s), (r, s + 1)),
                    ((r, self.cols - 1 - s), (r, self.cols - 2 - s)),
                ]
        for c, slots in enumerate(self.slots):
            if s in slots:
                j = slots.index(s)
                pairs += [
                    ((j, c), (j + 1, c)),
                    ((self.rows - 1 - j, c), (self.rows - 2 - j, c)),
                ]
        number = lambda place: place[0] * self.cols + place[1]
        return [(number(a), number(b)) for a, b in pairs]


def in_vmem(count):
    return [pl.BlockSpec(memory_space=pltpu.VMEM)] * count


def in_smem(count):
    return [pl.BlockSpec(memory_space=pltpu.SMEM)] * count


def shards(costs, p_small, p_large):
    rows, cols, depth = costs.shape
    lanes = 4 * rows
    plan = Plan(lax.axis_size("row"), lax.axis_size("col"))
    params = pltpu.CompilerParams(vmem_limit_bytes=LIMIT)
    place = jnp.stack([lax.axis_index("col"), lax.axis_index("row")]).astype(jnp.int32)
    layered = pl.pallas_call(
        prepare_kernel,
        out_shape=jax.ShapeDtypeStruct((cols, depth, lanes), jnp.bfloat16),
        in_specs=in_vmem(1),
        out_specs=pl.BlockSpec(memory_space=pltpu.VMEM),
        scratch_shapes=[pltpu.VMEM((rows * cols, depth), jnp.float32)],
        compiler_params=params,
        name="prepare",
    )(costs)

    front = jax.ShapeDtypeStruct((depth, lanes), jnp.bfloat16)
    arrivals = []
    for s in range(plan.stages):
        sent = pl.pallas_call(
            functools.partial(stage_kernel, plan, s, rows),
            out_shape=front,
            in_specs=in_smem(3) + in_vmem(1 + s),
            out_specs=pl.BlockSpec(memory_space=pltpu.VMEM),
            scratch_shapes=[pltpu.VMEM((depth, lanes), jnp.bfloat16)],
            compiler_params=params,
            name=f"stage{s}",
        )(place, p_small, p_large, layered, *arrivals)
        arrivals.append(lax.ppermute(sent, ("row", "col"), plan.route(s)))

    tile = jax.ShapeDtypeStruct((rows, cols, depth), jnp.bfloat16)
    left_view, skewed = pl.pallas_call(
        functools.partial(final_kernel, plan, plan.stages),
        out_shape=(tile, tile),
        in_specs=in_smem(3) + in_vmem(2 + plan.stages),
        out_specs=tuple(in_vmem(2)),
        scratch_shapes=[
            pltpu.VMEM((4, depth, lanes), jnp.bfloat16),
            pltpu.VMEM((cols, depth, lanes), jnp.bfloat16),
            pltpu.VMEM((cols * rows, depth), jnp.float32),
            pltpu.VMEM((cols * rows, depth), jnp.float32),
            pltpu.VMEM((2, rows, cols, depth), jnp.float32),
        ],
        compiler_params=params,
        name="final",
    )(place, p_small, p_large, layered, costs, *arrivals)

    arrived = lax.ppermute(skewed, "col", [(i, i - 1) for i in range(1, plan.cols)])
    x = lax.broadcasted_iota(jnp.int32, (cols, depth), 0)
    d = lax.broadcasted_iota(jnp.int32, (cols, depth), 1)
    right_view = jnp.where((x + d < cols)[None], skewed, arrived)
    return left_view, right_view


def solution(mesh):
    placed = (P("row", "col", None), P(), P())
    return jax.shard_map(
        shards,
        mesh=mesh,
        in_specs=placed,
        out_specs=(P("row", "col", None), P("row", "col", None)),
        check_vma=False,
    )
```

time: 117 us -> 90.8 us (0.78)
  Pallas kernels: 61.9 us -> 32 us
  waiting for transfers between devices: 30.1 us -> 41.3 us
  local copies, waits for them, and re-layouts: 5.36 us -> 1.22 us
  starting transfers between devices: 15.7 us -> 12.7 us
    pallas_call x8, Pallas kernels: 55.1 us -> 25.5 us  [the longest x1 13.2 us: shards(): pl.pallas_call(functools.partial(final_kernel, plan, plan.stages), out_sh...]
    ppermute x11 -> x8, waiting for transfers between devices: 30.1 us -> 41.3 us  [the longest x7 24.2 us: shards(): arrivals.append(lax.ppermute(sent, ('row', 'col'), plan.route(s)))]
    unnamed x11 -> x2, local copies, waits for them, and re-layouts: 5.33 us -> 1.22 us
    ppermute x11 -> x8, starting transfers between devices: 15.7 us -> 12.7 us  [the longest x7 10.4 us: shards(): arrivals.append(lax.ppermute(sent, ('row', 'col'), plan.route(s)))]
  transfers between devices with their start and end apart: 11 -> 8, of which waited for: 5 -> 7; matrix products, arithmetic and copies ran while one was open for 0% -> 0% of each run, Pallas kernels for 9% -> 0%
where the time goes in v2:
time: 90.8 us; the launch traced here: 90.5 us
  waiting for transfers between devices  41.3 us (45%)
  Pallas kernels  32 us (35%)
  starting transfers between devices  12.7 us (14%)
  between operations  2.08 us (2%)
  local copies, waits for them, and re-layouts  1.22 us (1%)
  other arithmetic  1.21 us (1%)
    ppermute x7, waiting for transfers between devices, shards(): arrivals.append(lax.ppermute(sent, ('row', 'col'), plan.route(s)))  24.2 us
    ppermute x1, waiting for transfers between devices, shards(): lax.ppermute(skewed, 'col', [(i, i - 1) for i in range(1, plan.cols)])  17.1 us
    pallas_call x1, Pallas kernels, shards(): pl.pallas_call(functools.partial(final_kernel, plan, plan.stages), out_sh...  13.2 us
    pallas_call x7, Pallas kernels, shards(): pl.pallas_call(functools.partial(stage_kernel, plan, s, rows), out_shape=...  12.2 us
    ppermute x7, starting transfers between devices, shards(): arrivals.append(lax.ppermute(sent, ('row', 'col'), plan.route(s)))  10.4 us
    pallas_call x1, Pallas kernels, shards(): pl.pallas_call(prepare_kernel, out_shape=jax.ShapeDtypeStruct((cols, dept...  6.59 us
    ppermute x1, starting transfers between devices, shards(): lax.ppermute(skewed, 'col', [(i, i - 1) for i in range(1, plan.cols)])  2.25 us
  transfers between devices with their start and end apart: 8, of which 7 were waited for; matrix products, arithmetic and copies ran while one was open for 0% of the time, Pallas kernels for 0%

profile of v2, /device:TPU:1, one launch (start us, length us, event | category | flops | bytes accessed | tf_op | source)
XLA Modules:
  0.0 90.5 jit_solution(9941757993533488217)
XLA Ops:
  0.6 1.2 %copy-done = bf16[32,128,128]{2,1,0:T(8,128)(2,1)S(1)} copy-done((bf16[32,128,128]{2,1,0:T(8,128)(2,1)S(1)}, bf16[32,128,128]{2,1,0:T(8,128)(2,1)}, u32[]{:S(2)}) %copy-start) | copy-done | bytes 1048600
  1.9 6.6 %prepare.1.c_ref.refs_3_ = bf16[128,128,128]{2,1,0:T(8,128)(2,1)S(1)} custom-call(bf16[32,128,128]{2,1,0:T(8,128)(2,1)S(1)} %copy-done), custom_call_target="tpu_custom_call" | custom-call | tf_op jit(solution)/shard_map/prepare/pallas_call | solution.py:330
  10.4 1.3 %collective-permute-start = (bf16[128,128]{1,0:T(8,128)(2,1)S(1)}, bf16[128,128]{1,0:T(8,128)(2,1)S(1)}, u32[]{:S(2)}, u32[]{:S(2)}) collective-permute-start(bf16[128,128]{1,0:T(8,128)(2,1)S(1)} %stage0.1), channel_id=1, source_target_pairs={{0,1},{7,6},{8,9},{15,14},{16,17},{23,22},{24,25},{31,30},{2,10},{... | collective-permute-start | bytes 98312 | tf_op jit(solution)/shard_map/ppermute | solution.py:352
  11.7 3.3 %collective-permute-done.refs_0_.refs_5_ = bf16[128,128]{1,0:T(8,128)(2,1)S(1)} collective-permute-done((bf16[128,128]{1,0:T(8,128)(2,1)S(1)}, bf16[128,128]{1,0:T(8,128)(2,1)S(1)}, u32[]{:S(2)}, u32[]{:S(2)}) %collective-permute-start) | collective-permute-done | bytes 32800 | tf_op jit(solution)/shard_map/ppermute | solution.py:352
  15.0 3.2 %stage1.1 = bf16[128,128]{1,0:T(8,128)(2,1)S(1)} custom-call(s32[2]{0:T(128)S(1)} %pad_add_fusion.place_ref.refs_0_, s32[1]{0:T(128)S(6)} %copy.5.small_ref.refs_1_, s32[1]{0:T(128)S(6)} %copy.6.large_ref.refs_2_, bf16[128,128,128]{2,1,0:T(8,128)(2,1)S(1)} %prepare.1.c_ref.refs_3_, bf16[128,128]{1,0:T(8,128)(2,1)S(1)} %collective-permute-done.refs_0_.refs_5_), custom_call_target="tpu_custom_call" | custom-call | tf_op jit(solution)/shard_map/stage1/pallas_call | solution.py:343
  18.2 3.3 %collective-permute-start.1 = (bf16[128,128]{1,0:T(8,128)(2,1)S(1)}, bf16[128,128]{1,0:T(8,128)(2,1)S(1)}, u32[]{:S(2)}, u32[]{:S(2)}) collective-permute-start(bf16[128,128]{1,0:T(8,128)(2,1)S(1)} %stage1.1), channel_id=1, source_target_pairs={{1,2},{6,5},{9,10},{14,13},{17,18},{22,21},{25,26},{30,29},{0,8},{... | collective-permute-start | bytes 98312 | tf_op jit(solution)/shard_map/ppermute | solution.py:352
  21.5 1.0 %collective-permute-done.1.refs_1_.refs_6_ = bf16[128,128]{1,0:T(8,128)(2,1)S(1)} collective-permute-done((bf16[128,128]{1,0:T(8,128)(2,1)S(1)}, bf16[128,128]{1,0:T(8,128)(2,1)S(1)}, u32[]{:S(2)}, u32[]{:S(2)}) %collective-permute-start.1) | collective-permute-done | bytes 32800 | tf_op jit(solution)/shard_map/ppermute | solution.py:352
  22.5 3.7 %stage2.1 = bf16[128,128]{1,0:T(8,128)(2,1)S(1)} custom-call(s32[2]{0:T(128)S(1)} %pad_add_fusion.place_ref.refs_0_, s32[1]{0:T(128)S(6)} %copy.5.small_ref.refs_1_, s32[1]{0:T(128)S(6)} %copy.6.large_ref.refs_2_, bf16[128,128,128]{2,1,0:T(8,128)(2,1)S(1)} %prepare.1.c_ref.refs_3_, bf16[128,128]{1,0:T(8,128)(2,1)S(1)} %collective-permute-done.refs_0_.refs_5_, ...), custom_call_target="tpu_custom_call" | custom-call | tf_op jit(solution)/shard_map/stage2/pallas_call | solution.py:343
  26.2 1.3 %collective-permute-start.2 = (bf16[128,128]{1,0:T(8,128)(2,1)S(1)}, bf16[128,128]{1,0:T(8,128)(2,1)S(1)}, u32[]{:S(2)}, u32[]{:S(2)}) collective-permute-start(bf16[128,128]{1,0:T(8,128)(2,1)S(1)} %stage2.1), channel_id=1, source_target_pairs={{2,3},{5,4},{10,11},{13,12},{18,19},{21,20},{26,27},{29,28},{8,16}... | collective-permute-start | bytes 98312 | tf_op jit(solution)/shard_map/ppermute | solution.py:352
  27.5 1.0 %collective-permute-done.2.refs_2_.refs_7_ = bf16[128,128]{1,0:T(8,128)(2,1)S(1)} collective-permute-done((bf16[128,128]{1,0:T(8,128)(2,1)S(1)}, bf16[128,128]{1,0:T(8,128)(2,1)S(1)}, u32[]{:S(2)}, u32[]{:S(2)}) %collective-permute-start.2) | collective-permute-done | bytes 32800 | tf_op jit(solution)/shard_map/ppermute | solution.py:352
  28.5 0.6 stage3.1
  29.1 0.7 collective-permute-start.3
  29.7 0.6 stage4.1
  30.3 1.3 %collective-permute-start.4 = (bf16[128,128]{1,0:T(8,128)(2,1)S(1)}, bf16[128,128]{1,0:T(8,128)(2,1)S(1)}, u32[]{:S(2)}, u32[]{:S(2)}) collective-permute-start(bf16[128,128]{1,0:T(8,128)(2,1)S(1)} %stage4.1), channel_id=1, source_target_pairs={{4,5},{3,2},{12,13},{11,10},{20,21},{19,18},{28,29},{27,26},{17,25... | collective-permute-start | bytes 98312 | tf_op jit(solution)/shard_map/ppermute | solution.py:352
  31.6 14.1 %collective-permute-done.4.refs_4_.refs_9_ = bf16[128,128]{1,0:T(8,128)(2,1)S(1)} collective-permute-done((bf16[128,128]{1,0:T(8,128)(2,1)S(1)}, bf16[128,128]{1,0:T(8,128)(2,1)S(1)}, u32[]{:S(2)}, u32[]{:S(2)}) %collective-permute-start.4) | collective-permute-done | bytes 32800 | tf_op jit(solution)/shard_map/ppermute | solution.py:352
  46.3 1.3 %collective-permute-start.5 = (bf16[128,128]{1,0:T(8,128)(2,1)S(1)}, bf16[128,128]{1,0:T(8,128)(2,1)S(1)}, u32[]{:S(2)}, u32[]{:S(2)}) collective-permute-start(bf16[128,128]{1,0:T(8,128)(2,1)S(1)} %stage5.1), channel_id=1, source_target_pairs={{5,6},{2,1},{13,14},{10,9},{21,22},{18,17},{29,30},{26,25},{19,27}... | collective-permute-start | bytes 98312 | tf_op jit(solution)/shard_map/ppermute | solution.py:352
  47.6 3.9 %collective-permute-done.5.refs_5_.refs_10_ = bf16[128,128]{1,0:T(8,128)(2,1)S(1)} collective-permute-done((bf16[128,128]{1,0:T(8,128)(2,1)S(1)}, bf16[128,128]{1,0:T(8,128)(2,1)S(1)}, u32[]{:S(2)}, u32[]{:S(2)}) %collective-permute-start.5) | collective-permute-done | bytes 32800 | tf_op jit(solution)/shard_map/ppermute | solution.py:352
  51.5 3.2 %stage6.1 = bf16[128,128]{1,0:T(8,128)(2,1)S(1)} custom-call(s32[2]{0:T(128)S(1)} %pad_add_fusion.place_ref.refs_0_, s32[1]{0:T(128)S(6)} %copy.5.small_ref.refs_1_, s32[1]{0:T(128)S(6)} %copy.6.large_ref.refs_2_, bf16[128,128,128]{2,1,0:T(8,128)(2,1)S(1)} %prepare.1.c_ref.refs_3_, bf16[128,128]{1,0:T(8,128)(2,1)S(1)} %collective-permute-done.refs_0_.refs_5_, ...), custom_call_target="tpu_custom_call" | custom-call | tf_op jit(solution)/shard_map/stage6/pallas_call | solution.py:343
  54.7 1.3 %collective-permute-start.6 = (bf16[128,128]{1,0:T(8,128)(2,1)S(1)}, bf16[128,128]{1,0:T(8,128)(2,1)S(1)}, u32[]{:S(2)}, u32[]{:S(2)}) collective-permute-start(bf16[128,128]{1,0:T(8,128)(2,1)S(1)} %stage6.1), channel_id=1, source_target_pairs={{6,7},{1,0},{14,15},{9,8},{22,23},{17,16},{30,31},{25,24},{18,26},... | collective-permute-start | bytes 98312 | tf_op jit(solution)/shard_map/ppermute | solution.py:352
  56.0 0.8 collective-permute-done.6.refs_11_
  56.8 13.2 %final.1 = (bf16[32,128,128]{2,1,0:T(8,128)(2,1)}, bf16[32,128,128]{2,1,0:T(8,128)(2,1)S(1)}) custom-call(s32[2]{0:T(128)S(1)} %pad_add_fusion.place_ref.refs_0_, s32[1]{0:T(128)S(6)} %copy.5.small_ref.refs_1_, s32[1]{0:T(128)S(6)} %copy.6.large_ref.refs_2_, bf16[128,128,128]{2,1,0:T(8,128)(2,1)S(1)} %prepare.1.c_ref.refs_3_, ...), custom_call_target="tpu_custom_call" | custom-call | tf_op jit(solution)/shard_map/final/pallas_call | solution.py:355
  70.0 2.2 %collective-permute-start.7 = (bf16[32,128,128]{2,1,0:T(8,128)(2,1)S(1)}, bf16[32,128,128]{2,1,0:T(8,128)(2,1)S(1)}, u32[]{:S(2)}, u32[]{:S(2)}) collective-permute-start(bf16[32,128,128]{2,1,0:T(8,128)(2,1)S(1)} %get-tuple-element.5), channel_id=1, source_target_pairs={{1,0},{2,1},{3,2},{4,3},{5,4},{6,5},{7,6},{9,8},{10,9},{11,10},{12... | collective-permute-start | bytes 3145736 | tf_op jit(solution)/shard_map/ppermute | solution.py:371
  72.3 17.1 %collective-permute-done.7 = bf16[32,128,128]{2,1,0:T(8,128)(2,1)S(1)} collective-permute-done((bf16[32,128,128]{2,1,0:T(8,128)(2,1)S(1)}, bf16[32,128,128]{2,1,0:T(8,128)(2,1)S(1)}, u32[]{:S(2)}, u32[]{:S(2)}) %collective-permute-start.7) | collective-permute-done | bytes 1048608 | tf_op jit(solution)/shard_map/ppermute | solution.py:371
  89.4 1.1 %broadcast_select_fusion = bf16[32,128,128]{2,1,0:T(8,128)(2,1)} fusion(bf16[32,128,128]{2,1,0:T(8,128)(2,1)S(1)} %get-tuple-element.5, bf16[32,128,128]{2,1,0:T(8,128)(2,1)S(1)} %collective-permute-done.7, pred[128,128]{1,0:T(8,128)(4,1)S(1)} %add_compare_fusion), kind=kLoop, calls=%fused_computation | loop fusion | flops 524288 | bytes 3162112 | tf_op jit(solution)/shard_map/jit(_where)/select_n | solution.py:374
  (6 shorter events, 1.2 us)
Async XLA Ops:
  0.6 1.2 %copy-start = (bf16[32,128,128]{2,1,0:T(8,128)(2,1)S(1)}, bf16[32,128,128]{2,1,0:T(8,128)(2,1)}, u32[]{:S(2)}) copy-start(bf16[32,128,128]{2,1,0:T(8,128)(2,1)} %refs_4_.1) | copy-start | bytes 3145732
  10.4 4.6 %collective-permute-start = (bf16[128,128]{1,0:T(8,128)(2,1)S(1)}, bf16[128,128]{1,0:T(8,128)(2,1)S(1)}, u32[]{:S(2)}, u32[]{:S(2)}) collective-permute-start(bf16[128,128]{1,0:T(8,128)(2,1)S(1)} %stage0.1), channel_id=1, source_target_pairs={{0,1},{7,6},{8,9},{15,14},{16,17},{23,22},{24,25},{31,30},{2,10},{... | collective-permute-start | bytes 98312 | tf_op jit(solution)/shard_map/ppermute | solution.py:352
  18.2 4.3 %collective-permute-start.1 = (bf16[128,128]{1,0:T(8,128)(2,1)S(1)}, bf16[128,128]{1,0:T(8,128)(2,1)S(1)}, u32[]{:S(2)}, u32[]{:S(2)}) collective-permute-start(bf16[128,128]{1,0:T(8,128)(2,1)S(1)} %stage1.1), channel_id=1, source_target_pairs={{1,2},{6,5},{9,10},{14,13},{17,18},{22,21},{25,26},{30,29},{0,8},{... | collective-permute-start | bytes 98312 | tf_op jit(solution)/shard_map/ppermute | solution.py:352
  26.2 2.3 %collective-permute-start.2 = (bf16[128,128]{1,0:T(8,128)(2,1)S(1)}, bf16[128,128]{1,0:T(8,128)(2,1)S(1)}, u32[]{:S(2)}, u32[]{:S(2)}) collective-permute-start(bf16[128,128]{1,0:T(8,128)(2,1)S(1)} %stage2.1), channel_id=1, source_target_pairs={{2,3},{5,4},{10,11},{13,12},{18,19},{21,20},{26,27},{29,28},{8,16}... | collective-permute-start | bytes 98312 | tf_op jit(solution)/shard_map/ppermute | solution.py:352
  29.1 0.7 collective-permute-start.3
  30.3 15.4 %collective-permute-start.4 = (bf16[128,128]{1,0:T(8,128)(2,1)S(1)}, bf16[128,128]{1,0:T(8,128)(2,1)S(1)}, u32[]{:S(2)}, u32[]{:S(2)}) collective-permute-start(bf16[128,128]{1,0:T(8,128)(2,1)S(1)} %stage4.1), channel_id=1, source_target_pairs={{4,5},{3,2},{12,13},{11,10},{20,21},{19,18},{28,29},{27,26},{17,25... | collective-permute-start | bytes 98312 | tf_op jit(solution)/shard_map/ppermute | solution.py:352
  46.3 5.2 %collective-permute-start.5 = (bf16[128,128]{1,0:T(8,128)(2,1)S(1)}, bf16[128,128]{1,0:T(8,128)(2,1)S(1)}, u32[]{:S(2)}, u32[]{:S(2)}) collective-permute-start(bf16[128,128]{1,0:T(8,128)(2,1)S(1)} %stage5.1), channel_id=1, source_target_pairs={{5,6},{2,1},{13,14},{10,9},{21,22},{18,17},{29,30},{26,25},{19,27}... | collective-permute-start | bytes 98312 | tf_op jit(solution)/shard_map/ppermute | solution.py:352
  54.7 2.1 %collective-permute-start.6 = (bf16[128,128]{1,0:T(8,128)(2,1)S(1)}, bf16[128,128]{1,0:T(8,128)(2,1)S(1)}, u32[]{:S(2)}, u32[]{:S(2)}) collective-permute-start(bf16[128,128]{1,0:T(8,128)(2,1)S(1)} %stage6.1), channel_id=1, source_target_pairs={{6,7},{1,0},{14,15},{9,8},{22,23},{17,16},{30,31},{25,24},{18,26},... | collective-permute-start | bytes 98312 | tf_op jit(solution)/shard_map/ppermute | solution.py:352
  70.0 19.4 %collective-permute-start.7 = (bf16[32,128,128]{2,1,0:T(8,128)(2,1)S(1)}, bf16[32,128,128]{2,1,0:T(8,128)(2,1)S(1)}, u32[]{:S(2)}, u32[]{:S(2)}) collective-permute-start(bf16[32,128,128]{2,1,0:T(8,128)(2,1)S(1)} %get-tuple-element.5), channel_id=1, source_target_pairs={{1,0},{2,1},{3,2},{4,3},{5,4},{6,5},{7,6},{9,8},{10,9},{11,10},{12... | collective-permute-start | bytes 3145736 | tf_op jit(solution)/shard_map/ppermute | solution.py:371

commit v3 on v2

v3 whole, which is shorter than its diff:
```python
import functools

import jax
import jax.numpy as jnp
from jax import lax
from jax.experimental import pallas as pl
from jax.experimental.pallas import tpu as pltpu
from jax.sharding import PartitionSpec as P

SUB = 8
BIG = 1e30
TRANSPOSED = (((1,), (1,)), ((), ()))
PLAIN = (((1,), (0,)), ((), ()))
LIMIT = 40 * 1024 * 1024


def one_hot(rule, size):
    row = lax.broadcasted_iota(jnp.int32, (size, size), 0)
    col = lax.broadcasted_iota(jnp.int32, (size, size), 1)
    return jnp.where(rule(row, col), 1.0, 0.0).astype(jnp.bfloat16)


def interleave(size):
    return one_hot(lambda r, c: c == (r % SUB) * (size // SUB) + r // SUB, size)


def identity(size):
    return one_hot(lambda r, c: r == c, size)


def dot(a, b, dims):
    return lax.dot_general(a, b, dims, preferred_element_type=jnp.float32)


def split(block):
    wide = block.astype(jnp.float32)
    return [wide[i : i + SUB] for i in range(0, wide.shape[0], SUB)]


def join(parts):
    return jnp.concatenate(parts, axis=0).astype(jnp.bfloat16)


def fold_min(parts):
    parts = list(parts)
    while len(parts) > 1:
        parts = [jnp.minimum(a, b) for a, b in zip(parts[::2], parts[1::2])]
    low = parts[0]
    for shift in (4, 2, 1):
        low = jnp.minimum(low, pltpu.roll(low, shift, 0))
    return low


def relax(v, q1, q2):
    sub = lax.broadcasted_iota(jnp.int32, v[0].shape, 0)
    under = jnp.where(sub == 0, BIG, pltpu.roll(v[-1], 1, 0))
    over = jnp.where(sub == SUB - 1, BIG, pltpu.roll(v[0], SUB - 1, 0))
    low = fold_min(v)
    jump = low + q2
    below = [under] + v[:-1]
    above = v[1:] + [over]
    best = [
        jnp.minimum(jnp.minimum(x, jump), jnp.minimum(a, b) + q1)
        for x, a, b in zip(v, below, above)
    ]
    return best, low


def penalties(small_ref, large_ref, lanes):
    shape = (SUB, lanes)
    q1 = jnp.full(shape, small_ref[0], jnp.int32).astype(jnp.float32)
    q2 = jnp.full(shape, large_ref[0], jnp.int32).astype(jnp.float32)
    return q1, q2


def prepare_kernel(costs_ref, out_ref, wide_ref):
    rows, cols, depth = costs_ref.shape
    pack = cols // rows
    mix = interleave(depth)
    batch = 4

    def widen(y, carry):
        where = pl.ds(pl.multiple_of(y * cols, cols), cols)
        wide_ref[where, :] = costs_ref[y].astype(jnp.float32)
        return carry

    lax.fori_loop(0, rows, widen, 0, unroll=4)

    def body(i, carry):
        parts = [
            wide_ref[pl.ds(i * batch * pack + n, rows, stride=cols), :].astype(jnp.bfloat16)
            for n in range(batch * pack)
        ]
        flat = dot(mix, jnp.concatenate(parts, axis=0), TRANSPOSED).astype(jnp.bfloat16)
        for n in range(batch):
            out_ref[i * batch + n] = flat[:, n * cols : (n + 1) * cols]
        return carry

    lax.fori_loop(0, cols // pack // batch, body, 0, unroll=2)


def turn_rows(costs_ref, tiles_ref):
    rows, cols, depth = costs_ref.shape
    mix = interleave(depth)
    batch = 4

    def body(i, carry):
        block = costs_ref[pl.ds(i * batch, batch)].reshape(batch * cols, depth)
        flat = dot(mix, block, TRANSPOSED).astype(jnp.bfloat16)
        for n in range(batch):
            tiles_ref[i * batch + n] = flat[:, n * cols : (n + 1) * cols]
        return carry

    lax.fori_loop(0, rows // batch, body, 0, unroll=2)


def sweep(v, tiles_ref, sums_ref, rows, west, first, q1, q2):
    tiles, depth, lanes = tiles_ref.shape
    pack = lanes // rows
    lane = lax.broadcasted_iota(jnp.int32, (SUB, lanes), 1)
    groups = [jnp.where(west, pack - 1 - j, j) for j in range(pack)]
    inward = [lax.rem(lanes - g * rows, lanes) for g in groups]
    outward = [g * rows for g in groups]
    mine = [(lane >= g * rows) & (lane < (g + 1) * rows) for g in groups]

    def body(i, v):
        v = list(v)
        at = jnp.where(west, tiles - 1 - i, i)
        tile = split(tiles_ref[at])
        kept = None if first else split(sums_ref[at])
        found = None
        for j in range(pack):
            best, low = relax(v, q1, q2)
            extra = [pltpu.roll(x - low, outward[j], 1) for x in best]
            v = [a + pltpu.roll(c, inward[j], 1) for a, c in zip(best, tile)]
            if found is None:
                found = extra
            else:
                found = [jnp.where(mine[j], a, b) for a, b in zip(extra, found)]
        if kept is not None:
            found = [a + b for a, b in zip(found, kept)]
        sums_ref[at] = join(found)
        return tuple(v)

    return list(lax.fori_loop(0, tiles, body, tuple(v)))


def descend(v, tiles_ref, north, q1, q2):
    rows = tiles_ref.shape[0]

    def body(i, v):
        best, _ = relax(list(v), q1, q2)
        at = jnp.where(north, rows - 1 - i, i)
        return tuple(a + b for a, b in zip(best, split(tiles_ref[at])))

    return list(lax.fori_loop(0, rows, body, tuple(v), unroll=4))


def settle(south, north, costs_ref, tiles_ref, sums_ref, base_ref, q1, q2):
    rows, cols, depth = costs_ref.shape
    count = len(south)

    def both(first, i, v):
        out = []
        for at, part in ((i, v[:count]), (rows - 1 - i, v[count:])):
            best, low = relax(list(part), q1, q2)
            extra = [x - low for x in best]
            if not first:
                extra = [a + b for a, b in zip(extra, split(sums_ref[at]))]
            sums_ref[at] = join(extra)
            out += [a + b for a, b in zip(best, split(tiles_ref[at]))]
        return tuple(out)

    v = lax.fori_loop(0, rows // 2, functools.partial(both, True), tuple(south + north), unroll=2)
    lax.fori_loop(rows // 2, rows, functools.partial(both, False), v, unroll=2)

    ident, mix = identity(cols), interleave(depth)
    batch = 4

    def body(i, carry):
        block = sums_ref[pl.ds(i * batch, batch)].reshape(batch * depth, cols)
        flat = dot(ident, block, TRANSPOSED).astype(jnp.bfloat16)
        for n in range(batch):
            y = i * batch + n
            extra = dot(flat[:, n * depth : (n + 1) * depth], mix, PLAIN)
            base_ref[y] = extra + 4.0 * costs_ref[y].astype(jnp.float32)
        return carry

    lax.fori_loop(0, rows // batch, body, 0, unroll=2)


def lowered(v):
    low = fold_min(v)
    return [x - low for x in v]


def choose(table, here):
    found = jnp.int32(-1)
    for n, value in enumerate(table):
        found = jnp.where(here == n, jnp.int32(value), found)
    return found


def load_arrival(index, arrivals, held_ref):
    @pl.when(index < 0)
    def _():
        held_ref[...] = jnp.zeros(held_ref.shape, held_ref.dtype)

    for n, ref in enumerate(arrivals):

        @pl.when(index == n)
        def _():
            held_ref[...] = ref[...]


def load_verticals(plan, col_here, row_here, arrivals, held_ref):
    for n in range(2):
        hop = row_here - 1 if n == 0 else plan.rows - 2 - row_here
        source = jnp.int32(-1)
        for j in range(plan.rows - 1):
            found = choose([slots[j] for slots in plan.slots], col_here)
            source = jnp.where(hop == j, found, source)
        load_arrival(source, arrivals, held_ref.at[n])


def among(here, columns):
    hit = here == columns[0]
    for c in columns[1:]:
        hit = hit | (here == c)
    return hit


def stage_kernel(plan, s, names, place_ref, small_ref, large_ref, costs_ref, *refs):
    refs = dict(zip(names, refs))
    arrivals = [refs[f"arrival{n}"] for n in range(s)]
    tiles_ref, turned_ref = refs["tiles"], refs["turned"]
    out_ref, held_ref = refs["sent"], refs["held"]
    rows, cols, depth = costs_ref.shape
    col_here, row_here = place_ref[0], place_ref[1]
    q1, q2 = penalties(small_ref, large_ref, cols)

    if s < plan.cols - 1:

        @pl.when((col_here == s) | (col_here == plan.cols - 1 - s))
        def _():
            if s:
                v = split(arrivals[s - 1][...])
            else:
                v = [jnp.zeros((SUB, cols), jnp.float32)] * (depth // SUB)
            west = col_here != s
            v = sweep(v, tiles_ref, refs["sums"], rows, west, 2 * s < plan.cols, q1, q2)
            out_ref[...] = join(lowered(v))

    turning = plan.turning(s)
    if turning:

        @pl.when(among(col_here, turning))
        def _():
            turn_rows(costs_ref, turned_ref)

    if any(s in slots for slots in plan.slots):
        hops = [slots.index(s) if s in slots else -1 for slots in plan.slots]
        source = [slots[j - 1] if j > 0 else -1 for slots, j in zip(plan.slots, hops)]
        hop = choose(hops, col_here)
        north = row_here == plan.rows - 1 - hop

        @pl.when((hop >= 0) & ((row_here == hop) | north))
        def _():
            load_arrival(choose(source, col_here), arrivals, held_ref.at[0])
            v = descend(split(held_ref[0]), turned_ref, north, q1, q2)
            out_ref[...] = join(lowered(v))

    settling = plan.settling(s)
    if settling:

        @pl.when(among(col_here, settling))
        def _():
            load_verticals(plan, col_here, row_here, arrivals, held_ref)
            south, north = split(held_ref[0]), split(held_ref[1])
            settle(south, north, costs_ref, turned_ref, refs["vsums"], refs["base"], q1, q2)


def skew(v, lane, sub):
    count = len(v)
    bit = 1
    while bit < SUB:
        taken = (lane & bit) != 0
        inner = sub < SUB - bit
        up = [pltpu.roll(a, SUB - bit, 0) for a in v]
        v = [
            jnp.where(taken, jnp.where(inner, up[k], up[(k + 1) % count]), v[k])
            for k in range(count)
        ]
        bit *= 2
    while bit < SUB * count:
        taken = (lane & bit) != 0
        v = [jnp.where(taken, v[(k + bit // SUB) % count], v[k]) for k in range(count)]
        bit *= 2
    return v


def unroll_rows(v, sub):
    lanes = v[0].shape[1]
    out = []
    for k, part in enumerate(v):
        if k:
            part = pltpu.roll(part, lanes - k * SUB, 1)
        bit = 1
        while bit < SUB:
            part = jnp.where((sub & bit) != 0, pltpu.roll(part, lanes - bit, 1), part)
            bit *= 2
        out.append(part)
    return out


def final_kernel(plan, names, place_ref, small_ref, large_ref, costs_ref, *refs):
    refs = dict(zip(names, refs))
    arrivals = [refs[f"arrival{n}"] for n in range(plan.stages)]
    rows, cols, depth = costs_ref.shape
    lanes = cols
    held_ref, sums_ref, base_ref, natural_ref = (
        refs["held"], refs["sums"], refs["base"], refs["natural"]
    )
    q1, q2 = penalties(small_ref, large_ref, lanes)
    col_here, row_here = place_ref[0], place_ref[1]

    late = plan.settling(plan.stages)
    if late:

        @pl.when(among(col_here, late))
        def _():
            load_verticals(plan, col_here, row_here, arrivals, held_ref)
            south, north = split(held_ref[0]), split(held_ref[1])
            settle(south, north, costs_ref, refs["turned"], refs["vsums"], base_ref, q1, q2)

    @pl.when((col_here == 0) | (col_here == plan.cols - 1))
    def _():
        v = split(arrivals[plan.cols - 2][...])
        sweep(v, refs["tiles"], sums_ref, rows, col_here == 0, False, q1, q2)

    ident, mix = identity(lanes), interleave(depth)
    batch = 4

    def turn(i, carry):
        block = sums_ref[pl.ds(i * batch, batch)].reshape(batch * depth, lanes)
        flat = dot(ident, block, TRANSPOSED).astype(jnp.bfloat16)
        for n in range(batch):
            at = pl.ds(pl.multiple_of((i * batch + n) * lanes, lanes), lanes)
            natural_ref[at, :] = dot(flat[:, n * depth : (n + 1) * depth], mix, PLAIN)
        return carry

    lax.fori_loop(0, sums_ref.shape[0] // batch, turn, 0, unroll=2)

    lane = lax.broadcasted_iota(jnp.int32, (SUB, lanes), 1)
    sub = lax.broadcasted_iota(jnp.int32, (SUB, lanes), 0)
    half = rows // 2

    def finish(y, carry):
        left, turned = [], []
        for at in (y, y + half):
            across = natural_ref[pl.ds(at, cols, stride=rows), :]
            summed = across + base_ref[at]
            view = (summed * (1.0 / 64.0)).astype(jnp.bfloat16)
            refs["left"][at] = view
            left.append(split(view))
            turned.append(skew(left[-1], lane, sub))
            refs["skewed"][at] = join(turned[-1])
        other = pltpu.roll(jnp.concatenate(turned[1], axis=0), 0, 1, stride=1, stride_axis=0)
        other = [other[i : i + SUB] for i in range(0, cols, SUB)]
        refs["packed"][y] = join(
            [
                jnp.where(lane > sub + k * SUB, a, b)
                for k, (a, b) in enumerate(zip(left[0], other))
            ]
        )
        return carry

    lax.fori_loop(0, half, finish, 0, unroll=2)


def merge_kernel(skewed_ref, packed_ref, right_ref):
    rows, cols, depth = skewed_ref.shape
    lane = lax.broadcasted_iota(jnp.int32, (SUB, depth), 1)
    sub = lax.broadcasted_iota(jnp.int32, (SUB, depth), 0)
    half = rows // 2

    def body(y, carry):
        packed = split(packed_ref[y])
        theirs = [
            skew(packed, lane, sub),
            unroll_rows(packed, sub),
        ]
        for at, other in zip((y, y + half), theirs):
            mine = split(skewed_ref[at])
            right_ref[at] = join(
                [
                    jnp.where(lane + sub + k * SUB < cols, a, b)
                    for k, (a, b) in enumerate(zip(mine, other))
                ]
            )
        return carry

    lax.fori_loop(0, half, body, 0, unroll=2)


class Plan:
    def __init__(self, rows, cols):
        self.rows, self.cols = rows, cols
        self.slots = []
        for c in range(cols):
            busy = {c - 1, c, cols - 2 - c, cols - 1 - c}
            free = [s for s in range(cols + 4 + rows) if s not in busy or s >= cols - 1]
            self.slots.append(free[: rows - 1])
        last = [slots[-1] + 1 for slots in self.slots if slots]
        self.stages = max([cols - 1] + last)

    def route(self, s):
        pairs = []
        if s < self.cols - 1:
            for r in range(self.rows):
                pairs += [
                    ((r, s), (r, s + 1)),
                    ((r, self.cols - 1 - s), (r, self.cols - 2 - s)),
                ]
        for c, slots in enumerate(self.slots):
            if s in slots:
                j = slots.index(s)
                pairs += [
                    ((j, c), (j + 1, c)),
                    ((self.rows - 1 - j, c), (self.rows - 2 - j, c)),
                ]
        number = lambda place: place[0] * self.cols + place[1]
        return [(number(a), number(b)) for a, b in pairs]

    def turning(self, s):
        ends = {0, self.cols - 1}
        return [c for c in range(self.cols) if s == (1 if c in ends else 0)]

    def settling(self, s):
        found = []
        for c, slots in enumerate(self.slots):
            at = slots[-1] + 1
            while at < self.stages and at in (c, self.cols - 1 - c):
                at += 1
            if at == s:
                found.append(c)
        return found


def in_vmem(count):
    return [pl.BlockSpec(memory_space=pltpu.VMEM)] * count


def in_smem(count):
    return [pl.BlockSpec(memory_space=pltpu.SMEM)] * count


def shards(costs, p_small, p_large):
    rows, cols, depth = costs.shape
    plan = Plan(lax.axis_size("row"), lax.axis_size("col"))
    params = {"vmem_limit_bytes": LIMIT}
    place = jnp.stack([lax.axis_index("col"), lax.axis_index("row")]).astype(jnp.int32)
    front = jax.ShapeDtypeStruct((depth, cols), jnp.bfloat16)
    tile = jax.ShapeDtypeStruct((rows, cols, depth), jnp.bfloat16)
    tall = jax.ShapeDtypeStruct((cols * rows // cols, depth, cols), jnp.bfloat16)
    shapes = {
        "sums": tall,
        "turned": jax.ShapeDtypeStruct((rows, depth, cols), jnp.bfloat16),
        "base": jax.ShapeDtypeStruct((rows, cols, depth), jnp.float32),
    }
    held = pltpu.VMEM((2, depth, cols), jnp.bfloat16)
    vsums = pltpu.VMEM((rows, depth, cols), jnp.bfloat16)

    buffers = {
        "tiles": pl.pallas_call(
            prepare_kernel,
            out_shape=tall,
            in_specs=in_vmem(1),
            out_specs=pl.BlockSpec(memory_space=pltpu.VMEM),
            scratch_shapes=[pltpu.VMEM((rows * cols, depth), jnp.float32)],
            compiler_params=pltpu.CompilerParams(**params),
            name="prepare",
        )(costs)
    }

    def run(body, name, results, reads, writes, scratch):
        known = [n for n in writes if n in buffers]
        inputs = reads + known
        outputs = list(results) + writes
        names = [n for n in reads] + [f"{n}_before" for n in known] + outputs + list(scratch)
        lead = 4
        values = pl.pallas_call(
            functools.partial(body, names),
            out_shape=tuple([results[n] for n in results] + [shapes[n] for n in writes]),
            in_specs=in_smem(3) + in_vmem(1 + len(inputs)),
            out_specs=tuple(in_vmem(len(outputs))),
            scratch_shapes=list(scratch.values()),
            input_output_aliases={
                lead + len(reads) + n: outputs.index(name) for n, name in enumerate(known)
            },
            compiler_params=pltpu.CompilerParams(**params),
            name=name,
        )(place, p_small, p_large, costs, *[buffers[n] for n in inputs])
        buffers.update(zip(outputs, values))

    for s in range(plan.stages):
        writes = ["sums"] if s < plan.cols - 1 else []
        writes += ["turned"] if s < 2 else []
        writes += ["base"] if plan.settling(s) else []
        reads = ["tiles"] + ([] if "turned" in writes else ["turned"])
        reads += [f"arrival{n}" for n in range(s)]
        run(
            functools.partial(stage_kernel, plan, s),
            f"stage{s}",
            {"sent": front},
            reads,
            writes,
            {"held": held, "vsums": vsums},
        )
        buffers[f"arrival{s}"] = lax.ppermute(buffers["sent"], ("row", "col"), plan.route(s))

    run(
        functools.partial(final_kernel, plan),
        "final",
        {
            "left": tile,
            "skewed": tile,
            "packed": jax.ShapeDtypeStruct((rows // 2, cols, depth), jnp.bfloat16),
        },
        ["tiles", "turned"] + [f"arrival{n}" for n in range(plan.stages)],
        ["sums", "base"],
        {
            "held": held,
            "vsums": vsums,
            "natural": pltpu.VMEM((cols * rows, depth), jnp.float32),
        },
    )
    arrived = lax.ppermute(buffers["packed"], "col", [(i, i - 1) for i in range(1, plan.cols)])
    right_view = pl.pallas_call(
        merge_kernel,
        out_shape=tile,
        in_specs=in_vmem(2),
        out_specs=pl.BlockSpec(memory_space=pltpu.VMEM),
        compiler_params=pltpu.CompilerParams(**params),
        name="merge",
    )(buffers["skewed"], arrived)
    return buffers["left"], right_view


def solution(mesh):
    placed = (P("row", "col", None), P(), P())
    return jax.shard_map(
        shards,
        mesh=mesh,
        in_specs=placed,
        out_specs=(P("row", "col", None), P("row", "col", None)),
        check_vma=False,
    )
```

time: 90.8 us -> 108 us (1.19)
  starting transfers between devices: 12.7 us -> 21.3 us
  Pallas kernels: 32 us -> 37 us
  waiting for transfers between devices: 41.3 us -> 45.7 us
  other arithmetic: 1.21 us -> 0.08 us
    ppermute x8, starting transfers between devices: 12.7 us -> 21.3 us  [the longest x7 11 us: shards(): lax.ppermute(buffers['sent'], ('row', 'col'), plan.route(s))]
    pallas_call x9 -> x10, Pallas kernels: 32 us -> 37 us  [the longest x8 31.4 us: run(): pl.pallas_call(functools.partial(body, names), out_shape=tuple([results[n...]
    ppermute x8, waiting for transfers between devices: 41.3 us -> 45.7 us  [the longest x7 44.1 us: shards(): lax.ppermute(buffers['sent'], ('row', 'col'), plan.route(s))]
    select_n x1 -> x0, other arithmetic: 1.11 us -> none  [shards(): right_view = jnp.where((x + d < cols)[None], skewed, arrived)]
where the time goes in v3:
time: 108 us; the launch traced here: 107 us
  waiting for transfers between devices  45.7 us (42%)
  Pallas kernels  37 us (34%)
  starting transfers between devices  21.3 us (20%)
  between operations  2.06 us (2%)
  local copies, waits for them, and re-layouts  1.22 us (1%)
    ppermute x7, waiting for transfers between devices, shards(): lax.ppermute(buffers['sent'], ('row', 'col'), plan.route(s))  44.1 us
    pallas_call x8, Pallas kernels, run(): pl.pallas_call(functools.partial(body, names), out_shape=tuple([results[n...  31.4 us
    ppermute x7, starting transfers between devices, shards(): lax.ppermute(buffers['sent'], ('row', 'col'), plan.route(s))  11 us
    ppermute x1, starting transfers between devices, shards(): lax.ppermute(buffers['packed'], 'col', [(i, i - 1) for i in range(1, plan...  10.3 us
    pallas_call x1, Pallas kernels, shards(): pl.pallas_call(merge_kernel, out_shape=tile, in_specs=in_vmem(2), out_spe...  3.55 us
  transfers between devices with their start and end apart: 8, of which 7 were waited for; matrix products, arithmetic and copies ran while one was open for 0% of the time, Pallas kernels for 0%

profile of v3, /device:TPU:1, one launch (start us, length us, event | category | flops | bytes accessed | tf_op | source)
XLA Modules:
  0.0 107.3 jit_solution(8069487175718318502)
XLA Ops:
  1.9 1.2 %copy-done = bf16[32,128,128]{2,1,0:T(8,128)(2,1)S(1)} copy-done((bf16[32,128,128]{2,1,0:T(8,128)(2,1)S(1)}, bf16[32,128,128]{2,1,0:T(8,128)(2,1)}, u32[]{:S(2)}) %copy-start) | copy-done | bytes 1048600
  3.2 2.0 %prepare.1.refs_0_ = bf16[32,128,128]{2,1,0:T(8,128)(2,1)S(1)} custom-call(bf16[32,128,128]{2,1,0:T(8,128)(2,1)S(1)} %copy-done), custom_call_target="tpu_custom_call" | custom-call | tf_op jit(solution)/shard_map/prepare/pallas_call | solution.py:475
  5.2 1.5 %stage0.1 = (bf16[128,128]{1,0:T(8,128)(2,1)S(1)}, bf16[32,128,128]{2,1,0:T(8,128)(2,1)S(1)}, bf16[32,128,128]{2,1,0:T(8,128)(2,1)S(1)}) custom-call(s32[2]{0:T(128)S(1)} %pad_add_fusion.place_ref, s32[1]{0:T(128)S(6)} %copy.27.small_ref, s32[1]{0:T(128)S(6)} %copy.28.large_ref, bf16[32,128,128]{2,1,0:T(8,128)(2,1)S(1)} %copy-done, ...), custom_call_target="tpu_custom_call" | custom-call | tf_op jit(solution)/shard_map/stage0/pallas_call | solution.py:492
  6.7 1.3 %collective-permute-start = (bf16[128,128]{1,0:T(8,128)(2,1)S(1)}, bf16[128,128]{1,0:T(8,128)(2,1)S(1)}, u32[]{:S(2)}, u32[]{:S(2)}) collective-permute-start(bf16[128,128]{1,0:T(8,128)(2,1)S(1)} %get-tuple-element.24), channel_id=1, source_target_pairs={{0,1},{7,6},{8,9},{15,14},{16,17},{23,22},{24,25},{31,30},{2,10},{... | collective-permute-start | bytes 98312 | tf_op jit(solution)/shard_map/ppermute | solution.py:520
  8.0 6.9 %collective-permute-done.refs_1_.refs_2_ = bf16[128,128]{1,0:T(8,128)(2,1)S(1)} collective-permute-done((bf16[128,128]{1,0:T(8,128)(2,1)S(1)}, bf16[128,128]{1,0:T(8,128)(2,1)S(1)}, u32[]{:S(2)}, u32[]{:S(2)}) %collective-permute-start) | collective-permute-done | bytes 32800 | tf_op jit(solution)/shard_map/ppermute | solution.py:520
  14.9 7.6 %stage1.1 = (bf16[128,128]{1,0:T(8,128)(2,1)S(1)}, bf16[32,128,128]{2,1,0:T(8,128)(2,1)S(1)}, bf16[32,128,128]{2,1,0:T(8,128)(2,1)S(1)}) custom-call(s32[2]{0:T(128)S(1)} %pad_add_fusion.place_ref, s32[1]{0:T(128)S(6)} %copy.27.small_ref, s32[1]{0:T(128)S(6)} %copy.28.large_ref, ...), custom_call_target="tpu_custom_call", output_to_operand_aliasing={{1}: (6, {}), {2}: (7, {})} | custom-call | tf_op jit(solution)/shard_map/stage1/pallas_call | solution.py:492
  22.6 1.3 %collective-permute-start.1 = (bf16[128,128]{1,0:T(8,128)(2,1)S(1)}, bf16[128,128]{1,0:T(8,128)(2,1)S(1)}, u32[]{:S(2)}, u32[]{:S(2)}) collective-permute-start(bf16[128,128]{1,0:T(8,128)(2,1)S(1)} %get-tuple-element.28), channel_id=1, source_target_pairs={{1,2},{6,5},{9,10},{14,13},{17,18},{22,21},{25,26},{30,29},{0,8},{... | collective-permute-start | bytes 98312 | tf_op jit(solution)/shard_map/ppermute | solution.py:520
  23.9 1.0 collective-permute-done.1.refs_3_
  24.9 1.3 %stage2.1 = (bf16[128,128]{1,0:T(8,128)(2,1)S(1)}, bf16[32,128,128]{2,1,0:T(8,128)(2,1)S(1)}) custom-call(s32[2]{0:T(128)S(1)} %pad_add_fusion.place_ref, s32[1]{0:T(128)S(6)} %copy.27.small_ref, s32[1]{0:T(128)S(6)} %copy.28.large_ref, bf16[32,128,128]{2,1,0:T(8,128)(2,1)S(1)} %copy-done, ...), custom_call_target="tpu_custom_call", output_to_operand_aliasing={{1}: (8, {})} | custom-call | tf_op jit(solution)/shard_map/stage2/pallas_call | solution.py:492
  26.1 3.9 %collective-permute-start.2 = (bf16[128,128]{1,0:T(8,128)(2,1)S(1)}, bf16[128,128]{1,0:T(8,128)(2,1)S(1)}, u32[]{:S(2)}, u32[]{:S(2)}) collective-permute-start(bf16[128,128]{1,0:T(8,128)(2,1)S(1)} %get-tuple-element.30), channel_id=1, source_target_pairs={{2,3},{5,4},{10,11},{13,12},{18,19},{21,20},{26,27},{29,28},{8,16}... | collective-permute-start | bytes 98312 | tf_op jit(solution)/shard_map/ppermute | solution.py:520
  30.0 1.0 collective-permute-done.2.refs_4_
  31.6 0.7 collective-permute-start.3
  32.8 1.3 %collective-permute-start.4 = (bf16[128,128]{1,0:T(8,128)(2,1)S(1)}, bf16[128,128]{1,0:T(8,128)(2,1)S(1)}, u32[]{:S(2)}, u32[]{:S(2)}) collective-permute-start(bf16[128,128]{1,0:T(8,128)(2,1)S(1)} %get-tuple-element.34), channel_id=1, source_target_pairs={{4,5},{3,2},{12,13},{11,10},{20,21},{19,18},{28,29},{27,26},{17,25... | collective-permute-start | bytes 98312 | tf_op jit(solution)/shard_map/ppermute | solution.py:520
  34.1 9.3 %collective-permute-done.4.refs_6_ = bf16[128,128]{1,0:T(8,128)(2,1)S(1)} collective-permute-done((bf16[128,128]{1,0:T(8,128)(2,1)S(1)}, bf16[128,128]{1,0:T(8,128)(2,1)S(1)}, u32[]{:S(2)}, u32[]{:S(2)}) %collective-permute-start.4) | collective-permute-done | bytes 32800 | tf_op jit(solution)/shard_map/ppermute | solution.py:520
  43.4 4.4 %stage5.1 = (bf16[128,128]{1,0:T(8,128)(2,1)S(1)}, bf16[32,128,128]{2,1,0:T(8,128)(2,1)S(1)}, f32[32,128,128]{2,1,0:T(8,128)S(1)}) custom-call(s32[2]{0:T(128)S(1)} %pad_add_fusion.place_ref, s32[1]{0:T(128)S(6)} %copy.27.small_ref, s32[1]{0:T(128)S(6)} %copy.28.large_ref, ...), custom_call_target="tpu_custom_call", output_to_operand_aliasing={{1}: (11, {}), {2}: (12, {})} | custom-call | tf_op jit(solution)/shard_map/stage5/pallas_call | solution.py:492
  47.8 1.3 %collective-permute-start.5 = (bf16[128,128]{1,0:T(8,128)(2,1)S(1)}, bf16[128,128]{1,0:T(8,128)(2,1)S(1)}, u32[]{:S(2)}, u32[]{:S(2)}) collective-permute-start(bf16[128,128]{1,0:T(8,128)(2,1)S(1)} %get-tuple-element.37), channel_id=1, source_target_pairs={{5,6},{2,1},{13,14},{10,9},{21,22},{18,17},{29,30},{26,25},{19,27}... | collective-permute-start | bytes 98312 | tf_op jit(solution)/shard_map/ppermute | solution.py:520
  49.1 25.1 %collective-permute-done.5.refs_7_ = bf16[128,128]{1,0:T(8,128)(2,1)S(1)} collective-permute-done((bf16[128,128]{1,0:T(8,128)(2,1)S(1)}, bf16[128,128]{1,0:T(8,128)(2,1)S(1)}, u32[]{:S(2)}, u32[]{:S(2)}) %collective-permute-start.5) | collective-permute-done | bytes 32800 | tf_op jit(solution)/shard_map/ppermute | solution.py:520
  74.3 8.7 %stage6.1 = (bf16[128,128]{1,0:T(8,128)(2,1)S(1)}, bf16[32,128,128]{2,1,0:T(8,128)(2,1)S(1)}, f32[32,128,128]{2,1,0:T(8,128)S(1)}) custom-call(s32[2]{0:T(128)S(1)} %pad_add_fusion.place_ref, s32[1]{0:T(128)S(6)} %copy.27.small_ref, s32[1]{0:T(128)S(6)} %copy.28.large_ref, ...), custom_call_target="tpu_custom_call", output_to_operand_aliasing={{1}: (12, {}), {2}: (13, {})} | custom-call | tf_op jit(solution)/shard_map/stage6/pallas_call | solution.py:492
  82.9 1.3 %collective-permute-start.6 = (bf16[128,128]{1,0:T(8,128)(2,1)S(1)}, bf16[128,128]{1,0:T(8,128)(2,1)S(1)}, u32[]{:S(2)}, u32[]{:S(2)}) collective-permute-start(bf16[128,128]{1,0:T(8,128)(2,1)S(1)} %get-tuple-element.40), channel_id=1, source_target_pairs={{6,7},{1,0},{14,15},{9,8},{22,23},{17,16},{30,31},{25,24},{18,26},... | collective-permute-start | bytes 98312 | tf_op jit(solution)/shard_map/ppermute | solution.py:520
  84.2 0.8 collective-permute-done.6.refs_8_
  85.1 6.8 %final.1 = (bf16[32,128,128]{2,1,0:T(8,128)(2,1)}, bf16[32,128,128]{2,1,0:T(8,128)(2,1)S(1)}, bf16[16,128,128]{2,1,0:T(8,128)(2,1)S(1)}, bf16[32,128,128]{2,1,0:T(8,128)(2,1)S(1)}, f32[32,128,128]{2,1,0:T(8,128)S(1)}) custom-call(s32[2]{0:T(128)S(1)} %pad_add_fusion.place_ref, s32[1]{0:T(128)S(6)} %copy.27.small_ref, ...), custom_call_target="tpu_custom_call", output_to_operand_aliasing={{3}: (13, {}), {4}: (14, {})} | custom-call | tf_op jit(solution)/shard_map/final/pallas_call | solution.py:492
  91.9 10.3 %collective-permute-start.7 = (bf16[16,128,128]{2,1,0:T(8,128)(2,1)S(1)}, bf16[16,128,128]{2,1,0:T(8,128)(2,1)S(1)}, u32[]{:S(2)}, u32[]{:S(2)}) collective-permute-start(bf16[16,128,128]{2,1,0:T(8,128)(2,1)S(1)} %get-tuple-element.45), channel_id=1, source_target_pairs={{1,0},{2,1},{3,2},{4,3},{5,4},{6,5},{7,6},{9,8},{10,9},{11,10},{12... | collective-permute-start | bytes 1572872 | tf_op jit(solution)/shard_map/ppermute | solution.py:538
  102.2 1.5 %collective-permute-done.7.packed_ref = bf16[16,128,128]{2,1,0:T(8,128)(2,1)S(1)} collective-permute-done((bf16[16,128,128]{2,1,0:T(8,128)(2,1)S(1)}, bf16[16,128,128]{2,1,0:T(8,128)(2,1)S(1)}, u32[]{:S(2)}, u32[]{:S(2)}) %collective-permute-start.7) | collective-permute-done | bytes 524320 | tf_op jit(solution)/shard_map/ppermute | solution.py:538
  103.7 3.6 %merge.1 = bf16[32,128,128]{2,1,0:T(8,128)(2,1)} custom-call(bf16[32,128,128]{2,1,0:T(8,128)(2,1)S(1)} %get-tuple-element.44.skewed_ref, bf16[16,128,128]{2,1,0:T(8,128)(2,1)S(1)} %collective-permute-done.7.packed_ref), custom_call_target="tpu_custom_call" | custom-call | tf_op jit(solution)/shard_map/merge/pallas_call | solution.py:539
  (5 shorter events, 1.2 us)
Async XLA Ops:
  1.9 1.2 %copy-start = (bf16[32,128,128]{2,1,0:T(8,128)(2,1)S(1)}, bf16[32,128,128]{2,1,0:T(8,128)(2,1)}, u32[]{:S(2)}) copy-start(bf16[32,128,128]{2,1,0:T(8,128)(2,1)} %costs_ref.17) | copy-start | bytes 3145732
  6.7 8.2 %collective-permute-start = (bf16[128,128]{1,0:T(8,128)(2,1)S(1)}, bf16[128,128]{1,0:T(8,128)(2,1)S(1)}, u32[]{:S(2)}, u32[]{:S(2)}) collective-permute-start(bf16[128,128]{1,0:T(8,128)(2,1)S(1)} %get-tuple-element.24), channel_id=1, source_target_pairs={{0,1},{7,6},{8,9},{15,14},{16,17},{23,22},{24,25},{31,30},{2,10},{... | collective-permute-start | bytes 98312 | tf_op jit(solution)/shard_map/ppermute | solution.py:520
  22.6 2.3 %collective-permute-start.1 = (bf16[128,128]{1,0:T(8,128)(2,1)S(1)}, bf16[128,128]{1,0:T(8,128)(2,1)S(1)}, u32[]{:S(2)}, u32[]{:S(2)}) collective-permute-start(bf16[128,128]{1,0:T(8,128)(2,1)S(1)} %get-tuple-element.28), channel_id=1, source_target_pairs={{1,2},{6,5},{9,10},{14,13},{17,18},{22,21},{25,26},{30,29},{0,8},{... | collective-permute-start | bytes 98312 | tf_op jit(solution)/shard_map/ppermute | solution.py:520
  26.1 4.9 %collective-permute-start.2 = (bf16[128,128]{1,0:T(8,128)(2,1)S(1)}, bf16[128,128]{1,0:T(8,128)(2,1)S(1)}, u32[]{:S(2)}, u32[]{:S(2)}) collective-permute-start(bf16[128,128]{1,0:T(8,128)(2,1)S(1)} %get-tuple-element.30), channel_id=1, source_target_pairs={{2,3},{5,4},{10,11},{13,12},{18,19},{21,20},{26,27},{29,28},{8,16}... | collective-permute-start | bytes 98312 | tf_op jit(solution)/shard_map/ppermute | solution.py:520
  31.6 0.7 collective-permute-start.3
  32.8 10.6 %collective-permute-start.4 = (bf16[128,128]{1,0:T(8,128)(2,1)S(1)}, bf16[128,128]{1,0:T(8,128)(2,1)S(1)}, u32[]{:S(2)}, u32[]{:S(2)}) collective-permute-start(bf16[128,128]{1,0:T(8,128)(2,1)S(1)} %get-tuple-element.34), channel_id=1, source_target_pairs={{4,5},{3,2},{12,13},{11,10},{20,21},{19,18},{28,29},{27,26},{17,25... | collective-permute-start | bytes 98312 | tf_op jit(solution)/shard_map/ppermute | solution.py:520
  47.8 26.4 %collective-permute-start.5 = (bf16[128,128]{1,0:T(8,128)(2,1)S(1)}, bf16[128,128]{1,0:T(8,128)(2,1)S(1)}, u32[]{:S(2)}, u32[]{:S(2)}) collective-permute-start(bf16[128,128]{1,0:T(8,128)(2,1)S(1)} %get-tuple-element.37), channel_id=1, source_target_pairs={{5,6},{2,1},{13,14},{10,9},{21,22},{18,17},{29,30},{26,25},{19,27}... | collective-permute-start | bytes 98312 | tf_op jit(solution)/shard_map/ppermute | solution.py:520
  82.9 2.1 %collective-permute-start.6 = (bf16[128,128]{1,0:T(8,128)(2,1)S(1)}, bf16[128,128]{1,0:T(8,128)(2,1)S(1)}, u32[]{:S(2)}, u32[]{:S(2)}) collective-permute-start(bf16[128,128]{1,0:T(8,128)(2,1)S(1)} %get-tuple-element.40), channel_id=1, source_target_pairs={{6,7},{1,0},{14,15},{9,8},{22,23},{17,16},{30,31},{25,24},{18,26},... | collective-permute-start | bytes 98312 | tf_op jit(solution)/shard_map/ppermute | solution.py:520
  91.9 11.8 %collective-permute-start.7 = (bf16[16,128,128]{2,1,0:T(8,128)(2,1)S(1)}, bf16[16,128,128]{2,1,0:T(8,128)(2,1)S(1)}, u32[]{:S(2)}, u32[]{:S(2)}) collective-permute-start(bf16[16,128,128]{2,1,0:T(8,128)(2,1)S(1)} %get-tuple-element.45), channel_id=1, source_target_pairs={{1,0},{2,1},{3,2},{4,3},{5,4},{6,5},{7,6},{9,8},{10,9},{11,10},{12... | collective-permute-start | bytes 1572872 | tf_op jit(solution)/shard_map/ppermute | solution.py:538

commit v4 on v3

--- a/solution.py
+++ b/solution.py
@@ -73,30 +73,37 @@
     return q1, q2
 
 
-def prepare_kernel(costs_ref, out_ref, wide_ref):
+def spread(rows, lanes, first):
+    row = lax.broadcasted_iota(jnp.int32, (rows * SUB, 2 * lanes), 0)
+    col = lax.broadcasted_iota(jnp.int32, (rows * SUB, 2 * lanes), 1)
+    hit = row == (col % lanes % rows) * SUB + first + col // lanes
+    return jnp.where(hit, 1.0, 0.0).astype(jnp.bfloat16)
+
+
+def prepare_kernel(costs_ref, out_ref, mixed_ref):
     rows, cols, depth = costs_ref.shape
-    pack = cols // rows
     mix = interleave(depth)
-    batch = 4
-
-    def widen(y, carry):
-        where = pl.ds(pl.multiple_of(y * cols, cols), cols)
-        wide_ref[where, :] = costs_ref[y].astype(jnp.float32)
+
+    def mixed(i, carry):
+        at = pl.ds(pl.multiple_of(i * 2 * SUB, 2 * SUB), 2 * SUB)
+        wide = costs_ref[:, at, :].astype(jnp.float32)
+        for n in range(2):
+            part = wide[:, n * SUB : (n + 1) * SUB].reshape(rows * SUB, depth)
+            flat = dot(mix, part.astype(jnp.bfloat16), TRANSPOSED)
+            mixed_ref[2 * i + n] = flat.astype(jnp.bfloat16)
         return carry
 
-    lax.fori_loop(0, rows, widen, 0, unroll=4)
-
-    def body(i, carry):
-        parts = [
-            wide_ref[pl.ds(i * batch * pack + n, rows, stride=cols), :].astype(jnp.bfloat16)
-            for n in range(batch * pack)
-        ]
-        flat = dot(mix, jnp.concatenate(parts, axis=0), TRANSPOSED).astype(jnp.bfloat16)
-        for n in range(batch):
-            out_ref[i * batch + n] = flat[:, n * cols : (n + 1) * cols]
-        return carry
-
-    lax.fori_loop(0, cols // pack // batch, body, 0, unroll=2)
+    lax.fori_loop(0, cols // SUB // 2, mixed, 0, unroll=2)
+    for j in range(0, SUB, 2):
+        pick = spread(rows, cols, j)
+
+        def body(i, carry):
+            flat = dot(mixed_ref[i], pick, PLAIN).astype(jnp.bfloat16)
+            out_ref[i * SUB + j] = flat[:, :cols]
+            out_ref[i * SUB + j + 1] = flat[:, cols:]
+            return carry
+
+        lax.fori_loop(0, cols // SUB, body, 0, unroll=4)
 
 
 def turn_rows(costs_ref, tiles_ref):
@@ -115,34 +122,30 @@
 
 
 def sweep(v, tiles_ref, sums_ref, rows, west, first, q1, q2):
-    tiles, depth, lanes = tiles_ref.shape
+    cols, depth, lanes = tiles_ref.shape
     pack = lanes // rows
     lane = lax.broadcasted_iota(jnp.int32, (SUB, lanes), 1)
     groups = [jnp.where(west, pack - 1 - j, j) for j in range(pack)]
-    inward = [lax.rem(lanes - g * rows, lanes) for g in groups]
-    outward = [g * rows for g in groups]
     mine = [(lane >= g * rows) & (lane < (g + 1) * rows) for g in groups]
 
     def body(i, v):
         v = list(v)
-        at = jnp.where(west, tiles - 1 - i, i)
-        tile = split(tiles_ref[at])
-        kept = None if first else split(sums_ref[at])
+        at = jnp.where(west, cols // pack - 1 - i, i)
         found = None
         for j in range(pack):
             best, low = relax(v, q1, q2)
-            extra = [pltpu.roll(x - low, outward[j], 1) for x in best]
-            v = [a + pltpu.roll(c, inward[j], 1) for a, c in zip(best, tile)]
+            extra = [x - low for x in best]
+            v = [a + c for a, c in zip(best, split(tiles_ref[at * pack + groups[j]]))]
             if found is None:
                 found = extra
             else:
                 found = [jnp.where(mine[j], a, b) for a, b in zip(extra, found)]
-        if kept is not None:
-            found = [a + b for a, b in zip(found, kept)]
+        if not first:
+            found = [a + b for a, b in zip(found, split(sums_ref[at]))]
         sums_ref[at] = join(found)
         return tuple(v)
 
-    return list(lax.fori_loop(0, tiles, body, tuple(v)))
+    return list(lax.fori_loop(0, cols // pack, body, tuple(v)))
 
 
 def descend(v, tiles_ref, north, q1, q2):
@@ -243,11 +246,14 @@
 
         @pl.when((col_here == s) | (col_here == plan.cols - 1 - s))
         def _():
+            west = col_here != s
             if s:
                 v = split(arrivals[s - 1][...])
             else:
                 v = [jnp.zeros((SUB, cols), jnp.float32)] * (depth // SUB)
-            west = col_here != s
+            if plan.crossing(s - 1):
+                other = split(refs["crossed"][...])
+                v = [jnp.where(west, b, a) for a, b in zip(v, other)]
             v = sweep(v, tiles_ref, refs["sums"], rows, west, 2 * s < plan.cols, q1, q2)
             out_ref[...] = join(lowered(v))
 
@@ -299,20 +305,6 @@
     return v
 
 
-def unroll_rows(v, sub):
-    lanes = v[0].shape[1]
-    out = []
-    for k, part in enumerate(v):
-        if k:
-            part = pltpu.roll(part, lanes - k * SUB, 1)
-        bit = 1
-        while bit < SUB:
-            part = jnp.where((sub & bit) != 0, pltpu.roll(part, lanes - bit, 1), part)
-            bit *= 2
-        out.append(part)
-    return out
-
-
 def final_kernel(plan, names, place_ref, small_ref, large_ref, costs_ref, *refs):
     refs = dict(zip(names, refs))
     arrivals = [refs[f"arrival{n}"] for n in range(plan.stages)]
@@ -338,41 +330,35 @@
         v = split(arrivals[plan.cols - 2][...])
         sweep(v, refs["tiles"], sums_ref, rows, col_here == 0, False, q1, q2)
 
-    ident, mix = identity(lanes), interleave(depth)
-    batch = 4
+    order, mix = interleave(2 * cols), interleave(depth)
 
     def turn(i, carry):
-        block = sums_ref[pl.ds(i * batch, batch)].reshape(batch * depth, lanes)
-        flat = dot(ident, block, TRANSPOSED).astype(jnp.bfloat16)
-        for n in range(batch):
-            at = pl.ds(pl.multiple_of((i * batch + n) * lanes, lanes), lanes)
-            natural_ref[at, :] = dot(flat[:, n * depth : (n + 1) * depth], mix, PLAIN)
+        pair = jnp.concatenate([sums_ref[2 * i], sums_ref[2 * i + 1]], axis=1)
+        flat = dot(order, pair, TRANSPOSED).astype(jnp.bfloat16)
+        at = pl.ds(pl.multiple_of(i * SUB, SUB), SUB)
+        natural_ref[:, at, :] = dot(flat, mix, PLAIN).reshape(rows, SUB, depth)
         return carry
 
-    lax.fori_loop(0, sums_ref.shape[0] // batch, turn, 0, unroll=2)
+    lax.fori_loop(0, cols // SUB, turn, 0, unroll=4)
 
     lane = lax.broadcasted_iota(jnp.int32, (SUB, lanes), 1)
     sub = lax.broadcasted_iota(jnp.int32, (SUB, lanes), 0)
     half = rows // 2
+    middle = cols // SUB // 2
 
     def finish(y, carry):
-        left, turned = [], []
+        turned = []
         for at in (y, y + half):
-            across = natural_ref[pl.ds(at, cols, stride=rows), :]
-            summed = across + base_ref[at]
+            summed = natural_ref[at] + base_ref[at]
             view = (summed * (1.0 / 64.0)).astype(jnp.bfloat16)
             refs["left"][at] = view
-            left.append(split(view))
-            turned.append(skew(left[-1], lane, sub))
+            turned.append(skew(split(view), lane, sub))
             refs["skewed"][at] = join(turned[-1])
-        other = pltpu.roll(jnp.concatenate(turned[1], axis=0), 0, 1, stride=1, stride_axis=0)
-        other = [other[i : i + SUB] for i in range(0, cols, SUB)]
-        refs["packed"][y] = join(
-            [
-                jnp.where(lane > sub + k * SUB, a, b)
-                for k, (a, b) in enumerate(zip(left[0], other))
-            ]
-        )
+        corner = [
+            jnp.where(lane >= lanes // 2, a, pltpu.roll(b, lanes // 2, 1))
+            for a, b in zip(turned[0][:middle], turned[1][:middle])
+        ]
+        refs["packed"][y] = join(corner + turned[0][middle:] + turned[1][middle:])
         return carry
 
     lax.fori_loop(0, half, finish, 0, unroll=2)
@@ -383,12 +369,14 @@
     lane = lax.broadcasted_iota(jnp.int32, (SUB, depth), 1)
     sub = lax.broadcasted_iota(jnp.int32, (SUB, depth), 0)
     half = rows // 2
+    middle = cols // SUB // 2
 
     def body(y, carry):
         packed = split(packed_ref[y])
+        corner = packed[:middle]
         theirs = [
-            skew(packed, lane, sub),
-            unroll_rows(packed, sub),
+            corner + packed[middle : 2 * middle],
+            [pltpu.roll(x, depth // 2, 1) for x in corner] + packed[2 * middle :],
         ]
         for at, other in zip((y, y + half), theirs):
             mine = split(skewed_ref[at])
@@ -414,14 +402,23 @@
         last = [slots[-1] + 1 for slots in self.slots if slots]
         self.stages = max([cols - 1] + last)
 
+    def crossing(self, s):
+        return 2 * s == self.cols - 2
+
+    def numbers(self, pairs):
+        number = lambda place: place[0] * self.cols + place[1]
+        return [(number(a), number(b)) for a, b in pairs]
+
+    def crossed_route(self, s):
+        return self.numbers([((r, s + 1), (r, s)) for r in range(self.rows)])
+
     def route(self, s):
         pairs = []
         if s < self.cols - 1:
             for r in range(self.rows):
-                pairs += [
-                    ((r, s), (r, s + 1)),
-                    ((r, self.cols - 1 - s), (r, self.cols - 2 - s)),
-                ]
+                pairs.append(((r, s), (r, s + 1)))
+                if not self.crossing(s):
+                    pairs.append(((r, self.cols - 1 - s), (r, self.cols - 2 - s)))
         for c, slots in enumerate(self.slots):
             if s in slots:
                 j = slots.index(s)
@@ -429,8 +426,7 @@
                     ((j, c), (j + 1, c)),
                     ((self.rows - 1 - j, c), (self.rows - 2 - j, c)),
                 ]
-        number = lambda place: place[0] * self.cols + place[1]
-        return [(number(a), number(b)) for a, b in pairs]
+        return self.numbers(pairs)
 
     def turning(self, s):
         ends = {0, self.cols - 1}
@@ -462,9 +458,8 @@
     place = jnp.stack([lax.axis_index("col"), lax.axis_index("row")]).astype(jnp.int32)
     front = jax.ShapeDtypeStruct((depth, cols), jnp.bfloat16)
     tile = jax.ShapeDtypeStruct((rows, cols, depth), jnp.bfloat16)
-    tall = jax.ShapeDtypeStruct((cols * rows // cols, depth, cols), jnp.bfloat16)
     shapes = {
-        "sums": tall,
+        "sums": jax.ShapeDtypeStruct((rows, depth, cols), jnp.bfloat16),
         "turned": jax.ShapeDtypeStruct((rows, depth, cols), jnp.bfloat16),
         "base": jax.ShapeDtypeStruct((rows, cols, depth), jnp.float32),
     }
@@ -474,10 +469,10 @@
     buffers = {
         "tiles": pl.pallas_call(
             prepare_kernel,
-            out_shape=tall,
+            out_shape=jax.ShapeDtypeStruct((cols, depth, cols), jnp.bfloat16),
             in_specs=in_vmem(1),
             out_specs=pl.BlockSpec(memory_space=pltpu.VMEM),
-            scratch_shapes=[pltpu.VMEM((rows * cols, depth), jnp.float32)],
+            scratch_shapes=[pltpu.VMEM((cols // SUB, depth, rows * SUB), jnp.bfloat16)],
             compiler_params=pltpu.CompilerParams(**params),
             name="prepare",
         )(costs)
@@ -509,6 +504,7 @@
         writes += ["base"] if plan.settling(s) else []
         reads = ["tiles"] + ([] if "turned" in writes else ["turned"])
         reads += [f"arrival{n}" for n in range(s)]
+        reads += ["crossed"] if plan.crossing(s - 1) else []
         run(
             functools.partial(stage_kernel, plan, s),
             f"stage{s}",
@@ -518,6 +514,9 @@
             {"held": held, "vsums": vsums},
         )
         buffers[f"arrival{s}"] = lax.ppermute(buffers["sent"], ("row", "col"), plan.route(s))
+        if plan.crossing(s):
+            route = plan.crossed_route(s)
+            buffers["crossed"] = lax.ppermute(buffers["sent"], ("row", "col"), route)
 
     run(
         functools.partial(final_kernel, plan),
@@ -525,14 +524,14 @@
         {
             "left": tile,
             "skewed": tile,
-            "packed": jax.ShapeDtypeStruct((rows // 2, cols, depth), jnp.bfloat16),
+            "packed": jax.ShapeDtypeStruct((rows // 2, cols // 2 * 3, depth), jnp.bfloat16),
         },
         ["tiles", "turned"] + [f"arrival{n}" for n in range(plan.stages)],
         ["sums", "base"],
         {
             "held": held,
             "vsums": vsums,
-            "natural": pltpu.VMEM((cols * rows, depth), jnp.float32),
+            "natural": pltpu.VMEM((rows, cols, depth), jnp.float32),
         },
     )
     arrived = lax.ppermute(buffers["packed"], "col", [(i, i - 1) for i in range(1, plan.cols)])

time: 108 us -> 82 us (0.76)
  waiting for transfers between devices: 45.7 us -> 32.3 us
  Pallas kernels: 37 us -> 28.2 us
  starting transfers between devices: 21.3 us -> 17.8 us
    ppermute x7, waiting for transfers between devices: 44.1 us -> 21.8 us  [shards(): lax.ppermute(buffers['sent'], ('row', 'col'), plan.route(s))]
    pallas_call x8, Pallas kernels: 31.4 us -> 21.6 us  [run(): pl.pallas_call(functools.partial(body, names), out_shape=tuple([results[n...]
    ppermute x1, waiting for transfers between devices: 1.51 us -> 10.5 us  [shards(): lax.ppermute(buffers['packed'], 'col', [(i, i - 1) for i in range(1, plan...]
    ppermute x1, starting transfers between devices: 10.3 us -> 5.55 us  [shards(): lax.ppermute(buffers['packed'], 'col', [(i, i - 1) for i in range(1, plan...]
    pallas_call x1, Pallas kernels: 1.99 us -> 4.81 us  [shards(): pl.pallas_call(prepare_kernel, out_shape=jax.ShapeDtypeStruct((cols, dept...]
    pallas_call x1, Pallas kernels: 3.55 us -> 1.77 us  [shards(): pl.pallas_call(merge_kernel, out_shape=tile, in_specs=in_vmem(2), out_spe...]
  transfers between devices with their start and end apart: 8 -> 9, of which waited for: 7 -> 7; matrix products, arithmetic and copies ran while one was open for 0% -> 0% of each run, Pallas kernels for 0% -> 0%
where the time goes in v4:
time: 82 us; the launch traced here: 81.7 us
  waiting for transfers between devices  32.3 us (39%)
  Pallas kernels  28.2 us (34%)
  starting transfers between devices  17.8 us (22%)
  between operations  2.07 us (3%)
  local copies, waits for them, and re-layouts  1.22 us (1%)
    ppermute x7, waiting for transfers between devices, shards(): lax.ppermute(buffers['sent'], ('row', 'col'), plan.route(s))  21.8 us
    pallas_call x8, Pallas kernels, run(): pl.pallas_call(functools.partial(body, names), out_shape=tuple([results[n...  21.6 us
    ppermute x7, starting transfers between devices, shards(): lax.ppermute(buffers['sent'], ('row', 'col'), plan.route(s))  11.6 us
    ppermute x1, waiting for transfers between devices, shards(): lax.ppermute(buffers['packed'], 'col', [(i, i - 1) for i in range(1, plan...  10.5 us
    ppermute x1, starting transfers between devices, shards(): lax.ppermute(buffers['packed'], 'col', [(i, i - 1) for i in range(1, plan...  5.55 us
    pallas_call x1, Pallas kernels, shards(): pl.pallas_call(prepare_kernel, out_shape=jax.ShapeDtypeStruct((cols, dept...  4.81 us
    pallas_call x1, Pallas kernels, shards(): pl.pallas_call(merge_kernel, out_shape=tile, in_specs=in_vmem(2), out_spe...  1.77 us
  transfers between devices with their start and end apart: 9, of which 7 were waited for; matrix products, arithmetic and copies ran while one was open for 0% of the time, Pallas kernels for 0%

profile of v4, /device:TPU:1, one launch (start us, length us, event | category | flops | bytes accessed | tf_op | source)
XLA Modules:
  0.0 81.7 jit_solution(7379564369028397508)
XLA Ops:
  1.9 1.2 %copy-done = bf16[32,128,128]{2,1,0:T(8,128)(2,1)S(1)} copy-done((bf16[32,128,128]{2,1,0:T(8,128)(2,1)S(1)}, bf16[32,128,128]{2,1,0:T(8,128)(2,1)}, u32[]{:S(2)}) %copy-start) | copy-done | bytes 1048600
  3.2 4.8 %prepare.1.refs_0_ = bf16[128,128,128]{2,1,0:T(8,128)(2,1)S(1)} custom-call(bf16[32,128,128]{2,1,0:T(8,128)(2,1)S(1)} %copy-done), custom_call_target="tpu_custom_call" | custom-call | tf_op jit(solution)/shard_map/prepare/pallas_call | solution.py:470
  8.0 1.5 %stage0.1 = (bf16[128,128]{1,0:T(8,128)(2,1)S(1)}, bf16[32,128,128]{2,1,0:T(8,128)(2,1)S(1)}, bf16[32,128,128]{2,1,0:T(8,128)(2,1)S(1)}) custom-call(s32[2]{0:T(128)S(1)} %pad_add_fusion.place_ref, s32[1]{0:T(128)S(6)} %copy.27.small_ref, s32[1]{0:T(128)S(6)} %copy.28.large_ref, bf16[32,128,128]{2,1,0:T(8,128)(2,1)S(1)} %copy-done, ...), custom_call_target="tpu_custom_call" | custom-call | tf_op jit(solution)/shard_map/stage0/pallas_call | solution.py:487
  9.5 1.3 %collective-permute-start = (bf16[128,128]{1,0:T(8,128)(2,1)S(1)}, bf16[128,128]{1,0:T(8,128)(2,1)S(1)}, u32[]{:S(2)}, u32[]{:S(2)}) collective-permute-start(bf16[128,128]{1,0:T(8,128)(2,1)S(1)} %get-tuple-element.24), channel_id=1, source_target_pairs={{0,1},{7,6},{8,9},{15,14},{16,17},{23,22},{24,25},{31,30},{2,10},{... | collective-permute-start | bytes 98312 | tf_op jit(solution)/shard_map/ppermute | solution.py:516
  10.8 2.8 %collective-permute-done.refs_1_.refs_2_ = bf16[128,128]{1,0:T(8,128)(2,1)S(1)} collective-permute-done((bf16[128,128]{1,0:T(8,128)(2,1)S(1)}, bf16[128,128]{1,0:T(8,128)(2,1)S(1)}, u32[]{:S(2)}, u32[]{:S(2)}) %collective-permute-start) | collective-permute-done | bytes 32800 | tf_op jit(solution)/shard_map/ppermute | solution.py:516
  13.6 3.5 %stage1.1 = (bf16[128,128]{1,0:T(8,128)(2,1)S(1)}, bf16[32,128,128]{2,1,0:T(8,128)(2,1)S(1)}, bf16[32,128,128]{2,1,0:T(8,128)(2,1)S(1)}) custom-call(s32[2]{0:T(128)S(1)} %pad_add_fusion.place_ref, s32[1]{0:T(128)S(6)} %copy.27.small_ref, s32[1]{0:T(128)S(6)} %copy.28.large_ref, ...), custom_call_target="tpu_custom_call", output_to_operand_aliasing={{1}: (6, {}), {2}: (7, {})} | custom-call | tf_op jit(solution)/shard_map/stage1/pallas_call | solution.py:487
  17.2 2.5 %collective-permute-start.1 = (bf16[128,128]{1,0:T(8,128)(2,1)S(1)}, bf16[128,128]{1,0:T(8,128)(2,1)S(1)}, u32[]{:S(2)}, u32[]{:S(2)}) collective-permute-start(bf16[128,128]{1,0:T(8,128)(2,1)S(1)} %get-tuple-element.28), channel_id=1, source_target_pairs={{1,2},{6,5},{9,10},{14,13},{17,18},{22,21},{25,26},{30,29},{0,8},{... | collective-permute-start | bytes 98312 | tf_op jit(solution)/shard_map/ppermute | solution.py:516
  19.7 1.0 %collective-permute-done.1.refs_3_ = bf16[128,128]{1,0:T(8,128)(2,1)S(1)} collective-permute-done((bf16[128,128]{1,0:T(8,128)(2,1)S(1)}, bf16[128,128]{1,0:T(8,128)(2,1)S(1)}, u32[]{:S(2)}, u32[]{:S(2)}) %collective-permute-start.1) | collective-permute-done | bytes 32800 | tf_op jit(solution)/shard_map/ppermute | solution.py:516
  20.7 1.2 %stage2.1 = (bf16[128,128]{1,0:T(8,128)(2,1)S(1)}, bf16[32,128,128]{2,1,0:T(8,128)(2,1)S(1)}) custom-call(s32[2]{0:T(128)S(1)} %pad_add_fusion.place_ref, s32[1]{0:T(128)S(6)} %copy.27.small_ref, s32[1]{0:T(128)S(6)} %copy.28.large_ref, bf16[32,128,128]{2,1,0:T(8,128)(2,1)S(1)} %copy-done, ...), custom_call_target="tpu_custom_call", output_to_operand_aliasing={{1}: (8, {})} | custom-call | tf_op jit(solution)/shard_map/stage2/pallas_call | solution.py:487
  22.0 3.3 %collective-permute-start.2 = (bf16[128,128]{1,0:T(8,128)(2,1)S(1)}, bf16[128,128]{1,0:T(8,128)(2,1)S(1)}, u32[]{:S(2)}, u32[]{:S(2)}) collective-permute-start(bf16[128,128]{1,0:T(8,128)(2,1)S(1)} %get-tuple-element.30), channel_id=1, source_target_pairs={{2,3},{5,4},{10,11},{13,12},{18,19},{21,20},{26,27},{29,28},{8,16}... | collective-permute-start | bytes 98312 | tf_op jit(solution)/shard_map/ppermute | solution.py:516
  25.2 1.0 %collective-permute-done.2.refs_4_ = bf16[128,128]{1,0:T(8,128)(2,1)S(1)} collective-permute-done((bf16[128,128]{1,0:T(8,128)(2,1)S(1)}, bf16[128,128]{1,0:T(8,128)(2,1)S(1)}, u32[]{:S(2)}, u32[]{:S(2)}) %collective-permute-start.2) | collective-permute-done | bytes 32800 | tf_op jit(solution)/shard_map/ppermute | solution.py:516
  26.8 0.7 collective-permute-start.4
  28.7 1.3 %collective-permute-start.5 = (bf16[128,128]{1,0:T(8,128)(2,1)S(1)}, bf16[128,128]{1,0:T(8,128)(2,1)S(1)}, u32[]{:S(2)}, u32[]{:S(2)}) collective-permute-start(bf16[128,128]{1,0:T(8,128)(2,1)S(1)} %get-tuple-element.34), channel_id=1, source_target_pairs={{4,5},{3,2},{12,13},{11,10},{20,21},{19,18},{28,29},{27,26},{17,25... | collective-permute-start | bytes 98312 | tf_op jit(solution)/shard_map/ppermute | solution.py:516
  30.0 9.3 %collective-permute-done.5.refs_6_ = bf16[128,128]{1,0:T(8,128)(2,1)S(1)} collective-permute-done((bf16[128,128]{1,0:T(8,128)(2,1)S(1)}, bf16[128,128]{1,0:T(8,128)(2,1)S(1)}, u32[]{:S(2)}, u32[]{:S(2)}) %collective-permute-start.5) | collective-permute-done | bytes 32800 | tf_op jit(solution)/shard_map/ppermute | solution.py:516
  39.3 4.4 %stage5.1 = (bf16[128,128]{1,0:T(8,128)(2,1)S(1)}, bf16[32,128,128]{2,1,0:T(8,128)(2,1)S(1)}, f32[32,128,128]{2,1,0:T(8,128)S(1)}) custom-call(s32[2]{0:T(128)S(1)} %pad_add_fusion.place_ref, s32[1]{0:T(128)S(6)} %copy.27.small_ref, s32[1]{0:T(128)S(6)} %copy.28.large_ref, ...), custom_call_target="tpu_custom_call", output_to_operand_aliasing={{1}: (11, {}), {2}: (12, {})} | custom-call | tf_op jit(solution)/shard_map/stage5/pallas_call | solution.py:487
  43.7 1.3 %collective-permute-start.6 = (bf16[128,128]{1,0:T(8,128)(2,1)S(1)}, bf16[128,128]{1,0:T(8,128)(2,1)S(1)}, u32[]{:S(2)}, u32[]{:S(2)}) collective-permute-start(bf16[128,128]{1,0:T(8,128)(2,1)S(1)} %get-tuple-element.37), channel_id=1, source_target_pairs={{5,6},{2,1},{13,14},{10,9},{21,22},{18,17},{29,30},{26,25},{19,27}... | collective-permute-start | bytes 98312 | tf_op jit(solution)/shard_map/ppermute | solution.py:516
  45.0 6.9 %collective-permute-done.6.refs_7_ = bf16[128,128]{1,0:T(8,128)(2,1)S(1)} collective-permute-done((bf16[128,128]{1,0:T(8,128)(2,1)S(1)}, bf16[128,128]{1,0:T(8,128)(2,1)S(1)}, u32[]{:S(2)}, u32[]{:S(2)}) %collective-permute-start.6) | collective-permute-done | bytes 32800 | tf_op jit(solution)/shard_map/ppermute | solution.py:516
  51.9 3.9 %stage6.1 = (bf16[128,128]{1,0:T(8,128)(2,1)S(1)}, bf16[32,128,128]{2,1,0:T(8,128)(2,1)S(1)}, f32[32,128,128]{2,1,0:T(8,128)S(1)}) custom-call(s32[2]{0:T(128)S(1)} %pad_add_fusion.place_ref, s32[1]{0:T(128)S(6)} %copy.27.small_ref, s32[1]{0:T(128)S(6)} %copy.28.large_ref, ...), custom_call_target="tpu_custom_call", output_to_operand_aliasing={{1}: (12, {}), {2}: (13, {})} | custom-call | tf_op jit(solution)/shard_map/stage6/pallas_call | solution.py:487
  55.8 1.3 %collective-permute-start.7 = (bf16[128,128]{1,0:T(8,128)(2,1)S(1)}, bf16[128,128]{1,0:T(8,128)(2,1)S(1)}, u32[]{:S(2)}, u32[]{:S(2)}) collective-permute-start(bf16[128,128]{1,0:T(8,128)(2,1)S(1)} %get-tuple-element.40), channel_id=1, source_target_pairs={{6,7},{1,0},{14,15},{9,8},{22,23},{17,16},{30,31},{25,24},{18,26},... | collective-permute-start | bytes 98312 | tf_op jit(solution)/shard_map/ppermute | solution.py:516
  57.1 0.8 %collective-permute-done.7.refs_8_ = bf16[128,128]{1,0:T(8,128)(2,1)S(1)} collective-permute-done((bf16[128,128]{1,0:T(8,128)(2,1)S(1)}, bf16[128,128]{1,0:T(8,128)(2,1)S(1)}, u32[]{:S(2)}, u32[]{:S(2)}) %collective-permute-start.7) | collective-permute-done | bytes 32800 | tf_op jit(solution)/shard_map/ppermute | solution.py:516
  57.9 5.9 %final.1 = (bf16[32,128,128]{2,1,0:T(8,128)(2,1)}, bf16[32,128,128]{2,1,0:T(8,128)(2,1)S(1)}, bf16[16,192,128]{2,1,0:T(8,128)(2,1)S(1)}, bf16[32,128,128]{2,1,0:T(8,128)(2,1)S(1)}, f32[32,128,128]{2,1,0:T(8,128)S(1)}) custom-call(s32[2]{0:T(128)S(1)} %pad_add_fusion.place_ref, s32[1]{0:T(128)S(6)} %copy.27.small_ref, ...), custom_call_target="tpu_custom_call", output_to_operand_aliasing={{3}: (13, {}), {4}: (14, {})} | custom-call | tf_op jit(solution)/shard_map/final/pallas_call | solution.py:487
  63.8 5.6 %collective-permute-start.8 = (bf16[16,192,128]{2,1,0:T(8,128)(2,1)S(1)}, bf16[16,192,128]{2,1,0:T(8,128)(2,1)S(1)}, u32[]{:S(2)}, u32[]{:S(2)}) collective-permute-start(bf16[16,192,128]{2,1,0:T(8,128)(2,1)S(1)} %get-tuple-element.45), channel_id=1, source_target_pairs={{1,0},{2,1},{3,2},{4,3},{5,4},{6,5},{7,6},{9,8},{10,9},{11,10},{12... | collective-permute-start | bytes 2359304 | tf_op jit(solution)/shard_map/ppermute | solution.py:537
  69.4 10.5 %collective-permute-done.8.packed_ref = bf16[16,192,128]{2,1,0:T(8,128)(2,1)S(1)} collective-permute-done((bf16[16,192,128]{2,1,0:T(8,128)(2,1)S(1)}, bf16[16,192,128]{2,1,0:T(8,128)(2,1)S(1)}, u32[]{:S(2)}, u32[]{:S(2)}) %collective-permute-start.8) | collective-permute-done | bytes 786464 | tf_op jit(solution)/shard_map/ppermute | solution.py:537
  80.0 1.8 %merge.1 = bf16[32,128,128]{2,1,0:T(8,128)(2,1)} custom-call(bf16[32,128,128]{2,1,0:T(8,128)(2,1)S(1)} %get-tuple-element.44.skewed_ref, bf16[16,192,128]{2,1,0:T(8,128)(2,1)S(1)} %collective-permute-done.8.packed_ref), custom_call_target="tpu_custom_call" | custom-call | tf_op jit(solution)/shard_map/merge/pallas_call | solution.py:538
  (7 shorter events, 1.9 us)
Async XLA Ops:
  1.9 1.2 %copy-start = (bf16[32,128,128]{2,1,0:T(8,128)(2,1)S(1)}, bf16[32,128,128]{2,1,0:T(8,128)(2,1)}, u32[]{:S(2)}) copy-start(bf16[32,128,128]{2,1,0:T(8,128)(2,1)} %costs_ref.17) | copy-start | bytes 3145732
  9.5 4.1 %collective-permute-start = (bf16[128,128]{1,0:T(8,128)(2,1)S(1)}, bf16[128,128]{1,0:T(8,128)(2,1)S(1)}, u32[]{:S(2)}, u32[]{:S(2)}) collective-permute-start(bf16[128,128]{1,0:T(8,128)(2,1)S(1)} %get-tuple-element.24), channel_id=1, source_target_pairs={{0,1},{7,6},{8,9},{15,14},{16,17},{23,22},{24,25},{31,30},{2,10},{... | collective-permute-start | bytes 98312 | tf_op jit(solution)/shard_map/ppermute | solution.py:516
  17.2 3.5 %collective-permute-start.1 = (bf16[128,128]{1,0:T(8,128)(2,1)S(1)}, bf16[128,128]{1,0:T(8,128)(2,1)S(1)}, u32[]{:S(2)}, u32[]{:S(2)}) collective-permute-start(bf16[128,128]{1,0:T(8,128)(2,1)S(1)} %get-tuple-element.28), channel_id=1, source_target_pairs={{1,2},{6,5},{9,10},{14,13},{17,18},{22,21},{25,26},{30,29},{0,8},{... | collective-permute-start | bytes 98312 | tf_op jit(solution)/shard_map/ppermute | solution.py:516
  22.0 4.3 %collective-permute-start.2 = (bf16[128,128]{1,0:T(8,128)(2,1)S(1)}, bf16[128,128]{1,0:T(8,128)(2,1)S(1)}, u32[]{:S(2)}, u32[]{:S(2)}) collective-permute-start(bf16[128,128]{1,0:T(8,128)(2,1)S(1)} %get-tuple-element.30), channel_id=1, source_target_pairs={{2,3},{5,4},{10,11},{13,12},{18,19},{21,20},{26,27},{29,28},{8,16}... | collective-permute-start | bytes 98312 | tf_op jit(solution)/shard_map/ppermute | solution.py:516
  26.8 1.3 %collective-permute-start.4 = (bf16[128,128]{1,0:T(8,128)(2,1)S(1)}, bf16[128,128]{1,0:T(8,128)(2,1)S(1)}, u32[]{:S(2)}, u32[]{:S(2)}) collective-permute-start(bf16[128,128]{1,0:T(8,128)(2,1)S(1)} %get-tuple-element.32), channel_id=1, source_target_pairs={{4,3},{12,11},{20,19},{28,27}} | collective-permute-start | bytes 98312 | tf_op jit(solution)/shard_map/ppermute | solution.py:519
  27.5 0.7 collective-permute-start.3
  28.7 10.6 %collective-permute-start.5 = (bf16[128,128]{1,0:T(8,128)(2,1)S(1)}, bf16[128,128]{1,0:T(8,128)(2,1)S(1)}, u32[]{:S(2)}, u32[]{:S(2)}) collective-permute-start(bf16[128,128]{1,0:T(8,128)(2,1)S(1)} %get-tuple-element.34), channel_id=1, source_target_pairs={{4,5},{3,2},{12,13},{11,10},{20,21},{19,18},{28,29},{27,26},{17,25... | collective-permute-start | bytes 98312 | tf_op jit(solution)/shard_map/ppermute | solution.py:516
  43.7 8.2 %collective-permute-start.6 = (bf16[128,128]{1,0:T(8,128)(2,1)S(1)}, bf16[128,128]{1,0:T(8,128)(2,1)S(1)}, u32[]{:S(2)}, u32[]{:S(2)}) collective-permute-start(bf16[128,128]{1,0:T(8,128)(2,1)S(1)} %get-tuple-element.37), channel_id=1, source_target_pairs={{5,6},{2,1},{13,14},{10,9},{21,22},{18,17},{29,30},{26,25},{19,27}... | collective-permute-start | bytes 98312 | tf_op jit(solution)/shard_map/ppermute | solution.py:516
  55.8 2.1 %collective-permute-start.7 = (bf16[128,128]{1,0:T(8,128)(2,1)S(1)}, bf16[128,128]{1,0:T(8,128)(2,1)S(1)}, u32[]{:S(2)}, u32[]{:S(2)}) collective-permute-start(bf16[128,128]{1,0:T(8,128)(2,1)S(1)} %get-tuple-element.40), channel_id=1, source_target_pairs={{6,7},{1,0},{14,15},{9,8},{22,23},{17,16},{30,31},{25,24},{18,26},... | collective-permute-start | bytes 98312 | tf_op jit(solution)/shard_map/ppermute | solution.py:516
  63.8 16.1 %collective-permute-start.8 = (bf16[16,192,128]{2,1,0:T(8,128)(2,1)S(1)}, bf16[16,192,128]{2,1,0:T(8,128)(2,1)S(1)}, u32[]{:S(2)}, u32[]{:S(2)}) collective-permute-start(bf16[16,192,128]{2,1,0:T(8,128)(2,1)S(1)} %get-tuple-element.45), channel_id=1, source_target_pairs={{1,0},{2,1},{3,2},{4,3},{5,4},{6,5},{7,6},{9,8},{10,9},{11,10},{12... | collective-permute-start | bytes 2359304 | tf_op jit(solution)/shard_map/ppermute | solution.py:537

commit v5 on v4

--- a/solution.py
+++ b/solution.py
@@ -11,7 +11,7 @@
 BIG = 1e30
 TRANSPOSED = (((1,), (1,)), ((), ()))
 PLAIN = (((1,), (0,)), ((), ()))
-LIMIT = 40 * 1024 * 1024
+LIMIT = 20 * 1024 * 1024
 
 
 def one_hot(rule, size):
@@ -66,11 +66,8 @@
     return best, low
 
 
-def penalties(small_ref, large_ref, lanes):
-    shape = (SUB, lanes)
-    q1 = jnp.full(shape, small_ref[0], jnp.int32).astype(jnp.float32)
-    q2 = jnp.full(shape, large_ref[0], jnp.int32).astype(jnp.float32)
-    return q1, q2
+def penalties(prices_ref):
+    return prices_ref[0], prices_ref[1]
 
 
 def spread(rows, lanes, first):
@@ -80,13 +77,25 @@
     return jnp.where(hit, 1.0, 0.0).astype(jnp.bfloat16)
 
 
-def prepare_kernel(costs_ref, out_ref, mixed_ref):
+def prepare_kernel(
+    costs_ref, small_ref, large_ref,
+    out_ref, low_ref, prices_ref, near_ref,
+    mixed_ref, price_refs, arrived,
+):
     rows, cols, depth = costs_ref.shape
     mix = interleave(depth)
+    fetches = [
+        pltpu.make_async_copy(ref, price_refs.at[n], arrived.at[n])
+        for n, ref in enumerate((small_ref, large_ref))
+    ]
+    for fetch in fetches:
+        fetch.start()
 
     def mixed(i, carry):
         at = pl.ds(pl.multiple_of(i * 2 * SUB, 2 * SUB), 2 * SUB)
-        wide = costs_ref[:, at, :].astype(jnp.float32)
+        block = costs_ref[:, at, :]
+        near_ref[:, at, :] = block
+        wide = block.astype(jnp.float32)
         for n in range(2):
             part = wide[:, n * SUB : (n + 1) * SUB].reshape(rows * SUB, depth)
             flat = dot(mix, part.astype(jnp.bfloat16), TRANSPOSED)
@@ -98,12 +107,19 @@
         pick = spread(rows, cols, j)
 
         def body(i, carry):
-            flat = dot(mixed_ref[i], pick, PLAIN).astype(jnp.bfloat16)
-            out_ref[i * SUB + j] = flat[:, :cols]
-            out_ref[i * SUB + j + 1] = flat[:, cols:]
+            flat = dot(mixed_ref[i], pick, PLAIN)
+            for n in range(2):
+                part = flat[:, n * cols : (n + 1) * cols]
+                out_ref[i * SUB + j + n] = part
+                low_ref[i * SUB + j + n] = fold_min(split(part))
             return carry
 
         lax.fori_loop(0, cols // SUB, body, 0, unroll=4)
+
+    for n, fetch in enumerate(fetches):
+        fetch.wait()
+        price = jnp.full(prices_ref.shape[1:], price_refs[n, 0], jnp.int32)
+        prices_ref[n] = price.astype(jnp.float32)
 
 
 def turn_rows(costs_ref, tiles_ref):
@@ -121,21 +137,31 @@
     lax.fori_loop(0, rows // batch, body, 0, unroll=2)
 
 
-def sweep(v, tiles_ref, sums_ref, rows, west, first, q1, q2):
+def sweep(v, tiles_ref, lows_ref, sums_ref, rows, west, first, q1, q2):
     cols, depth, lanes = tiles_ref.shape
     pack = lanes // rows
     lane = lax.broadcasted_iota(jnp.int32, (SUB, lanes), 1)
+    sub = lax.broadcasted_iota(jnp.int32, (SUB, lanes), 0)
     groups = [jnp.where(west, pack - 1 - j, j) for j in range(pack)]
     mine = [(lane >= g * rows) & (lane < (g + 1) * rows) for g in groups]
 
-    def body(i, v):
-        v = list(v)
+    def body(i, carry):
+        v, jump = list(carry[:-1]), carry[-1]
         at = jnp.where(west, cols // pack - 1 - i, i)
         found = None
         for j in range(pack):
-            best, low = relax(v, q1, q2)
-            extra = [x - low for x in best]
-            v = [a + c for a, c in zip(best, split(tiles_ref[at * pack + groups[j]]))]
+            x = at * pack + groups[j]
+            c = split(tiles_ref[x])
+            below = [jnp.where(sub == 0, BIG, pltpu.roll(v[-1], 1, 0))] + v[:-1]
+            above = v[1:] + [jnp.where(sub == SUB - 1, BIG, pltpu.roll(v[0], SUB - 1, 0))]
+            near = [
+                jnp.minimum(n, jnp.minimum(a, b) + q1) + k
+                for n, a, b, k in zip(v, below, above, c)
+            ]
+            far = [k + jump for k in c]
+            v = [jnp.minimum(a, b) for a, b in zip(near, far)]
+            jump = jnp.minimum(fold_min(near), lows_ref[x] + jump) + q2
+            extra = [a - b for a, b in zip(v, far)]
             if found is None:
                 found = extra
             else:
@@ -143,9 +169,11 @@
         if not first:
             found = [a + b for a, b in zip(found, split(sums_ref[at]))]
         sums_ref[at] = join(found)
-        return tuple(v)
-
-    return list(lax.fori_loop(0, cols // pack, body, tuple(v)))
+        return tuple(v) + (jump,)
+
+    last = lax.fori_loop(0, cols // pack, body, tuple(v) + (fold_min(v) + q2,))
+    low = last[-1] - q2
+    return [x - low for x in last[:-1]]
 
 
 def descend(v, tiles_ref, north, q1, q2):
@@ -186,7 +214,7 @@
         for n in range(batch):
             y = i * batch + n
             extra = dot(flat[:, n * depth : (n + 1) * depth], mix, PLAIN)
-            base_ref[y] = extra + 4.0 * costs_ref[y].astype(jnp.float32)
+            base_ref[y] = extra + 4.0 * costs_ref[y].astype(jnp.float32) + 2.0 * q2[:1]
         return carry
 
     lax.fori_loop(0, rows // batch, body, 0, unroll=2)
@@ -233,14 +261,14 @@
     return hit
 
 
-def stage_kernel(plan, s, names, place_ref, small_ref, large_ref, costs_ref, *refs):
+def stage_kernel(plan, s, names, prices_ref, costs_ref, *refs):
     refs = dict(zip(names, refs))
     arrivals = [refs[f"arrival{n}"] for n in range(s)]
     tiles_ref, turned_ref = refs["tiles"], refs["turned"]
     out_ref, held_ref = refs["sent"], refs["held"]
     rows, cols, depth = costs_ref.shape
-    col_here, row_here = place_ref[0], place_ref[1]
-    q1, q2 = penalties(small_ref, large_ref, cols)
+    col_here, row_here = lax.axis_index("col"), lax.axis_index("row")
+    q1, q2 = penalties(prices_ref)
 
     if s < plan.cols - 1:
 
@@ -254,8 +282,9 @@
             if plan.crossing(s - 1):
                 other = split(refs["crossed"][...])
                 v = [jnp.where(west, b, a) for a, b in zip(v, other)]
-            v = sweep(v, tiles_ref, refs["sums"], rows, west, 2 * s < plan.cols, q1, q2)
-            out_ref[...] = join(lowered(v))
+            first = 2 * s < plan.cols
+            v = sweep(v, tiles_ref, refs["lows"], refs["sums"], rows, west, first, q1, q2)
+            out_ref[...] = join(v)
 
     turning = plan.turning(s)
     if turning:
@@ -305,7 +334,7 @@
     return v
 
 
-def final_kernel(plan, names, place_ref, small_ref, large_ref, costs_ref, *refs):
+def final_kernel(plan, names, prices_ref, costs_ref, *refs):
     refs = dict(zip(names, refs))
     arrivals = [refs[f"arrival{n}"] for n in range(plan.stages)]
     rows, cols, depth = costs_ref.shape
@@ -313,8 +342,8 @@
     held_ref, sums_ref, base_ref, natural_ref = (
         refs["held"], refs["sums"], refs["base"], refs["natural"]
     )
-    q1, q2 = penalties(small_ref, large_ref, lanes)
-    col_here, row_here = place_ref[0], place_ref[1]
+    q1, q2 = penalties(prices_ref)
+    col_here, row_here = lax.axis_index("col"), lax.axis_index("row")
 
     late = plan.settling(plan.stages)
     if late:
@@ -328,7 +357,7 @@
     @pl.when((col_here == 0) | (col_here == plan.cols - 1))
     def _():
         v = split(arrivals[plan.cols - 2][...])
-        sweep(v, refs["tiles"], sums_ref, rows, col_here == 0, False, q1, q2)
+        sweep(v, refs["tiles"], refs["lows"], sums_ref, rows, col_here == 0, False, q1, q2)
 
     order, mix = interleave(2 * cols), interleave(depth)
 
@@ -447,15 +476,10 @@
     return [pl.BlockSpec(memory_space=pltpu.VMEM)] * count
 
 
-def in_smem(count):
-    return [pl.BlockSpec(memory_space=pltpu.SMEM)] * count
-
-
 def shards(costs, p_small, p_large):
     rows, cols, depth = costs.shape
     plan = Plan(lax.axis_size("row"), lax.axis_size("col"))
     params = {"vmem_limit_bytes": LIMIT}
-    place = jnp.stack([lax.axis_index("col"), lax.axis_index("row")]).astype(jnp.int32)
     front = jax.ShapeDtypeStruct((depth, cols), jnp.bfloat16)
     tile = jax.ShapeDtypeStruct((rows, cols, depth), jnp.bfloat16)
     shapes = {
@@ -466,28 +490,36 @@
     held = pltpu.VMEM((2, depth, cols), jnp.bfloat16)
     vsums = pltpu.VMEM((rows, depth, cols), jnp.bfloat16)
 
-    buffers = {
-        "tiles": pl.pallas_call(
-            prepare_kernel,
-            out_shape=jax.ShapeDtypeStruct((cols, depth, cols), jnp.bfloat16),
-            in_specs=in_vmem(1),
-            out_specs=pl.BlockSpec(memory_space=pltpu.VMEM),
-            scratch_shapes=[pltpu.VMEM((cols // SUB, depth, rows * SUB), jnp.bfloat16)],
-            compiler_params=pltpu.CompilerParams(**params),
-            name="prepare",
-        )(costs)
-    }
+    tiles, lows, prices, near = pl.pallas_call(
+        prepare_kernel,
+        out_shape=(
+            jax.ShapeDtypeStruct((cols, depth, cols), jnp.float32),
+            jax.ShapeDtypeStruct((cols, SUB, cols), jnp.float32),
+            jax.ShapeDtypeStruct((2, SUB, cols), jnp.float32),
+            tile,
+        ),
+        in_specs=in_vmem(1) + [pl.BlockSpec(memory_space=pltpu.HBM)] * 2,
+        out_specs=tuple(in_vmem(4)),
+        scratch_shapes=[
+            pltpu.VMEM((cols // SUB, depth, rows * SUB), jnp.bfloat16),
+            pltpu.SMEM((2, 1), jnp.int32),
+            pltpu.SemaphoreType.DMA((2,)),
+        ],
+        compiler_params=pltpu.CompilerParams(**params),
+        name="prepare",
+    )(costs, p_small, p_large)
+    buffers = {"tiles": tiles, "lows": lows}
 
     def run(body, name, results, reads, writes, scratch):
         known = [n for n in writes if n in buffers]
         inputs = reads + known
         outputs = list(results) + writes
         names = [n for n in reads] + [f"{n}_before" for n in known] + outputs + list(scratch)
-        lead = 4
+        lead = 2
         values = pl.pallas_call(
             functools.partial(body, names),
             out_shape=tuple([results[n] for n in results] + [shapes[n] for n in writes]),
-            in_specs=in_smem(3) + in_vmem(1 + len(inputs)),
+            in_specs=in_vmem(lead + len(inputs)),
             out_specs=tuple(in_vmem(len(outputs))),
             scratch_shapes=list(scratch.values()),
             input_output_aliases={
@@ -495,14 +527,14 @@
             },
             compiler_params=pltpu.CompilerParams(**params),
             name=name,
-        )(place, p_small, p_large, costs, *[buffers[n] for n in inputs])
+        )(prices, near, *[buffers[n] for n in inputs])
         buffers.update(zip(outputs, values))
 
     for s in range(plan.stages):
         writes = ["sums"] if s < plan.cols - 1 else []
         writes += ["turned"] if s < 2 else []
         writes += ["base"] if plan.settling(s) else []
-        reads = ["tiles"] + ([] if "turned" in writes else ["turned"])
+        reads = ["tiles", "lows"] + ([] if "turned" in writes else ["turned"])
         reads += [f"arrival{n}" for n in range(s)]
         reads += ["crossed"] if plan.crossing(s - 1) else []
         run(
@@ -526,7 +558,7 @@
             "skewed": tile,
             "packed": jax.ShapeDtypeStruct((rows // 2, cols // 2 * 3, depth), jnp.bfloat16),
         },
-        ["tiles", "turned"] + [f"arrival{n}" for n in range(plan.stages)],
+        ["tiles", "lows", "turned"] + [f"arrival{n}" for n in range(plan.stages)],
         ["sums", "base"],
         {
             "held": held,

time: 82 us -> 78.1 us (0.952)
  Pallas kernels: 28.2 us -> 24.2 us
    pallas_call x8, Pallas kernels: 21.6 us -> 17.2 us  [run(): pl.pallas_call(functools.partial(body, names), out_shape=tuple([results[n...]
    ppermute x7, waiting for transfers between devices: 21.8 us -> 22.8 us  [shards(): lax.ppermute(buffers['sent'], ('row', 'col'), plan.route(s))]
where the time goes in v5:
time: 78.1 us; the launch traced here: 77.8 us
  waiting for transfers between devices  33.1 us (42%)
  Pallas kernels  24.2 us (31%)
  starting transfers between devices  17.2 us (22%)
  between operations  2.06 us (3%)
  local copies, waits for them, and re-layouts  1.22 us (2%)
    ppermute x7, waiting for transfers between devices, shards(): lax.ppermute(buffers['sent'], ('row', 'col'), plan.route(s))  22.8 us
    pallas_call x8, Pallas kernels, run(): pl.pallas_call(functools.partial(body, names), out_shape=tuple([results[n...  17.2 us
    ppermute x7, starting transfers between devices, shards(): lax.ppermute(buffers['sent'], ('row', 'col'), plan.route(s))  11.1 us
    ppermute x1, waiting for transfers between devices, shards(): lax.ppermute(buffers['packed'], 'col', [(i, i - 1) for i in range(1, plan...  10.3 us
    ppermute x1, starting transfers between devices, shards(): lax.ppermute(buffers['packed'], 'col', [(i, i - 1) for i in range(1, plan...  5.45 us
    pallas_call x1, Pallas kernels, shards(): pl.pallas_call(prepare_kernel, out_shape=(jax.ShapeDtypeStruct((cols, dep...  5.16 us
    pallas_call x1, Pallas kernels, shards(): pl.pallas_call(merge_kernel, out_shape=tile, in_specs=in_vmem(2), out_spe...  1.78 us
  transfers between devices with their start and end apart: 9, of which 7 were waited for; matrix products, arithmetic and copies ran while one was open for 0% of the time, Pallas kernels for 0%

profile of v5, /device:TPU:1, one launch (start us, length us, event | category | flops | bytes accessed | tf_op | source)
XLA Modules:
  0.0 77.8 jit_solution(1832707566158221044)
XLA Ops:
  1.9 1.2 %copy-done = bf16[32,128,128]{2,1,0:T(8,128)(2,1)S(1)} copy-done((bf16[32,128,128]{2,1,0:T(8,128)(2,1)S(1)}, bf16[32,128,128]{2,1,0:T(8,128)(2,1)}, u32[]{:S(2)}) %copy-start) | copy-done | bytes 1048600
  3.1 5.2 %prepare.1 = (f32[128,128,128]{2,1,0:T(8,128)S(1)}, f32[128,8,128]{2,1,0:T(8,128)S(1)}, f32[2,8,128]{2,1,0:T(8,128)S(1)}, bf16[32,128,128]{2,1,0:T(8,128)(2,1)S(1)}) custom-call(bf16[32,128,128]{2,1,0:T(8,128)(2,1)S(1)} %copy-done, s32[1]{0:T(128)S(6)} %copy.27.small_ref, s32[1]{0:T(128)S(6)} %copy.28.large_ref), custom_call_target="tpu_custom_call" | custom-call | tf_op jit(solution)/shard_map/prepare/pallas_call | solution.py:493
  8.3 1.0 %stage0.1 = (bf16[128,128]{1,0:T(8,128)(2,1)S(1)}, bf16[32,128,128]{2,1,0:T(8,128)(2,1)S(1)}, bf16[32,128,128]{2,1,0:T(8,128)(2,1)S(1)}) custom-call(f32[2,8,128]{2,1,0:T(8,128)S(1)} %get-tuple-element.28.prices_ref, bf16[32,128,128]{2,1,0:T(8,128)(2,1)S(1)} %get-tuple-element.29.costs_ref, f32[128,128,128]{2,1,0:T(8,128)S(1)} %get-tuple-element.30.refs_0_, ...), custom_call_target="tpu_custom_call" | custom-call | tf_op jit(solution)/shard_map/stage0/pallas_call | solution.py:519
  9.3 1.3 %collective-permute-start = (bf16[128,128]{1,0:T(8,128)(2,1)S(1)}, bf16[128,128]{1,0:T(8,128)(2,1)S(1)}, u32[]{:S(2)}, u32[]{:S(2)}) collective-permute-start(bf16[128,128]{1,0:T(8,128)(2,1)S(1)} %get-tuple-element.32), channel_id=1, source_target_pairs={{0,1},{7,6},{8,9},{15,14},{16,17},{23,22},{24,25},{31,30},{2,10},{... | collective-permute-start | bytes 98312 | tf_op jit(solution)/shard_map/ppermute | solution.py:548
  10.6 3.0 %collective-permute-done.refs_2_.refs_3_ = bf16[128,128]{1,0:T(8,128)(2,1)S(1)} collective-permute-done((bf16[128,128]{1,0:T(8,128)(2,1)S(1)}, bf16[128,128]{1,0:T(8,128)(2,1)S(1)}, u32[]{:S(2)}, u32[]{:S(2)}) %collective-permute-start) | collective-permute-done | bytes 32800 | tf_op jit(solution)/shard_map/ppermute | solution.py:548
  13.6 3.2 %stage1.1 = (bf16[128,128]{1,0:T(8,128)(2,1)S(1)}, bf16[32,128,128]{2,1,0:T(8,128)(2,1)S(1)}, bf16[32,128,128]{2,1,0:T(8,128)(2,1)S(1)}) custom-call(f32[2,8,128]{2,1,0:T(8,128)S(1)} %get-tuple-element.28.prices_ref, bf16[32,128,128]{2,1,0:T(8,128)(2,1)S(1)} %get-tuple-element.29.costs_ref, ...), custom_call_target="tpu_custom_call", output_to_operand_aliasing={{1}: (5, {}), {2}: (6, {})} | custom-call | tf_op jit(solution)/shard_map/stage1/pallas_call | solution.py:519
  16.8 2.0 %collective-permute-start.1 = (bf16[128,128]{1,0:T(8,128)(2,1)S(1)}, bf16[128,128]{1,0:T(8,128)(2,1)S(1)}, u32[]{:S(2)}, u32[]{:S(2)}) collective-permute-start(bf16[128,128]{1,0:T(8,128)(2,1)S(1)} %get-tuple-element.36), channel_id=1, source_target_pairs={{1,2},{6,5},{9,10},{14,13},{17,18},{22,21},{25,26},{30,29},{0,8},{... | collective-permute-start | bytes 98312 | tf_op jit(solution)/shard_map/ppermute | solution.py:548
  18.9 1.0 %collective-permute-done.1.refs_4_ = bf16[128,128]{1,0:T(8,128)(2,1)S(1)} collective-permute-done((bf16[128,128]{1,0:T(8,128)(2,1)S(1)}, bf16[128,128]{1,0:T(8,128)(2,1)S(1)}, u32[]{:S(2)}, u32[]{:S(2)}) %collective-permute-start.1) | collective-permute-done | bytes 32800 | tf_op jit(solution)/shard_map/ppermute | solution.py:548
  19.9 0.7 stage2.1
  20.6 3.2 %collective-permute-start.2 = (bf16[128,128]{1,0:T(8,128)(2,1)S(1)}, bf16[128,128]{1,0:T(8,128)(2,1)S(1)}, u32[]{:S(2)}, u32[]{:S(2)}) collective-permute-start(bf16[128,128]{1,0:T(8,128)(2,1)S(1)} %get-tuple-element.38), channel_id=1, source_target_pairs={{2,3},{5,4},{10,11},{13,12},{18,19},{21,20},{26,27},{29,28},{8,16}... | collective-permute-start | bytes 98312 | tf_op jit(solution)/shard_map/ppermute | solution.py:548
  23.8 1.0 %collective-permute-done.2.refs_5_ = bf16[128,128]{1,0:T(8,128)(2,1)S(1)} collective-permute-done((bf16[128,128]{1,0:T(8,128)(2,1)S(1)}, bf16[128,128]{1,0:T(8,128)(2,1)S(1)}, u32[]{:S(2)}, u32[]{:S(2)}) %collective-permute-start.2) | collective-permute-done | bytes 32800 | tf_op jit(solution)/shard_map/ppermute | solution.py:548
  25.5 0.7 collective-permute-start.3
  26.2 1.3 %collective-permute-start.5 = (bf16[128,128]{1,0:T(8,128)(2,1)S(1)}, bf16[128,128]{1,0:T(8,128)(2,1)S(1)}, u32[]{:S(2)}, u32[]{:S(2)}) collective-permute-start(bf16[128,128]{1,0:T(8,128)(2,1)S(1)} %get-tuple-element.42), channel_id=1, source_target_pairs={{4,5},{3,2},{12,13},{11,10},{20,21},{19,18},{28,29},{27,26},{17,25... | collective-permute-start | bytes 98312 | tf_op jit(solution)/shard_map/ppermute | solution.py:548
  27.5 9.2 %collective-permute-done.5.refs_7_ = bf16[128,128]{1,0:T(8,128)(2,1)S(1)} collective-permute-done((bf16[128,128]{1,0:T(8,128)(2,1)S(1)}, bf16[128,128]{1,0:T(8,128)(2,1)S(1)}, u32[]{:S(2)}, u32[]{:S(2)}) %collective-permute-start.5) | collective-permute-done | bytes 32800 | tf_op jit(solution)/shard_map/ppermute | solution.py:548
  36.7 3.8 %stage5.1 = (bf16[128,128]{1,0:T(8,128)(2,1)S(1)}, bf16[32,128,128]{2,1,0:T(8,128)(2,1)S(1)}, f32[32,128,128]{2,1,0:T(8,128)S(1)}) custom-call(f32[2,8,128]{2,1,0:T(8,128)S(1)} %get-tuple-element.28.prices_ref, bf16[32,128,128]{2,1,0:T(8,128)(2,1)S(1)} %get-tuple-element.29.costs_ref, ...), custom_call_target="tpu_custom_call", output_to_operand_aliasing={{1}: (10, {}), {2}: (11, {})} | custom-call | tf_op jit(solution)/shard_map/stage5/pallas_call | solution.py:519
  40.5 1.3 %collective-permute-start.6 = (bf16[128,128]{1,0:T(8,128)(2,1)S(1)}, bf16[128,128]{1,0:T(8,128)(2,1)S(1)}, u32[]{:S(2)}, u32[]{:S(2)}) collective-permute-start(bf16[128,128]{1,0:T(8,128)(2,1)S(1)} %get-tuple-element.45), channel_id=1, source_target_pairs={{5,6},{2,1},{13,14},{10,9},{21,22},{18,17},{29,30},{26,25},{19,27}... | collective-permute-start | bytes 98312 | tf_op jit(solution)/shard_map/ppermute | solution.py:548
  41.8 7.7 %collective-permute-done.6.refs_8_ = bf16[128,128]{1,0:T(8,128)(2,1)S(1)} collective-permute-done((bf16[128,128]{1,0:T(8,128)(2,1)S(1)}, bf16[128,128]{1,0:T(8,128)(2,1)S(1)}, u32[]{:S(2)}, u32[]{:S(2)}) %collective-permute-start.6) | collective-permute-done | bytes 32800 | tf_op jit(solution)/shard_map/ppermute | solution.py:548
  49.5 3.2 %stage6.1 = (bf16[128,128]{1,0:T(8,128)(2,1)S(1)}, bf16[32,128,128]{2,1,0:T(8,128)(2,1)S(1)}, f32[32,128,128]{2,1,0:T(8,128)S(1)}) custom-call(f32[2,8,128]{2,1,0:T(8,128)S(1)} %get-tuple-element.28.prices_ref, bf16[32,128,128]{2,1,0:T(8,128)(2,1)S(1)} %get-tuple-element.29.costs_ref, ...), custom_call_target="tpu_custom_call", output_to_operand_aliasing={{1}: (11, {}), {2}: (12, {})} | custom-call | tf_op jit(solution)/shard_map/stage6/pallas_call | solution.py:519
  52.7 1.3 %collective-permute-start.7 = (bf16[128,128]{1,0:T(8,128)(2,1)S(1)}, bf16[128,128]{1,0:T(8,128)(2,1)S(1)}, u32[]{:S(2)}, u32[]{:S(2)}) collective-permute-start(bf16[128,128]{1,0:T(8,128)(2,1)S(1)} %get-tuple-element.48), channel_id=1, source_target_pairs={{6,7},{1,0},{14,15},{9,8},{22,23},{17,16},{30,31},{25,24},{18,26},... | collective-permute-start | bytes 98312 | tf_op jit(solution)/shard_map/ppermute | solution.py:548
  54.0 0.8 %collective-permute-done.7.refs_9_ = bf16[128,128]{1,0:T(8,128)(2,1)S(1)} collective-permute-done((bf16[128,128]{1,0:T(8,128)(2,1)S(1)}, bf16[128,128]{1,0:T(8,128)(2,1)S(1)}, u32[]{:S(2)}, u32[]{:S(2)}) %collective-permute-start.7) | collective-permute-done | bytes 32800 | tf_op jit(solution)/shard_map/ppermute | solution.py:548
  54.9 5.4 %final.1 = (bf16[32,128,128]{2,1,0:T(8,128)(2,1)}, bf16[32,128,128]{2,1,0:T(8,128)(2,1)S(1)}, bf16[16,192,128]{2,1,0:T(8,128)(2,1)S(1)}, bf16[32,128,128]{2,1,0:T(8,128)(2,1)S(1)}, f32[32,128,128]{2,1,0:T(8,128)S(1)}) custom-call(f32[2,8,128]{2,1,0:T(8,128)S(1)} %get-tuple-element.28.prices_ref, ...), custom_call_target="tpu_custom_call", output_to_operand_aliasing={{3}: (12, {}), {4}: (13, {})} | custom-call | tf_op jit(solution)/shard_map/final/pallas_call | solution.py:519
  60.2 5.5 %collective-permute-start.8 = (bf16[16,192,128]{2,1,0:T(8,128)(2,1)S(1)}, bf16[16,192,128]{2,1,0:T(8,128)(2,1)S(1)}, u32[]{:S(2)}, u32[]{:S(2)}) collective-permute-start(bf16[16,192,128]{2,1,0:T(8,128)(2,1)S(1)} %get-tuple-element.53), channel_id=1, source_target_pairs={{1,0},{2,1},{3,2},{4,3},{5,4},{6,5},{7,6},{9,8},{10,9},{11,10},{12... | collective-permute-start | bytes 2359304 | tf_op jit(solution)/shard_map/ppermute | solution.py:569
  65.7 10.3 %collective-permute-done.8.packed_ref = bf16[16,192,128]{2,1,0:T(8,128)(2,1)S(1)} collective-permute-done((bf16[16,192,128]{2,1,0:T(8,128)(2,1)S(1)}, bf16[16,192,128]{2,1,0:T(8,128)(2,1)S(1)}, u32[]{:S(2)}, u32[]{:S(2)}) %collective-permute-start.8) | collective-permute-done | bytes 786464 | tf_op jit(solution)/shard_map/ppermute | solution.py:569
  76.0 1.8 %merge.1 = bf16[32,128,128]{2,1,0:T(8,128)(2,1)} custom-call(bf16[32,128,128]{2,1,0:T(8,128)(2,1)S(1)} %get-tuple-element.52.skewed_ref, bf16[16,192,128]{2,1,0:T(8,128)(2,1)S(1)} %collective-permute-done.8.packed_ref), custom_call_target="tpu_custom_call" | custom-call | tf_op jit(solution)/shard_map/merge/pallas_call | solution.py:570
  (6 shorter events, 0.7 us)
Async XLA Ops:
  1.9 1.2 %copy-start = (bf16[32,128,128]{2,1,0:T(8,128)(2,1)S(1)}, bf16[32,128,128]{2,1,0:T(8,128)(2,1)}, u32[]{:S(2)}) copy-start(bf16[32,128,128]{2,1,0:T(8,128)(2,1)} %costs_ref.1) | copy-start | bytes 3145732
  9.3 4.3 %collective-permute-start = (bf16[128,128]{1,0:T(8,128)(2,1)S(1)}, bf16[128,128]{1,0:T(8,128)(2,1)S(1)}, u32[]{:S(2)}, u32[]{:S(2)}) collective-permute-start(bf16[128,128]{1,0:T(8,128)(2,1)S(1)} %get-tuple-element.32), channel_id=1, source_target_pairs={{0,1},{7,6},{8,9},{15,14},{16,17},{23,22},{24,25},{31,30},{2,10},{... | collective-permute-start | bytes 98312 | tf_op jit(solution)/shard_map/ppermute | solution.py:548
  16.8 3.1 %collective-permute-start.1 = (bf16[128,128]{1,0:T(8,128)(2,1)S(1)}, bf16[128,128]{1,0:T(8,128)(2,1)S(1)}, u32[]{:S(2)}, u32[]{:S(2)}) collective-permute-start(bf16[128,128]{1,0:T(8,128)(2,1)S(1)} %get-tuple-element.36), channel_id=1, source_target_pairs={{1,2},{6,5},{9,10},{14,13},{17,18},{22,21},{25,26},{30,29},{0,8},{... | collective-permute-start | bytes 98312 | tf_op jit(solution)/shard_map/ppermute | solution.py:548
  20.6 4.3 %collective-permute-start.2 = (bf16[128,128]{1,0:T(8,128)(2,1)S(1)}, bf16[128,128]{1,0:T(8,128)(2,1)S(1)}, u32[]{:S(2)}, u32[]{:S(2)}) collective-permute-start(bf16[128,128]{1,0:T(8,128)(2,1)S(1)} %get-tuple-element.38), channel_id=1, source_target_pairs={{2,3},{5,4},{10,11},{13,12},{18,19},{21,20},{26,27},{29,28},{8,16}... | collective-permute-start | bytes 98312 | tf_op jit(solution)/shard_map/ppermute | solution.py:548
  24.8 1.3 %collective-permute-start.4 = (bf16[128,128]{1,0:T(8,128)(2,1)S(1)}, bf16[128,128]{1,0:T(8,128)(2,1)S(1)}, u32[]{:S(2)}, u32[]{:S(2)}) collective-permute-start(bf16[128,128]{1,0:T(8,128)(2,1)S(1)} %get-tuple-element.40), channel_id=1, source_target_pairs={{4,3},{12,11},{20,19},{28,27}} | collective-permute-start | bytes 98312 | tf_op jit(solution)/shard_map/ppermute | solution.py:551
  25.5 0.7 collective-permute-start.3
  26.2 10.5 %collective-permute-start.5 = (bf16[128,128]{1,0:T(8,128)(2,1)S(1)}, bf16[128,128]{1,0:T(8,128)(2,1)S(1)}, u32[]{:S(2)}, u32[]{:S(2)}) collective-permute-start(bf16[128,128]{1,0:T(8,128)(2,1)S(1)} %get-tuple-element.42), channel_id=1, source_target_pairs={{4,5},{3,2},{12,13},{11,10},{20,21},{19,18},{28,29},{27,26},{17,25... | collective-permute-start | bytes 98312 | tf_op jit(solution)/shard_map/ppermute | solution.py:548
  40.5 9.0 %collective-permute-start.6 = (bf16[128,128]{1,0:T(8,128)(2,1)S(1)}, bf16[128,128]{1,0:T(8,128)(2,1)S(1)}, u32[]{:S(2)}, u32[]{:S(2)}) collective-permute-start(bf16[128,128]{1,0:T(8,128)(2,1)S(1)} %get-tuple-element.45), channel_id=1, source_target_pairs={{5,6},{2,1},{13,14},{10,9},{21,22},{18,17},{29,30},{26,25},{19,27}... | collective-permute-start | bytes 98312 | tf_op jit(solution)/shard_map/ppermute | solution.py:548
  52.7 2.1 %collective-permute-start.7 = (bf16[128,128]{1,0:T(8,128)(2,1)S(1)}, bf16[128,128]{1,0:T(8,128)(2,1)S(1)}, u32[]{:S(2)}, u32[]{:S(2)}) collective-permute-start(bf16[128,128]{1,0:T(8,128)(2,1)S(1)} %get-tuple-element.48), channel_id=1, source_target_pairs={{6,7},{1,0},{14,15},{9,8},{22,23},{17,16},{30,31},{25,24},{18,26},... | collective-permute-start | bytes 98312 | tf_op jit(solution)/shard_map/ppermute | solution.py:548
  60.2 15.8 %collective-permute-start.8 = (bf16[16,192,128]{2,1,0:T(8,128)(2,1)S(1)}, bf16[16,192,128]{2,1,0:T(8,128)(2,1)S(1)}, u32[]{:S(2)}, u32[]{:S(2)}) collective-permute-start(bf16[16,192,128]{2,1,0:T(8,128)(2,1)S(1)} %get-tuple-element.53), channel_id=1, source_target_pairs={{1,0},{2,1},{3,2},{4,3},{5,4},{6,5},{7,6},{9,8},{10,9},{11,10},{12... | collective-permute-start | bytes 2359304 | tf_op jit(solution)/shard_map/ppermute | solution.py:569

commit v6 on v5

--- a/solution.py
+++ b/solution.py
@@ -137,7 +137,7 @@
     lax.fori_loop(0, rows // batch, body, 0, unroll=2)
 
 
-def sweep(v, tiles_ref, lows_ref, sums_ref, rows, west, first, q1, q2):
+def sweep(v, tiles_ref, lows_ref, raw_ref, jumps_ref, rows, west, q1, q2):
     cols, depth, lanes = tiles_ref.shape
     pack = lanes // rows
     lane = lax.broadcasted_iota(jnp.int32, (SUB, lanes), 1)
@@ -148,27 +148,21 @@
     def body(i, carry):
         v, jump = list(carry[:-1]), carry[-1]
         at = jnp.where(west, cols // pack - 1 - i, i)
-        found = None
         for j in range(pack):
             x = at * pack + groups[j]
             c = split(tiles_ref[x])
             below = [jnp.where(sub == 0, BIG, pltpu.roll(v[-1], 1, 0))] + v[:-1]
             above = v[1:] + [jnp.where(sub == SUB - 1, BIG, pltpu.roll(v[0], SUB - 1, 0))]
             near = [
-                jnp.minimum(n, jnp.minimum(a, b) + q1) + k
-                for n, a, b, k in zip(v, below, above, c)
+                jnp.minimum(n, jnp.minimum(a, b) + q1) for n, a, b in zip(v, below, above)
             ]
-            far = [k + jump for k in c]
-            v = [jnp.minimum(a, b) for a, b in zip(near, far)]
-            jump = jnp.minimum(fold_min(near), lows_ref[x] + jump) + q2
-            extra = [a - b for a, b in zip(v, far)]
-            if found is None:
-                found = extra
-            else:
-                found = [jnp.where(mine[j], a, b) for a, b in zip(extra, found)]
-        if not first:
-            found = [a + b for a, b in zip(found, split(sums_ref[at]))]
-        sums_ref[at] = join(found)
+            best = [jnp.minimum(n, jump) for n in near]
+            for k, x_best in enumerate(best):
+                pltpu.store(raw_ref.at[at, pl.ds(k * SUB, SUB), :], x_best, mask=mine[j])
+            pltpu.store(jumps_ref.at[at], jump, mask=mine[j])
+            low = fold_min([n + k for n, k in zip(near, c)])
+            v = [n + k for n, k in zip(best, c)]
+            jump = jnp.minimum(low, lows_ref[x] + jump) + q2
         return tuple(v) + (jump,)
 
     last = lax.fori_loop(0, cols // pack, body, tuple(v) + (fold_min(v) + q2,))
@@ -270,21 +264,22 @@
     col_here, row_here = lax.axis_index("col"), lax.axis_index("row")
     q1, q2 = penalties(prices_ref)
 
-    if s < plan.cols - 1:
-
-        @pl.when((col_here == s) | (col_here == plan.cols - 1 - s))
+    hop = plan.hop_at(s)
+    if hop is None:
+        out_ref[...] = refs["passed"][...]
+    elif hop < plan.cols - 1:
+
+        @pl.when((col_here == hop) | (col_here == plan.cols - 1 - hop))
         def _():
-            west = col_here != s
-            if s:
-                v = split(arrivals[s - 1][...])
+            west = col_here != hop
+            if hop:
+                v = split(arrivals[plan.step(hop - 1, False)][...])
+                other = split(arrivals[plan.step(hop - 1, True)][...])
+                v = [jnp.where(west, b, a) for a, b in zip(v, other)]
             else:
                 v = [jnp.zeros((SUB, cols), jnp.float32)] * (depth // SUB)
-            if plan.crossing(s - 1):
-                other = split(refs["crossed"][...])
-                v = [jnp.where(west, b, a) for a, b in zip(v, other)]
-            first = 2 * s < plan.cols
-            v = sweep(v, tiles_ref, refs["lows"], refs["sums"], rows, west, first, q1, q2)
-            out_ref[...] = join(v)
+            raw, jumps = (refs[n] for n in plan.paths(hop))
+            out_ref[...] = join(sweep(v, tiles_ref, refs["lows"], raw, jumps, rows, west, q1, q2))
 
     turning = plan.turning(s)
     if turning:
@@ -339,9 +334,7 @@
     arrivals = [refs[f"arrival{n}"] for n in range(plan.stages)]
     rows, cols, depth = costs_ref.shape
     lanes = cols
-    held_ref, sums_ref, base_ref, natural_ref = (
-        refs["held"], refs["sums"], refs["base"], refs["natural"]
-    )
+    held_ref, base_ref, natural_ref = refs["held"], refs["base"], refs["natural"]
     q1, q2 = penalties(prices_ref)
     col_here, row_here = lax.axis_index("col"), lax.axis_index("row")
 
@@ -356,13 +349,22 @@
 
     @pl.when((col_here == 0) | (col_here == plan.cols - 1))
     def _():
-        v = split(arrivals[plan.cols - 2][...])
-        sweep(v, refs["tiles"], refs["lows"], sums_ref, rows, col_here == 0, False, q1, q2)
+        v = split(arrivals[plan.step(plan.cols - 2, True)][...])
+        raw, jumps = refs["second"], refs["second_jumps"]
+        sweep(v, refs["tiles"], refs["lows"], raw, jumps, rows, col_here == 0, q1, q2)
 
     order, mix = interleave(2 * cols), interleave(depth)
 
+    def added(at):
+        total = None
+        for name in ("first", "second"):
+            jump = refs[f"{name}_jumps"][at]
+            part = [x - jump for x in split(refs[name][at])]
+            total = part if total is None else [a + b for a, b in zip(total, part)]
+        return join(total)
+
     def turn(i, carry):
-        pair = jnp.concatenate([sums_ref[2 * i], sums_ref[2 * i + 1]], axis=1)
+        pair = jnp.concatenate([added(2 * i), added(2 * i + 1)], axis=1)
         flat = dot(order, pair, TRANSPOSED).astype(jnp.bfloat16)
         at = pl.ds(pl.multiple_of(i * SUB, SUB), SUB)
         natural_ref[:, at, :] = dot(flat, mix, PLAIN).reshape(rows, SUB, depth)
@@ -423,31 +425,43 @@
 class Plan:
     def __init__(self, rows, cols):
         self.rows, self.cols = rows, cols
+        self.half = cols // 2
         self.slots = []
         for c in range(cols):
-            busy = {c - 1, c, cols - 2 - c, cols - 1 - c}
-            free = [s for s in range(cols + 4 + rows) if s not in busy or s >= cols - 1]
+            busy = set()
+            if c > 0:
+                busy |= {self.step(c - 1, False), self.step(cols - 1 - c, True)}
+            if c < cols - 1:
+                busy |= {self.step(c, False), self.step(cols - 2 - c, True)}
+            free = [s for s in range(cols + 4 + rows) if s not in busy]
             self.slots.append(free[: rows - 1])
         last = [slots[-1] + 1 for slots in self.slots if slots]
-        self.stages = max([cols - 1] + last)
-
-    def crossing(self, s):
-        return 2 * s == self.cols - 2
-
-    def numbers(self, pairs):
-        number = lambda place: place[0] * self.cols + place[1]
-        return [(number(a), number(b)) for a, b in pairs]
-
-    def crossed_route(self, s):
-        return self.numbers([((r, s + 1), (r, s)) for r in range(self.rows)])
+        self.stages = max([cols] + last)
+
+    def step(self, hop, west):
+        if hop < self.half - 1:
+            return hop
+        if hop == self.half - 1:
+            return hop + 1 if west else hop
+        return hop + 1
+
+    def hop_at(self, s):
+        if s == self.half:
+            return None
+        return s if s < self.half else s - 1
+
+    def paths(self, hop):
+        name = "first" if hop < self.half else "second"
+        return [name, f"{name}_jumps"]
 
     def route(self, s):
         pairs = []
-        if s < self.cols - 1:
+        for h in range(self.cols - 1):
             for r in range(self.rows):
-                pairs.append(((r, s), (r, s + 1)))
-                if not self.crossing(s):
-                    pairs.append(((r, self.cols - 1 - s), (r, self.cols - 2 - s)))
+                if self.step(h, False) == s:
+                    pairs.append(((r, h), (r, h + 1)))
+                if self.step(h, True) == s:
+                    pairs.append(((r, self.cols - 1 - h), (r, self.cols - 2 - h)))
         for c, slots in enumerate(self.slots):
             if s in slots:
                 j = slots.index(s)
@@ -455,7 +469,8 @@
                     ((j, c), (j + 1, c)),
                     ((self.rows - 1 - j, c), (self.rows - 2 - j, c)),
                 ]
-        return self.numbers(pairs)
+        number = lambda place: place[0] * self.cols + place[1]
+        return [(number(a), number(b)) for a, b in pairs]
 
     def turning(self, s):
         ends = {0, self.cols - 1}
@@ -465,7 +480,7 @@
         found = []
         for c, slots in enumerate(self.slots):
             at = slots[-1] + 1
-            while at < self.stages and at in (c, self.cols - 1 - c):
+            while at < self.stages and self.hop_at(at) in (c, self.cols - 1 - c):
                 at += 1
             if at == s:
                 found.append(c)
@@ -483,7 +498,10 @@
     front = jax.ShapeDtypeStruct((depth, cols), jnp.bfloat16)
     tile = jax.ShapeDtypeStruct((rows, cols, depth), jnp.bfloat16)
     shapes = {
-        "sums": jax.ShapeDtypeStruct((rows, depth, cols), jnp.bfloat16),
+        "first": jax.ShapeDtypeStruct((rows, depth, cols), jnp.float32),
+        "first_jumps": jax.ShapeDtypeStruct((rows, SUB, cols), jnp.float32),
+        "second": jax.ShapeDtypeStruct((rows, depth, cols), jnp.float32),
+        "second_jumps": jax.ShapeDtypeStruct((rows, SUB, cols), jnp.float32),
         "turned": jax.ShapeDtypeStruct((rows, depth, cols), jnp.bfloat16),
         "base": jax.ShapeDtypeStruct((rows, cols, depth), jnp.float32),
     }
@@ -531,12 +549,13 @@
         buffers.update(zip(outputs, values))
 
     for s in range(plan.stages):
-        writes = ["sums"] if s < plan.cols - 1 else []
+        hop = plan.hop_at(s)
+        writes = plan.paths(hop) if hop is not None and hop < plan.cols - 1 else []
         writes += ["turned"] if s < 2 else []
         writes += ["base"] if plan.settling(s) else []
         reads = ["tiles", "lows"] + ([] if "turned" in writes else ["turned"])
         reads += [f"arrival{n}" for n in range(s)]
-        reads += ["crossed"] if plan.crossing(s - 1) else []
+        reads += ["passed"] if hop is None else []
         run(
             functools.partial(stage_kernel, plan, s),
             f"stage{s}",
@@ -546,9 +565,7 @@
             {"held": held, "vsums": vsums},
         )
         buffers[f"arrival{s}"] = lax.ppermute(buffers["sent"], ("row", "col"), plan.route(s))
-        if plan.crossing(s):
-            route = plan.crossed_route(s)
-            buffers["crossed"] = lax.ppermute(buffers["sent"], ("row", "col"), route)
+        buffers["passed"] = buffers["sent"]
 
     run(
         functools.partial(final_kernel, plan),
@@ -558,8 +575,9 @@
             "skewed": tile,
             "packed": jax.ShapeDtypeStruct((rows // 2, cols // 2 * 3, depth), jnp.bfloat16),
         },
-        ["tiles", "lows", "turned"] + [f"arrival{n}" for n in range(plan.stages)],
-        ["sums", "base"],
+        ["tiles", "lows", "turned", "first", "first_jumps"]
+        + [f"arrival{n}" for n in range(plan.stages)],
+        ["second", "second_jumps", "base"],
         {
             "held": held,
             "vsums": vsums,

time: 78.1 us -> 78.6 us (level)
  waiting for transfers between devices: 33.1 us -> 34.2 us
  Pallas kernels: 24.2 us -> 23.2 us
    ppermute x7 -> x8, waiting for transfers between devices: 22.8 us -> 25.7 us  [shards(): lax.ppermute(buffers['sent'], ('row', 'col'), plan.route(s))]
    ppermute x1, waiting for transfers between devices: 10.3 us -> 8.45 us  [shards(): lax.ppermute(buffers['packed'], 'col', [(i, i - 1) for i in range(1, plan...]
    ppermute x7 -> x8, starting transfers between devices: 11.1 us -> 12.8 us  [shards(): lax.ppermute(buffers['sent'], ('row', 'col'), plan.route(s))]
    pallas_call x8 -> x9, Pallas kernels: 17.2 us -> 16.3 us  [run(): pl.pallas_call(functools.partial(body, names), out_shape=tuple([results[n...]
where the time goes in v6:
time: 78.6 us; the launch traced here: 78.3 us
  waiting for transfers between devices  34.2 us (44%)
  Pallas kernels  23.2 us (30%)
  starting transfers between devices  17.7 us (23%)
  between operations  2.07 us (3%)
  local copies, waits for them, and re-layouts  1.22 us (2%)
    ppermute x8, waiting for transfers between devices, shards(): lax.ppermute(buffers['sent'], ('row', 'col'), plan.route(s))  25.7 us
    pallas_call x9, Pallas kernels, run(): pl.pallas_call(functools.partial(body, names), out_shape=tuple([results[n...  16.3 us
    ppermute x8, starting transfers between devices, shards(): lax.ppermute(buffers['sent'], ('row', 'col'), plan.route(s))  12.8 us
    ppermute x1, waiting for transfers between devices, shards(): lax.ppermute(buffers['packed'], 'col', [(i, i - 1) for i in range(1, plan...  8.45 us
    pallas_call x1, Pallas kernels, shards(): pl.pallas_call(prepare_kernel, out_shape=(jax.ShapeDtypeStruct((cols, dep...  5.16 us
    ppermute x1, starting transfers between devices, shards(): lax.ppermute(buffers['packed'], 'col', [(i, i - 1) for i in range(1, plan...  4.84 us
    pallas_call x1, Pallas kernels, shards(): pl.pallas_call(merge_kernel, out_shape=tile, in_specs=in_vmem(2), out_spe...  1.78 us
  transfers between devices with their start and end apart: 9, of which 7 were waited for; matrix products, arithmetic and copies ran while one was open for 0% of the time, Pallas kernels for 0%

profile of v6, /device:TPU:1, one launch (start us, length us, event | category | flops | bytes accessed | tf_op | source)
XLA Modules:
  0.0 78.3 jit_solution(10374477192061010549)
XLA Ops:
  1.9 1.2 %copy-done = bf16[32,128,128]{2,1,0:T(8,128)(2,1)S(1)} copy-done((bf16[32,128,128]{2,1,0:T(8,128)(2,1)S(1)}, bf16[32,128,128]{2,1,0:T(8,128)(2,1)}, u32[]{:S(2)}) %copy-start) | copy-done | bytes 1048600
  3.1 5.2 %prepare.1 = (f32[128,128,128]{2,1,0:T(8,128)S(1)}, f32[128,8,128]{2,1,0:T(8,128)S(1)}, f32[2,8,128]{2,1,0:T(8,128)S(1)}, bf16[32,128,128]{2,1,0:T(8,128)(2,1)S(1)}) custom-call(bf16[32,128,128]{2,1,0:T(8,128)(2,1)S(1)} %copy-done, s32[1]{0:T(128)S(6)} %copy.37.small_ref, s32[1]{0:T(128)S(6)} %copy.38.large_ref), custom_call_target="tpu_custom_call" | custom-call | tf_op jit(solution)/shard_map/prepare/pallas_call | solution.py:511
  8.3 1.0 %stage0.1 = (bf16[128,128]{1,0:T(8,128)(2,1)S(1)}, f32[32,128,128]{2,1,0:T(8,128)S(1)}, f32[32,8,128]{2,1,0:T(8,128)S(1)}, bf16[32,128,128]{2,1,0:T(8,128)(2,1)S(1)}) custom-call(f32[2,8,128]{2,1,0:T(8,128)S(1)} %get-tuple-element.36.prices_ref, bf16[32,128,128]{2,1,0:T(8,128)(2,1)S(1)} %get-tuple-element.37.costs_ref, ...), custom_call_target="tpu_custom_call" | custom-call | tf_op jit(solution)/shard_map/stage0/pallas_call | solution.py:537
  9.3 1.3 %collective-permute-start = (bf16[128,128]{1,0:T(8,128)(2,1)S(1)}, bf16[128,128]{1,0:T(8,128)(2,1)S(1)}, u32[]{:S(2)}, u32[]{:S(2)}) collective-permute-start(bf16[128,128]{1,0:T(8,128)(2,1)S(1)} %get-tuple-element.40), channel_id=1, source_target_pairs={{0,1},{7,6},{8,9},{15,14},{16,17},{23,22},{24,25},{31,30},{2,10},{... | collective-permute-start | bytes 98312 | tf_op jit(solution)/shard_map/ppermute | solution.py:567
  10.6 2.5 %collective-permute-done.refs_2_.refs_3_.refs_5_ = bf16[128,128]{1,0:T(8,128)(2,1)S(1)} collective-permute-done((bf16[128,128]{1,0:T(8,128)(2,1)S(1)}, bf16[128,128]{1,0:T(8,128)(2,1)S(1)}, u32[]{:S(2)}, u32[]{:S(2)}) %collective-permute-start) | collective-permute-done | bytes 32800 | tf_op jit(solution)/shard_map/ppermute | solution.py:567
  13.1 2.7 %stage1.1 = (bf16[128,128]{1,0:T(8,128)(2,1)S(1)}, f32[32,128,128]{2,1,0:T(8,128)S(1)}, f32[32,8,128]{2,1,0:T(8,128)S(1)}, bf16[32,128,128]{2,1,0:T(8,128)(2,1)S(1)}) custom-call(f32[2,8,128]{2,1,0:T(8,128)S(1)} %get-tuple-element.36.prices_ref, ...), custom_call_target="tpu_custom_call", output_to_operand_aliasing={{1}: (5, {}), {2}: (6, {}), {3}: (7, {})} | custom-call | tf_op jit(solution)/shard_map/stage1/pallas_call | solution.py:537
  15.8 3.1 %collective-permute-start.1 = (bf16[128,128]{1,0:T(8,128)(2,1)S(1)}, bf16[128,128]{1,0:T(8,128)(2,1)S(1)}, u32[]{:S(2)}, u32[]{:S(2)}) collective-permute-start(bf16[128,128]{1,0:T(8,128)(2,1)S(1)} %get-tuple-element.45), channel_id=1, source_target_pairs={{1,2},{6,5},{9,10},{14,13},{17,18},{22,21},{25,26},{30,29},{0,8},{... | collective-permute-start | bytes 98312 | tf_op jit(solution)/shard_map/ppermute | solution.py:567
  18.9 1.0 %collective-permute-done.1.refs_4_.refs_6_ = bf16[128,128]{1,0:T(8,128)(2,1)S(1)} collective-permute-done((bf16[128,128]{1,0:T(8,128)(2,1)S(1)}, bf16[128,128]{1,0:T(8,128)(2,1)S(1)}, u32[]{:S(2)}, u32[]{:S(2)}) %collective-permute-start.1) | collective-permute-done | bytes 32800 | tf_op jit(solution)/shard_map/ppermute | solution.py:567
  19.9 0.7 stage2.1
  20.6 3.2 %collective-permute-start.2 = (bf16[128,128]{1,0:T(8,128)(2,1)S(1)}, bf16[128,128]{1,0:T(8,128)(2,1)S(1)}, u32[]{:S(2)}, u32[]{:S(2)}) collective-permute-start(bf16[128,128]{1,0:T(8,128)(2,1)S(1)} %get-tuple-element.48), channel_id=1, source_target_pairs={{2,3},{5,4},{10,11},{13,12},{18,19},{21,20},{26,27},{29,28},{8,16}... | collective-permute-start | bytes 98312 | tf_op jit(solution)/shard_map/ppermute | solution.py:567
  23.8 1.0 %collective-permute-done.2.refs_5_.refs_7_ = bf16[128,128]{1,0:T(8,128)(2,1)S(1)} collective-permute-done((bf16[128,128]{1,0:T(8,128)(2,1)S(1)}, bf16[128,128]{1,0:T(8,128)(2,1)S(1)}, u32[]{:S(2)}, u32[]{:S(2)}) %collective-permute-start.2) | collective-permute-done | bytes 32800 | tf_op jit(solution)/shard_map/ppermute | solution.py:567
  25.5 1.3 %collective-permute-start.4 = (bf16[128,128]{1,0:T(8,128)(2,1)S(1)}, bf16[128,128]{1,0:T(8,128)(2,1)S(1)}, u32[]{:S(2)}, u32[]{:S(2)}) collective-permute-start(bf16[128,128]{1,0:T(8,128)(2,1)S(1)} %get-tuple-element.54), channel_id=1, source_target_pairs={{4,3},{12,11},{20,19},{28,27},{17,25},{9,1},{18,26},{10,2},{21,29}... | collective-permute-start | bytes 98312 | tf_op jit(solution)/shard_map/ppermute | solution.py:567
  26.8 9.2 %collective-permute-done.4.refs_7_.refs_9_ = bf16[128,128]{1,0:T(8,128)(2,1)S(1)} collective-permute-done((bf16[128,128]{1,0:T(8,128)(2,1)S(1)}, bf16[128,128]{1,0:T(8,128)(2,1)S(1)}, u32[]{:S(2)}, u32[]{:S(2)}) %collective-permute-start.4) | collective-permute-done | bytes 32800 | tf_op jit(solution)/shard_map/ppermute | solution.py:567
  36.1 3.8 %stage5.1 = (bf16[128,128]{1,0:T(8,128)(2,1)S(1)}, f32[32,128,128]{2,1,0:T(8,128)S(1)}, f32[32,8,128]{2,1,0:T(8,128)S(1)}, f32[32,128,128]{2,1,0:T(8,128)S(1)}) custom-call(f32[2,8,128]{2,1,0:T(8,128)S(1)} %get-tuple-element.36.prices_ref, bf16[32,128,128]{2,1,0:T(8,128)(2,1)S(1)} %get-tuple-element.37.costs_ref, ...), custom_call_target="tpu_custom_call", output_to_operand_aliasing={{3}: (10, {})} | custom-call | tf_op jit(solution)/shard_map/stage5/pallas_call | solution.py:537
  39.8 0.7 collective-permute-start.5
  40.6 1.3 %collective-permute-start.6 = (bf16[128,128]{1,0:T(8,128)(2,1)S(1)}, bf16[128,128]{1,0:T(8,128)(2,1)S(1)}, u32[]{:S(2)}, u32[]{:S(2)}) collective-permute-start(bf16[128,128]{1,0:T(8,128)(2,1)S(1)} %get-tuple-element.59), channel_id=1, source_target_pairs={{5,6},{2,1},{13,14},{10,9},{21,22},{18,17},{29,30},{26,25},{19,27}... | collective-permute-start | bytes 98312 | tf_op jit(solution)/shard_map/ppermute | solution.py:567
  41.9 11.2 %collective-permute-done.6.refs_9_.refs_11_ = bf16[128,128]{1,0:T(8,128)(2,1)S(1)} collective-permute-done((bf16[128,128]{1,0:T(8,128)(2,1)S(1)}, bf16[128,128]{1,0:T(8,128)(2,1)S(1)}, u32[]{:S(2)}, u32[]{:S(2)}) %collective-permute-start.6) | collective-permute-done | bytes 32800 | tf_op jit(solution)/shard_map/ppermute | solution.py:567
  53.0 2.7 %stage7.1 = (bf16[128,128]{1,0:T(8,128)(2,1)S(1)}, f32[32,128,128]{2,1,0:T(8,128)S(1)}, f32[32,8,128]{2,1,0:T(8,128)S(1)}, f32[32,128,128]{2,1,0:T(8,128)S(1)}) custom-call(f32[2,8,128]{2,1,0:T(8,128)S(1)} %get-tuple-element.36.prices_ref, ...), custom_call_target="tpu_custom_call", output_to_operand_aliasing={{1}: (12, {}), {2}: (13, {}), {3}: (14, {})} | custom-call | tf_op jit(solution)/shard_map/stage7/pallas_call | solution.py:537
  55.7 1.3 %collective-permute-start.7 = (bf16[128,128]{1,0:T(8,128)(2,1)S(1)}, bf16[128,128]{1,0:T(8,128)(2,1)S(1)}, u32[]{:S(2)}, u32[]{:S(2)}) collective-permute-start(bf16[128,128]{1,0:T(8,128)(2,1)S(1)} %get-tuple-element.63), channel_id=1, source_target_pairs={{6,7},{1,0},{14,15},{9,8},{22,23},{17,16},{30,31},{25,24}} | collective-permute-start | bytes 98312 | tf_op jit(solution)/shard_map/ppermute | solution.py:567
  57.0 0.8 %collective-permute-done.7.refs_12_ = bf16[128,128]{1,0:T(8,128)(2,1)S(1)} collective-permute-done((bf16[128,128]{1,0:T(8,128)(2,1)S(1)}, bf16[128,128]{1,0:T(8,128)(2,1)S(1)}, u32[]{:S(2)}, u32[]{:S(2)}) %collective-permute-start.7) | collective-permute-done | bytes 32800 | tf_op jit(solution)/shard_map/ppermute | solution.py:567
  57.9 5.4 %final.1 = (bf16[32,128,128]{2,1,0:T(8,128)(2,1)}, bf16[32,128,128]{2,1,0:T(8,128)(2,1)S(1)}, bf16[16,192,128]{2,1,0:T(8,128)(2,1)S(1)}, f32[32,128,128]{2,1,0:T...) custom-call(f32[2,8,128]{2,1,0:T(8,128)S(1)} %get-tuple-element.36.p, ...), custom_call_target="tpu_custom_call", output_to_operand_aliasing={{3}: (15, {}), {4}: (16, {}), {5}: (17, {})} | custom-call | tf_op jit(solution)/shard_map/final/pallas_call | solution.py:537
  63.3 4.8 %collective-permute-start.8 = (bf16[16,192,128]{2,1,0:T(8,128)(2,1)S(1)}, bf16[16,192,128]{2,1,0:T(8,128)(2,1)S(1)}, u32[]{:S(2)}, u32[]{:S(2)}) collective-permute-start(bf16[16,192,128]{2,1,0:T(8,128)(2,1)S(1)} %get-tuple-element.69), channel_id=1, source_target_pairs={{1,0},{2,1},{3,2},{4,3},{5,4},{6,5},{7,6},{9,8},{10,9},{11,10},{12... | collective-permute-start | bytes 2359304 | tf_op jit(solution)/shard_map/ppermute | solution.py:587
  68.1 8.4 %collective-permute-done.8.packed_ref = bf16[16,192,128]{2,1,0:T(8,128)(2,1)S(1)} collective-permute-done((bf16[16,192,128]{2,1,0:T(8,128)(2,1)S(1)}, bf16[16,192,128]{2,1,0:T(8,128)(2,1)S(1)}, u32[]{:S(2)}, u32[]{:S(2)}) %collective-permute-start.8) | collective-permute-done | bytes 786464 | tf_op jit(solution)/shard_map/ppermute | solution.py:587
  76.5 1.8 %merge.1 = bf16[32,128,128]{2,1,0:T(8,128)(2,1)} custom-call(bf16[32,128,128]{2,1,0:T(8,128)(2,1)S(1)} %get-tuple-element.68.skewed_ref, bf16[16,192,128]{2,1,0:T(8,128)(2,1)S(1)} %collective-permute-done.8.packed_ref), custom_call_target="tpu_custom_call" | custom-call | tf_op jit(solution)/shard_map/merge/pallas_call | solution.py:588
  (7 shorter events, 0.7 us)
Async XLA Ops:
  1.9 1.2 %copy-start = (bf16[32,128,128]{2,1,0:T(8,128)(2,1)S(1)}, bf16[32,128,128]{2,1,0:T(8,128)(2,1)}, u32[]{:S(2)}) copy-start(bf16[32,128,128]{2,1,0:T(8,128)(2,1)} %costs_ref.1) | copy-start | bytes 3145732
  9.3 3.8 %collective-permute-start = (bf16[128,128]{1,0:T(8,128)(2,1)S(1)}, bf16[128,128]{1,0:T(8,128)(2,1)S(1)}, u32[]{:S(2)}, u32[]{:S(2)}) collective-permute-start(bf16[128,128]{1,0:T(8,128)(2,1)S(1)} %get-tuple-element.40), channel_id=1, source_target_pairs={{0,1},{7,6},{8,9},{15,14},{16,17},{23,22},{24,25},{31,30},{2,10},{... | collective-permute-start | bytes 98312 | tf_op jit(solution)/shard_map/ppermute | solution.py:567
  15.8 4.1 %collective-permute-start.1 = (bf16[128,128]{1,0:T(8,128)(2,1)S(1)}, bf16[128,128]{1,0:T(8,128)(2,1)S(1)}, u32[]{:S(2)}, u32[]{:S(2)}) collective-permute-start(bf16[128,128]{1,0:T(8,128)(2,1)S(1)} %get-tuple-element.45), channel_id=1, source_target_pairs={{1,2},{6,5},{9,10},{14,13},{17,18},{22,21},{25,26},{30,29},{0,8},{... | collective-permute-start | bytes 98312 | tf_op jit(solution)/shard_map/ppermute | solution.py:567
  20.6 4.3 %collective-permute-start.2 = (bf16[128,128]{1,0:T(8,128)(2,1)S(1)}, bf16[128,128]{1,0:T(8,128)(2,1)S(1)}, u32[]{:S(2)}, u32[]{:S(2)}) collective-permute-start(bf16[128,128]{1,0:T(8,128)(2,1)S(1)} %get-tuple-element.48), channel_id=1, source_target_pairs={{2,3},{5,4},{10,11},{13,12},{18,19},{21,20},{26,27},{29,28},{8,16}... | collective-permute-start | bytes 98312 | tf_op jit(solution)/shard_map/ppermute | solution.py:567
  24.8 0.7 collective-permute-start.3
  25.5 10.5 %collective-permute-start.4 = (bf16[128,128]{1,0:T(8,128)(2,1)S(1)}, bf16[128,128]{1,0:T(8,128)(2,1)S(1)}, u32[]{:S(2)}, u32[]{:S(2)}) collective-permute-start(bf16[128,128]{1,0:T(8,128)(2,1)S(1)} %get-tuple-element.54), channel_id=1, source_target_pairs={{4,3},{12,11},{20,19},{28,27},{17,25},{9,1},{18,26},{10,2},{21,29}... | collective-permute-start | bytes 98312 | tf_op jit(solution)/shard_map/ppermute | solution.py:567
  39.8 0.7 collective-permute-start.5
  40.6 12.4 %collective-permute-start.6 = (bf16[128,128]{1,0:T(8,128)(2,1)S(1)}, bf16[128,128]{1,0:T(8,128)(2,1)S(1)}, u32[]{:S(2)}, u32[]{:S(2)}) collective-permute-start(bf16[128,128]{1,0:T(8,128)(2,1)S(1)} %get-tuple-element.59), channel_id=1, source_target_pairs={{5,6},{2,1},{13,14},{10,9},{21,22},{18,17},{29,30},{26,25},{19,27}... | collective-permute-start | bytes 98312 | tf_op jit(solution)/shard_map/ppermute | solution.py:567
  55.7 2.1 %collective-permute-start.7 = (bf16[128,128]{1,0:T(8,128)(2,1)S(1)}, bf16[128,128]{1,0:T(8,128)(2,1)S(1)}, u32[]{:S(2)}, u32[]{:S(2)}) collective-permute-start(bf16[128,128]{1,0:T(8,128)(2,1)S(1)} %get-tuple-element.63), channel_id=1, source_target_pairs={{6,7},{1,0},{14,15},{9,8},{22,23},{17,16},{30,31},{25,24}} | collective-permute-start | bytes 98312 | tf_op jit(solution)/shard_map/ppermute | solution.py:567
  63.3 13.3 %collective-permute-start.8 = (bf16[16,192,128]{2,1,0:T(8,128)(2,1)S(1)}, bf16[16,192,128]{2,1,0:T(8,128)(2,1)S(1)}, u32[]{:S(2)}, u32[]{:S(2)}) collective-permute-start(bf16[16,192,128]{2,1,0:T(8,128)(2,1)S(1)} %get-tuple-element.69), channel_id=1, source_target_pairs={{1,0},{2,1},{3,2},{4,3},{5,4},{6,5},{7,6},{9,8},{10,9},{11,10},{12... | collective-permute-start | bytes 2359304 | tf_op jit(solution)/shard_map/ppermute | solution.py:587

commit v7 on v6

--- a/solution.py
+++ b/solution.py
@@ -265,17 +265,16 @@
     q1, q2 = penalties(prices_ref)
 
     hop = plan.hop_at(s)
-    if hop is None:
-        out_ref[...] = refs["passed"][...]
-    elif hop < plan.cols - 1:
+    if hop is not None and hop < plan.cols - 1:
 
         @pl.when((col_here == hop) | (col_here == plan.cols - 1 - hop))
         def _():
             west = col_here != hop
             if hop:
-                v = split(arrivals[plan.step(hop - 1, False)][...])
-                other = split(arrivals[plan.step(hop - 1, True)][...])
-                v = [jnp.where(west, b, a) for a, b in zip(v, other)]
+                v = split(arrivals[plan.step(hop - 1)][...])
+                if hop == plan.half:
+                    other = split(refs["crossed"][...])
+                    v = [jnp.where(west, b, a) for a, b in zip(v, other)]
             else:
                 v = [jnp.zeros((SUB, cols), jnp.float32)] * (depth // SUB)
             raw, jumps = (refs[n] for n in plan.paths(hop))
@@ -349,7 +348,7 @@
 
     @pl.when((col_here == 0) | (col_here == plan.cols - 1))
     def _():
-        v = split(arrivals[plan.step(plan.cols - 2, True)][...])
+        v = split(arrivals[plan.step(plan.cols - 2)][...])
         raw, jumps = refs["second"], refs["second_jumps"]
         sweep(v, refs["tiles"], refs["lows"], raw, jumps, rows, col_here == 0, q1, q2)
 
@@ -426,24 +425,20 @@
     def __init__(self, rows, cols):
         self.rows, self.cols = rows, cols
         self.half = cols // 2
-        self.slots = []
+        self.busy, self.slots = [], []
         for c in range(cols):
-            busy = set()
-            if c > 0:
-                busy |= {self.step(c - 1, False), self.step(cols - 1 - c, True)}
-            if c < cols - 1:
-                busy |= {self.step(c, False), self.step(cols - 2 - c, True)}
+            busy = {self.step(c), self.step(cols - 1 - c)}
+            busy |= {self.step(h) for h in (c - 1, cols - 2 - c) if h >= 0}
+            if c in (self.half - 1, self.half):
+                busy.add(self.half)
             free = [s for s in range(cols + 4 + rows) if s not in busy]
+            self.busy.append(busy)
             self.slots.append(free[: rows - 1])
         last = [slots[-1] + 1 for slots in self.slots if slots]
         self.stages = max([cols] + last)
 
-    def step(self, hop, west):
-        if hop < self.half - 1:
-            return hop
-        if hop == self.half - 1:
-            return hop + 1 if west else hop
-        return hop + 1
+    def step(self, hop):
+        return hop if hop < self.half else hop + 1
 
     def hop_at(self, s):
         if s == self.half:
@@ -458,10 +453,10 @@
         pairs = []
         for h in range(self.cols - 1):
             for r in range(self.rows):
-                if self.step(h, False) == s:
+                if self.step(h) == s:
                     pairs.append(((r, h), (r, h + 1)))
-                if self.step(h, True) == s:
-                    pairs.append(((r, self.cols - 1 - h), (r, self.cols - 2 - h)))
+                    if h != self.half - 1:
+                        pairs.append(((r, self.cols - 1 - h), (r, self.cols - 2 - h)))
         for c, slots in enumerate(self.slots):
             if s in slots:
                 j = slots.index(s)
@@ -469,6 +464,12 @@
                     ((j, c), (j + 1, c)),
                     ((self.rows - 1 - j, c), (self.rows - 2 - j, c)),
                 ]
+        return self.numbers(pairs)
+
+    def crossed_route(self):
+        return self.numbers([((r, self.half), (r, self.half - 1)) for r in range(self.rows)])
+
+    def numbers(self, pairs):
         number = lambda place: place[0] * self.cols + place[1]
         return [(number(a), number(b)) for a, b in pairs]
 
@@ -480,7 +481,7 @@
         found = []
         for c, slots in enumerate(self.slots):
             at = slots[-1] + 1
-            while at < self.stages and self.hop_at(at) in (c, self.cols - 1 - c):
+            while at < self.stages and at in self.busy[c]:
                 at += 1
             if at == s:
                 found.append(c)
@@ -555,7 +556,7 @@
         writes += ["base"] if plan.settling(s) else []
         reads = ["tiles", "lows"] + ([] if "turned" in writes else ["turned"])
         reads += [f"arrival{n}" for n in range(s)]
-        reads += ["passed"] if hop is None else []
+        reads += ["crossed"] if hop == plan.half else []
         run(
             functools.partial(stage_kernel, plan, s),
             f"stage{s}",
@@ -565,7 +566,9 @@
             {"held": held, "vsums": vsums},
         )
         buffers[f"arrival{s}"] = lax.ppermute(buffers["sent"], ("row", "col"), plan.route(s))
-        buffers["passed"] = buffers["sent"]
+        if s == plan.half - 1:
+            route = plan.crossed_route()
+            buffers["crossed"] = lax.ppermute(buffers["sent"], ("row", "col"), route)
 
     run(
         functools.partial(final_kernel, plan),

time: 78.6 us -> 74.9 us (0.953)
  waiting for transfers between devices: 34.2 us -> 29.7 us
    ppermute x8, waiting for transfers between devices: 25.7 us -> 21.3 us  [shards(): lax.ppermute(buffers['sent'], ('row', 'col'), plan.route(s))]
  transfers between devices with their start and end apart: 9 -> 10, of which waited for: 7 -> 7; matrix products, arithmetic and copies ran while one was open for 0% -> 0% of each run, Pallas kernels for 0% -> 0%
where the time goes in v7:
time: 74.9 us; the launch traced here: 74.5 us
  waiting for transfers between devices  29.7 us (40%)
  Pallas kernels  23.2 us (31%)
  starting transfers between devices  18.3 us (24%)
  between operations  2.09 us (3%)
  local copies, waits for them, and re-layouts  1.22 us (2%)
    ppermute x8, waiting for transfers between devices, shards(): lax.ppermute(buffers['sent'], ('row', 'col'), plan.route(s))  21.3 us
    pallas_call x9, Pallas kernels, run(): pl.pallas_call(functools.partial(body, names), out_shape=tuple([results[n...  16.3 us
    ppermute x8, starting transfers between devices, shards(): lax.ppermute(buffers['sent'], ('row', 'col'), plan.route(s))  12.8 us
    ppermute x1, waiting for transfers between devices, shards(): lax.ppermute(buffers['packed'], 'col', [(i, i - 1) for i in range(1, plan...  8.45 us
    pallas_call x1, Pallas kernels, shards(): pl.pallas_call(prepare_kernel, out_shape=(jax.ShapeDtypeStruct((cols, dep...  5.16 us
    ppermute x1, starting transfers between devices, shards(): lax.ppermute(buffers['packed'], 'col', [(i, i - 1) for i in range(1, plan...  4.84 us
    pallas_call x1, Pallas kernels, shards(): pl.pallas_call(merge_kernel, out_shape=tile, in_specs=in_vmem(2), out_spe...  1.78 us
  transfers between devices with their start and end apart: 10, of which 7 were waited for; matrix products, arithmetic and copies ran while one was open for 0% of the time, Pallas kernels for 0%

profile of v7, /device:TPU:1, one launch (start us, length us, event | category | flops | bytes accessed | tf_op | source)
XLA Modules:
  0.0 74.5 jit_solution(7940981745603577677)
XLA Ops:
  1.9 1.2 %copy-done = bf16[32,128,128]{2,1,0:T(8,128)(2,1)S(1)} copy-done((bf16[32,128,128]{2,1,0:T(8,128)(2,1)S(1)}, bf16[32,128,128]{2,1,0:T(8,128)(2,1)}, u32[]{:S(2)}) %copy-start) | copy-done | bytes 1048600
  3.1 5.2 %prepare.1 = (f32[128,128,128]{2,1,0:T(8,128)S(1)}, f32[128,8,128]{2,1,0:T(8,128)S(1)}, f32[2,8,128]{2,1,0:T(8,128)S(1)}, bf16[32,128,128]{2,1,0:T(8,128)(2,1)S(1)}) custom-call(bf16[32,128,128]{2,1,0:T(8,128)(2,1)S(1)} %copy-done, s32[1]{0:T(128)S(6)} %copy.37.small_ref, s32[1]{0:T(128)S(6)} %copy.38.large_ref), custom_call_target="tpu_custom_call" | custom-call | tf_op jit(solution)/shard_map/prepare/pallas_call | solution.py:512
  8.3 1.0 %stage0.1 = (bf16[128,128]{1,0:T(8,128)(2,1)S(1)}, f32[32,128,128]{2,1,0:T(8,128)S(1)}, f32[32,8,128]{2,1,0:T(8,128)S(1)}, bf16[32,128,128]{2,1,0:T(8,128)(2,1)S(1)}) custom-call(f32[2,8,128]{2,1,0:T(8,128)S(1)} %get-tuple-element.36.prices_ref, bf16[32,128,128]{2,1,0:T(8,128)(2,1)S(1)} %get-tuple-element.37.costs_ref, ...), custom_call_target="tpu_custom_call" | custom-call | tf_op jit(solution)/shard_map/stage0/pallas_call | solution.py:538
  9.3 1.3 %collective-permute-start = (bf16[128,128]{1,0:T(8,128)(2,1)S(1)}, bf16[128,128]{1,0:T(8,128)(2,1)S(1)}, u32[]{:S(2)}, u32[]{:S(2)}) collective-permute-start(bf16[128,128]{1,0:T(8,128)(2,1)S(1)} %get-tuple-element.40), channel_id=1, source_target_pairs={{0,1},{7,6},{8,9},{15,14},{16,17},{23,22},{24,25},{31,30},{2,10},{... | collective-permute-start | bytes 98312 | tf_op jit(solution)/shard_map/ppermute | solution.py:568
  10.6 2.5 %collective-permute-done.refs_2_.refs_3_.refs_5_ = bf16[128,128]{1,0:T(8,128)(2,1)S(1)} collective-permute-done((bf16[128,128]{1,0:T(8,128)(2,1)S(1)}, bf16[128,128]{1,0:T(8,128)(2,1)S(1)}, u32[]{:S(2)}, u32[]{:S(2)}) %collective-permute-start) | collective-permute-done | bytes 32800 | tf_op jit(solution)/shard_map/ppermute | solution.py:568
  13.1 2.7 %stage1.1 = (bf16[128,128]{1,0:T(8,128)(2,1)S(1)}, f32[32,128,128]{2,1,0:T(8,128)S(1)}, f32[32,8,128]{2,1,0:T(8,128)S(1)}, bf16[32,128,128]{2,1,0:T(8,128)(2,1)S(1)}) custom-call(f32[2,8,128]{2,1,0:T(8,128)S(1)} %get-tuple-element.36.prices_ref, ...), custom_call_target="tpu_custom_call", output_to_operand_aliasing={{1}: (5, {}), {2}: (6, {}), {3}: (7, {})} | custom-call | tf_op jit(solution)/shard_map/stage1/pallas_call | solution.py:538
  15.8 3.1 %collective-permute-start.1 = (bf16[128,128]{1,0:T(8,128)(2,1)S(1)}, bf16[128,128]{1,0:T(8,128)(2,1)S(1)}, u32[]{:S(2)}, u32[]{:S(2)}) collective-permute-start(bf16[128,128]{1,0:T(8,128)(2,1)S(1)} %get-tuple-element.45), channel_id=1, source_target_pairs={{1,2},{6,5},{9,10},{14,13},{17,18},{22,21},{25,26},{30,29},{0,8},{... | collective-permute-start | bytes 98312 | tf_op jit(solution)/shard_map/ppermute | solution.py:568
  18.9 1.0 %collective-permute-done.1.refs_4_.refs_6_ = bf16[128,128]{1,0:T(8,128)(2,1)S(1)} collective-permute-done((bf16[128,128]{1,0:T(8,128)(2,1)S(1)}, bf16[128,128]{1,0:T(8,128)(2,1)S(1)}, u32[]{:S(2)}, u32[]{:S(2)}) %collective-permute-start.1) | collective-permute-done | bytes 32800 | tf_op jit(solution)/shard_map/ppermute | solution.py:568
  19.9 0.7 stage2.1
  20.6 3.2 %collective-permute-start.2 = (bf16[128,128]{1,0:T(8,128)(2,1)S(1)}, bf16[128,128]{1,0:T(8,128)(2,1)S(1)}, u32[]{:S(2)}, u32[]{:S(2)}) collective-permute-start(bf16[128,128]{1,0:T(8,128)(2,1)S(1)} %get-tuple-element.48), channel_id=1, source_target_pairs={{2,3},{5,4},{10,11},{13,12},{18,19},{21,20},{26,27},{29,28},{8,16}... | collective-permute-start | bytes 98312 | tf_op jit(solution)/shard_map/ppermute | solution.py:568
  23.8 1.0 %collective-permute-done.2.refs_5_.refs_7_ = bf16[128,128]{1,0:T(8,128)(2,1)S(1)} collective-permute-done((bf16[128,128]{1,0:T(8,128)(2,1)S(1)}, bf16[128,128]{1,0:T(8,128)(2,1)S(1)}, u32[]{:S(2)}, u32[]{:S(2)}) %collective-permute-start.2) | collective-permute-done | bytes 32800 | tf_op jit(solution)/shard_map/ppermute | solution.py:568
  25.5 0.7 collective-permute-start.5
  26.2 1.3 %collective-permute-start.4 = (bf16[128,128]{1,0:T(8,128)(2,1)S(1)}, bf16[128,128]{1,0:T(8,128)(2,1)S(1)}, u32[]{:S(2)}, u32[]{:S(2)}) collective-permute-start(bf16[128,128]{1,0:T(8,128)(2,1)S(1)} %get-tuple-element.54), channel_id=1, source_target_pairs={{17,25},{9,1},{18,26},{10,2},{21,29},{13,5},{22,30},{14,6}} | collective-permute-start | bytes 98312 | tf_op jit(solution)/shard_map/ppermute | solution.py:568
  27.5 8.6 %collective-permute-done.4.refs_7_.refs_9_ = bf16[128,128]{1,0:T(8,128)(2,1)S(1)} collective-permute-done((bf16[128,128]{1,0:T(8,128)(2,1)S(1)}, bf16[128,128]{1,0:T(8,128)(2,1)S(1)}, u32[]{:S(2)}, u32[]{:S(2)}) %collective-permute-start.4) | collective-permute-done | bytes 32800 | tf_op jit(solution)/shard_map/ppermute | solution.py:568
  36.1 3.8 %stage5.1 = (bf16[128,128]{1,0:T(8,128)(2,1)S(1)}, f32[32,128,128]{2,1,0:T(8,128)S(1)}, f32[32,8,128]{2,1,0:T(8,128)S(1)}, f32[32,128,128]{2,1,0:T(8,128)S(1)}) custom-call(f32[2,8,128]{2,1,0:T(8,128)S(1)} %get-tuple-element.36.prices_ref, bf16[32,128,128]{2,1,0:T(8,128)(2,1)S(1)} %get-tuple-element.37.costs_ref, ...), custom_call_target="tpu_custom_call", output_to_operand_aliasing={{3}: (11, {})} | custom-call | tf_op jit(solution)/shard_map/stage5/pallas_call | solution.py:538
  40.6 1.3 %collective-permute-start.7 = (bf16[128,128]{1,0:T(8,128)(2,1)S(1)}, bf16[128,128]{1,0:T(8,128)(2,1)S(1)}, u32[]{:S(2)}, u32[]{:S(2)}) collective-permute-start(bf16[128,128]{1,0:T(8,128)(2,1)S(1)} %get-tuple-element.59), channel_id=1, source_target_pairs={{5,6},{2,1},{13,14},{10,9},{21,22},{18,17},{29,30},{26,25},{19,27}... | collective-permute-start | bytes 98312 | tf_op jit(solution)/shard_map/ppermute | solution.py:568
  41.9 7.4 %collective-permute-done.7.refs_9_.refs_11_ = bf16[128,128]{1,0:T(8,128)(2,1)S(1)} collective-permute-done((bf16[128,128]{1,0:T(8,128)(2,1)S(1)}, bf16[128,128]{1,0:T(8,128)(2,1)S(1)}, u32[]{:S(2)}, u32[]{:S(2)}) %collective-permute-start.7) | collective-permute-done | bytes 32800 | tf_op jit(solution)/shard_map/ppermute | solution.py:568
  49.2 2.7 %stage7.1 = (bf16[128,128]{1,0:T(8,128)(2,1)S(1)}, f32[32,128,128]{2,1,0:T(8,128)S(1)}, f32[32,8,128]{2,1,0:T(8,128)S(1)}, f32[32,128,128]{2,1,0:T(8,128)S(1)}) custom-call(f32[2,8,128]{2,1,0:T(8,128)S(1)} %get-tuple-element.36.prices_ref, ...), custom_call_target="tpu_custom_call", output_to_operand_aliasing={{1}: (12, {}), {2}: (13, {}), {3}: (14, {})} | custom-call | tf_op jit(solution)/shard_map/stage7/pallas_call | solution.py:538
  51.9 1.3 %collective-permute-start.8 = (bf16[128,128]{1,0:T(8,128)(2,1)S(1)}, bf16[128,128]{1,0:T(8,128)(2,1)S(1)}, u32[]{:S(2)}, u32[]{:S(2)}) collective-permute-start(bf16[128,128]{1,0:T(8,128)(2,1)S(1)} %get-tuple-element.63), channel_id=1, source_target_pairs={{6,7},{1,0},{14,15},{9,8},{22,23},{17,16},{30,31},{25,24}} | collective-permute-start | bytes 98312 | tf_op jit(solution)/shard_map/ppermute | solution.py:568
  53.2 0.8 %collective-permute-done.8.refs_12_ = bf16[128,128]{1,0:T(8,128)(2,1)S(1)} collective-permute-done((bf16[128,128]{1,0:T(8,128)(2,1)S(1)}, bf16[128,128]{1,0:T(8,128)(2,1)S(1)}, u32[]{:S(2)}, u32[]{:S(2)}) %collective-permute-start.8) | collective-permute-done | bytes 32800 | tf_op jit(solution)/shard_map/ppermute | solution.py:568
  54.1 5.4 %final.1 = (bf16[32,128,128]{2,1,0:T(8,128)(2,1)}, bf16[32,128,128]{2,1,0:T(8,128)(2,1)S(1)}, bf16[16,192,128]{2,1,0:T(8,128)(2,1)S(1)}, f32[32,128,128]{2,1,0:T...) custom-call(f32[2,8,128]{2,1,0:T(8,128)S(1)} %get-tuple-element.36.p, ...), custom_call_target="tpu_custom_call", output_to_operand_aliasing={{3}: (15, {}), {4}: (16, {}), {5}: (17, {})} | custom-call | tf_op jit(solution)/shard_map/final/pallas_call | solution.py:538
  59.5 4.8 %collective-permute-start.9 = (bf16[16,192,128]{2,1,0:T(8,128)(2,1)S(1)}, bf16[16,192,128]{2,1,0:T(8,128)(2,1)S(1)}, u32[]{:S(2)}, u32[]{:S(2)}) collective-permute-start(bf16[16,192,128]{2,1,0:T(8,128)(2,1)S(1)} %get-tuple-element.69), channel_id=1, source_target_pairs={{1,0},{2,1},{3,2},{4,3},{5,4},{6,5},{7,6},{9,8},{10,9},{11,10},{12... | collective-permute-start | bytes 2359304 | tf_op jit(solution)/shard_map/ppermute | solution.py:590
  64.3 8.5 %collective-permute-done.9.packed_ref = bf16[16,192,128]{2,1,0:T(8,128)(2,1)S(1)} collective-permute-done((bf16[16,192,128]{2,1,0:T(8,128)(2,1)S(1)}, bf16[16,192,128]{2,1,0:T(8,128)(2,1)S(1)}, u32[]{:S(2)}, u32[]{:S(2)}) %collective-permute-start.9) | collective-permute-done | bytes 786464 | tf_op jit(solution)/shard_map/ppermute | solution.py:590
  72.8 1.8 %merge.1 = bf16[32,128,128]{2,1,0:T(8,128)(2,1)} custom-call(bf16[32,128,128]{2,1,0:T(8,128)(2,1)S(1)} %get-tuple-element.68.skewed_ref, bf16[16,192,128]{2,1,0:T(8,128)(2,1)S(1)} %collective-permute-done.9.packed_ref), custom_call_target="tpu_custom_call" | custom-call | tf_op jit(solution)/shard_map/merge/pallas_call | solution.py:591
  (9 shorter events, 1.4 us)
Async XLA Ops:
  1.9 1.2 %copy-start = (bf16[32,128,128]{2,1,0:T(8,128)(2,1)S(1)}, bf16[32,128,128]{2,1,0:T(8,128)(2,1)}, u32[]{:S(2)}) copy-start(bf16[32,128,128]{2,1,0:T(8,128)(2,1)} %costs_ref.1) | copy-start | bytes 3145732
  9.3 3.8 %collective-permute-start = (bf16[128,128]{1,0:T(8,128)(2,1)S(1)}, bf16[128,128]{1,0:T(8,128)(2,1)S(1)}, u32[]{:S(2)}, u32[]{:S(2)}) collective-permute-start(bf16[128,128]{1,0:T(8,128)(2,1)S(1)} %get-tuple-element.40), channel_id=1, source_target_pairs={{0,1},{7,6},{8,9},{15,14},{16,17},{23,22},{24,25},{31,30},{2,10},{... | collective-permute-start | bytes 98312 | tf_op jit(solution)/shard_map/ppermute | solution.py:568
  15.8 4.1 %collective-permute-start.1 = (bf16[128,128]{1,0:T(8,128)(2,1)S(1)}, bf16[128,128]{1,0:T(8,128)(2,1)S(1)}, u32[]{:S(2)}, u32[]{:S(2)}) collective-permute-start(bf16[128,128]{1,0:T(8,128)(2,1)S(1)} %get-tuple-element.45), channel_id=1, source_target_pairs={{1,2},{6,5},{9,10},{14,13},{17,18},{22,21},{25,26},{30,29},{0,8},{... | collective-permute-start | bytes 98312 | tf_op jit(solution)/shard_map/ppermute | solution.py:568
  20.6 4.3 %collective-permute-start.2 = (bf16[128,128]{1,0:T(8,128)(2,1)S(1)}, bf16[128,128]{1,0:T(8,128)(2,1)S(1)}, u32[]{:S(2)}, u32[]{:S(2)}) collective-permute-start(bf16[128,128]{1,0:T(8,128)(2,1)S(1)} %get-tuple-element.48), channel_id=1, source_target_pairs={{2,3},{5,4},{10,11},{13,12},{18,19},{21,20},{26,27},{29,28},{8,16}... | collective-permute-start | bytes 98312 | tf_op jit(solution)/shard_map/ppermute | solution.py:568
  24.8 1.3 %collective-permute-start.3 = (bf16[128,128]{1,0:T(8,128)(2,1)S(1)}, bf16[128,128]{1,0:T(8,128)(2,1)S(1)}, u32[]{:S(2)}, u32[]{:S(2)}) collective-permute-start(bf16[128,128]{1,0:T(8,128)(2,1)S(1)} %get-tuple-element.53), channel_id=1, source_target_pairs={{3,4},{11,12},{19,20},{27,28},{16,24},{8,0},{9,17},{17,9},{10,18},... | collective-permute-start | bytes 98312 | tf_op jit(solution)/shard_map/ppermute | solution.py:568
  25.5 2.0 %collective-permute-start.5 = (bf16[128,128]{1,0:T(8,128)(2,1)S(1)}, bf16[128,128]{1,0:T(8,128)(2,1)S(1)}, u32[]{:S(2)}, u32[]{:S(2)}) collective-permute-start(bf16[128,128]{1,0:T(8,128)(2,1)S(1)} %get-tuple-element.53), channel_id=1, source_target_pairs={{4,3},{12,11},{20,19},{28,27}} | collective-permute-start | bytes 98312 | tf_op jit(solution)/shard_map/ppermute | solution.py:571
  26.2 9.9 %collective-permute-start.4 = (bf16[128,128]{1,0:T(8,128)(2,1)S(1)}, bf16[128,128]{1,0:T(8,128)(2,1)S(1)}, u32[]{:S(2)}, u32[]{:S(2)}) collective-permute-start(bf16[128,128]{1,0:T(8,128)(2,1)S(1)} %get-tuple-element.54), channel_id=1, source_target_pairs={{17,25},{9,1},{18,26},{10,2},{21,29},{13,5},{22,30},{14,6}} | collective-permute-start | bytes 98312 | tf_op jit(solution)/shard_map/ppermute | solution.py:568
  39.8 0.7 collective-permute-start.6
  40.6 8.7 %collective-permute-start.7 = (bf16[128,128]{1,0:T(8,128)(2,1)S(1)}, bf16[128,128]{1,0:T(8,128)(2,1)S(1)}, u32[]{:S(2)}, u32[]{:S(2)}) collective-permute-start(bf16[128,128]{1,0:T(8,128)(2,1)S(1)} %get-tuple-element.59), channel_id=1, source_target_pairs={{5,6},{2,1},{13,14},{10,9},{21,22},{18,17},{29,30},{26,25},{19,27}... | collective-permute-start | bytes 98312 | tf_op jit(solution)/shard_map/ppermute | solution.py:568
  51.9 2.1 %collective-permute-start.8 = (bf16[128,128]{1,0:T(8,128)(2,1)S(1)}, bf16[128,128]{1,0:T(8,128)(2,1)S(1)}, u32[]{:S(2)}, u32[]{:S(2)}) collective-permute-start(bf16[128,128]{1,0:T(8,128)(2,1)S(1)} %get-tuple-element.63), channel_id=1, source_target_pairs={{6,7},{1,0},{14,15},{9,8},{22,23},{17,16},{30,31},{25,24}} | collective-permute-start | bytes 98312 | tf_op jit(solution)/shard_map/ppermute | solution.py:568
  59.5 13.3 %collective-permute-start.9 = (bf16[16,192,128]{2,1,0:T(8,128)(2,1)S(1)}, bf16[16,192,128]{2,1,0:T(8,128)(2,1)S(1)}, u32[]{:S(2)}, u32[]{:S(2)}) collective-permute-start(bf16[16,192,128]{2,1,0:T(8,128)(2,1)S(1)} %get-tuple-element.69), channel_id=1, source_target_pairs={{1,0},{2,1},{3,2},{4,3},{5,4},{6,5},{7,6},{9,8},{10,9},{11,10},{12... | collective-permute-start | bytes 2359304 | tf_op jit(solution)/shard_map/ppermute | solution.py:590

commit v8 on v7

--- a/solution.py
+++ b/solution.py
@@ -391,7 +391,7 @@
         refs["packed"][y] = join(corner + turned[0][middle:] + turned[1][middle:])
         return carry
 
-    lax.fori_loop(0, half, finish, 0, unroll=2)
+    lax.fori_loop(0, half, finish, 0, unroll=4)
 
 
 def merge_kernel(skewed_ref, packed_ref, right_ref):
@@ -418,7 +418,7 @@
             )
         return carry
 
-    lax.fori_loop(0, half, body, 0, unroll=2)
+    lax.fori_loop(0, half, body, 0, unroll=4)
 
 
 class Plan:

time: 74.9 us -> 74.6 us (level)
  no operation moved by 1% of the time
where the time goes in v8:
time: 74.6 us; the launch traced here: 74.2 us
  waiting for transfers between devices  29.7 us (40%)
  Pallas kernels  22.9 us (31%)
  starting transfers between devices  18.3 us (25%)
  between operations  2.09 us (3%)
  local copies, waits for them, and re-layouts  1.22 us (2%)
    ppermute x8, waiting for transfers between devices, shards(): lax.ppermute(buffers['sent'], ('row', 'col'), plan.route(s))  21.3 us
    pallas_call x9, Pallas kernels, run(): pl.pallas_call(functools.partial(body, names), out_shape=tuple([results[n...  16.3 us
    ppermute x8, starting transfers between devices, shards(): lax.ppermute(buffers['sent'], ('row', 'col'), plan.route(s))  12.8 us
    ppermute x1, waiting for transfers between devices, shards(): lax.ppermute(buffers['packed'], 'col', [(i, i - 1) for i in range(1, plan...  8.45 us
    pallas_call x1, Pallas kernels, shards(): pl.pallas_call(prepare_kernel, out_shape=(jax.ShapeDtypeStruct((cols, dep...  5.16 us
    ppermute x1, starting transfers between devices, shards(): lax.ppermute(buffers['packed'], 'col', [(i, i - 1) for i in range(1, plan...  4.84 us
  transfers between devices with their start and end apart: 10, of which 7 were waited for; matrix products, arithmetic and copies ran while one was open for 0% of the time, Pallas kernels for 0%

profile of v8, /device:TPU:1, one launch (start us, length us, event | category | flops | bytes accessed | tf_op | source)
XLA Modules:
  0.0 74.2 jit_solution(12710173457021122614)
XLA Ops:
  1.9 1.2 %copy-done = bf16[32,128,128]{2,1,0:T(8,128)(2,1)S(1)} copy-done((bf16[32,128,128]{2,1,0:T(8,128)(2,1)S(1)}, bf16[32,128,128]{2,1,0:T(8,128)(2,1)}, u32[]{:S(2)}) %copy-start) | copy-done | bytes 1048600
  3.1 5.2 %prepare.1 = (f32[128,128,128]{2,1,0:T(8,128)S(1)}, f32[128,8,128]{2,1,0:T(8,128)S(1)}, f32[2,8,128]{2,1,0:T(8,128)S(1)}, bf16[32,128,128]{2,1,0:T(8,128)(2,1)S(1)}) custom-call(bf16[32,128,128]{2,1,0:T(8,128)(2,1)S(1)} %copy-done, s32[1]{0:T(128)S(6)} %copy.37.small_ref, s32[1]{0:T(128)S(6)} %copy.38.large_ref), custom_call_target="tpu_custom_call" | custom-call | tf_op jit(solution)/shard_map/prepare/pallas_call | solution.py:512
  8.3 1.0 %stage0.1 = (bf16[128,128]{1,0:T(8,128)(2,1)S(1)}, f32[32,128,128]{2,1,0:T(8,128)S(1)}, f32[32,8,128]{2,1,0:T(8,128)S(1)}, bf16[32,128,128]{2,1,0:T(8,128)(2,1)S(1)}) custom-call(f32[2,8,128]{2,1,0:T(8,128)S(1)} %get-tuple-element.36.prices_ref, bf16[32,128,128]{2,1,0:T(8,128)(2,1)S(1)} %get-tuple-element.37.costs_ref, ...), custom_call_target="tpu_custom_call" | custom-call | tf_op jit(solution)/shard_map/stage0/pallas_call | solution.py:538
  9.3 1.3 %collective-permute-start = (bf16[128,128]{1,0:T(8,128)(2,1)S(1)}, bf16[128,128]{1,0:T(8,128)(2,1)S(1)}, u32[]{:S(2)}, u32[]{:S(2)}) collective-permute-start(bf16[128,128]{1,0:T(8,128)(2,1)S(1)} %get-tuple-element.40), channel_id=1, source_target_pairs={{0,1},{7,6},{8,9},{15,14},{16,17},{23,22},{24,25},{31,30},{2,10},{... | collective-permute-start | bytes 98312 | tf_op jit(solution)/shard_map/ppermute | solution.py:568
  10.6 2.5 %collective-permute-done.refs_2_.refs_3_.refs_5_ = bf16[128,128]{1,0:T(8,128)(2,1)S(1)} collective-permute-done((bf16[128,128]{1,0:T(8,128)(2,1)S(1)}, bf16[128,128]{1,0:T(8,128)(2,1)S(1)}, u32[]{:S(2)}, u32[]{:S(2)}) %collective-permute-start) | collective-permute-done | bytes 32800 | tf_op jit(solution)/shard_map/ppermute | solution.py:568
  13.1 2.7 %stage1.1 = (bf16[128,128]{1,0:T(8,128)(2,1)S(1)}, f32[32,128,128]{2,1,0:T(8,128)S(1)}, f32[32,8,128]{2,1,0:T(8,128)S(1)}, bf16[32,128,128]{2,1,0:T(8,128)(2,1)S(1)}) custom-call(f32[2,8,128]{2,1,0:T(8,128)S(1)} %get-tuple-element.36.prices_ref, ...), custom_call_target="tpu_custom_call", output_to_operand_aliasing={{1}: (5, {}), {2}: (6, {}), {3}: (7, {})} | custom-call | tf_op jit(solution)/shard_map/stage1/pallas_call | solution.py:538
  15.8 3.1 %collective-permute-start.1 = (bf16[128,128]{1,0:T(8,128)(2,1)S(1)}, bf16[128,128]{1,0:T(8,128)(2,1)S(1)}, u32[]{:S(2)}, u32[]{:S(2)}) collective-permute-start(bf16[128,128]{1,0:T(8,128)(2,1)S(1)} %get-tuple-element.45), channel_id=1, source_target_pairs={{1,2},{6,5},{9,10},{14,13},{17,18},{22,21},{25,26},{30,29},{0,8},{... | collective-permute-start | bytes 98312 | tf_op jit(solution)/shard_map/ppermute | solution.py:568
  18.9 1.0 %collective-permute-done.1.refs_4_.refs_6_ = bf16[128,128]{1,0:T(8,128)(2,1)S(1)} collective-permute-done((bf16[128,128]{1,0:T(8,128)(2,1)S(1)}, bf16[128,128]{1,0:T(8,128)(2,1)S(1)}, u32[]{:S(2)}, u32[]{:S(2)}) %collective-permute-start.1) | collective-permute-done | bytes 32800 | tf_op jit(solution)/shard_map/ppermute | solution.py:568
  19.9 0.7 stage2.1
  20.6 3.2 %collective-permute-start.2 = (bf16[128,128]{1,0:T(8,128)(2,1)S(1)}, bf16[128,128]{1,0:T(8,128)(2,1)S(1)}, u32[]{:S(2)}, u32[]{:S(2)}) collective-permute-start(bf16[128,128]{1,0:T(8,128)(2,1)S(1)} %get-tuple-element.48), channel_id=1, source_target_pairs={{2,3},{5,4},{10,11},{13,12},{18,19},{21,20},{26,27},{29,28},{8,16}... | collective-permute-start | bytes 98312 | tf_op jit(solution)/shard_map/ppermute | solution.py:568
  23.8 1.0 %collective-permute-done.2.refs_5_.refs_7_ = bf16[128,128]{1,0:T(8,128)(2,1)S(1)} collective-permute-done((bf16[128,128]{1,0:T(8,128)(2,1)S(1)}, bf16[128,128]{1,0:T(8,128)(2,1)S(1)}, u32[]{:S(2)}, u32[]{:S(2)}) %collective-permute-start.2) | collective-permute-done | bytes 32800 | tf_op jit(solution)/shard_map/ppermute | solution.py:568
  25.5 0.7 collective-permute-start.5
  26.2 1.3 %collective-permute-start.4 = (bf16[128,128]{1,0:T(8,128)(2,1)S(1)}, bf16[128,128]{1,0:T(8,128)(2,1)S(1)}, u32[]{:S(2)}, u32[]{:S(2)}) collective-permute-start(bf16[128,128]{1,0:T(8,128)(2,1)S(1)} %get-tuple-element.54), channel_id=1, source_target_pairs={{17,25},{9,1},{18,26},{10,2},{21,29},{13,5},{22,30},{14,6}} | collective-permute-start | bytes 98312 | tf_op jit(solution)/shard_map/ppermute | solution.py:568
  27.5 8.6 %collective-permute-done.4.refs_7_.refs_9_ = bf16[128,128]{1,0:T(8,128)(2,1)S(1)} collective-permute-done((bf16[128,128]{1,0:T(8,128)(2,1)S(1)}, bf16[128,128]{1,0:T(8,128)(2,1)S(1)}, u32[]{:S(2)}, u32[]{:S(2)}) %collective-permute-start.4) | collective-permute-done | bytes 32800 | tf_op jit(solution)/shard_map/ppermute | solution.py:568
  36.1 3.8 %stage5.1 = (bf16[128,128]{1,0:T(8,128)(2,1)S(1)}, f32[32,128,128]{2,1,0:T(8,128)S(1)}, f32[32,8,128]{2,1,0:T(8,128)S(1)}, f32[32,128,128]{2,1,0:T(8,128)S(1)}) custom-call(f32[2,8,128]{2,1,0:T(8,128)S(1)} %get-tuple-element.36.prices_ref, bf16[32,128,128]{2,1,0:T(8,128)(2,1)S(1)} %get-tuple-element.37.costs_ref, ...), custom_call_target="tpu_custom_call", output_to_operand_aliasing={{3}: (11, {})} | custom-call | tf_op jit(solution)/shard_map/stage5/pallas_call | solution.py:538
  40.6 1.3 %collective-permute-start.7 = (bf16[128,128]{1,0:T(8,128)(2,1)S(1)}, bf16[128,128]{1,0:T(8,128)(2,1)S(1)}, u32[]{:S(2)}, u32[]{:S(2)}) collective-permute-start(bf16[128,128]{1,0:T(8,128)(2,1)S(1)} %get-tuple-element.59), channel_id=1, source_target_pairs={{5,6},{2,1},{13,14},{10,9},{21,22},{18,17},{29,30},{26,25},{19,27}... | collective-permute-start | bytes 98312 | tf_op jit(solution)/shard_map/ppermute | solution.py:568
  41.9 7.4 %collective-permute-done.7.refs_9_.refs_11_ = bf16[128,128]{1,0:T(8,128)(2,1)S(1)} collective-permute-done((bf16[128,128]{1,0:T(8,128)(2,1)S(1)}, bf16[128,128]{1,0:T(8,128)(2,1)S(1)}, u32[]{:S(2)}, u32[]{:S(2)}) %collective-permute-start.7) | collective-permute-done | bytes 32800 | tf_op jit(solution)/shard_map/ppermute | solution.py:568
  49.2 2.7 %stage7.1 = (bf16[128,128]{1,0:T(8,128)(2,1)S(1)}, f32[32,128,128]{2,1,0:T(8,128)S(1)}, f32[32,8,128]{2,1,0:T(8,128)S(1)}, f32[32,128,128]{2,1,0:T(8,128)S(1)}) custom-call(f32[2,8,128]{2,1,0:T(8,128)S(1)} %get-tuple-element.36.prices_ref, ...), custom_call_target="tpu_custom_call", output_to_operand_aliasing={{1}: (12, {}), {2}: (13, {}), {3}: (14, {})} | custom-call | tf_op jit(solution)/shard_map/stage7/pallas_call | solution.py:538
  51.9 1.3 %collective-permute-start.8 = (bf16[128,128]{1,0:T(8,128)(2,1)S(1)}, bf16[128,128]{1,0:T(8,128)(2,1)S(1)}, u32[]{:S(2)}, u32[]{:S(2)}) collective-permute-start(bf16[128,128]{1,0:T(8,128)(2,1)S(1)} %get-tuple-element.63), channel_id=1, source_target_pairs={{6,7},{1,0},{14,15},{9,8},{22,23},{17,16},{30,31},{25,24}} | collective-permute-start | bytes 98312 | tf_op jit(solution)/shard_map/ppermute | solution.py:568
  53.2 0.8 %collective-permute-done.8.refs_12_ = bf16[128,128]{1,0:T(8,128)(2,1)S(1)} collective-permute-done((bf16[128,128]{1,0:T(8,128)(2,1)S(1)}, bf16[128,128]{1,0:T(8,128)(2,1)S(1)}, u32[]{:S(2)}, u32[]{:S(2)}) %collective-permute-start.8) | collective-permute-done | bytes 32800 | tf_op jit(solution)/shard_map/ppermute | solution.py:568
  54.1 5.4 %final.1 = (bf16[32,128,128]{2,1,0:T(8,128)(2,1)}, bf16[32,128,128]{2,1,0:T(8,128)(2,1)S(1)}, bf16[16,192,128]{2,1,0:T(8,128)(2,1)S(1)}, f32[32,128,128]{2,1,0:T...) custom-call(f32[2,8,128]{2,1,0:T(8,128)S(1)} %get-tuple-element.36.p, ...), custom_call_target="tpu_custom_call", output_to_operand_aliasing={{3}: (15, {}), {4}: (16, {}), {5}: (17, {})} | custom-call | tf_op jit(solution)/shard_map/final/pallas_call | solution.py:538
  59.5 4.8 %collective-permute-start.9 = (bf16[16,192,128]{2,1,0:T(8,128)(2,1)S(1)}, bf16[16,192,128]{2,1,0:T(8,128)(2,1)S(1)}, u32[]{:S(2)}, u32[]{:S(2)}) collective-permute-start(bf16[16,192,128]{2,1,0:T(8,128)(2,1)S(1)} %get-tuple-element.69), channel_id=1, source_target_pairs={{1,0},{2,1},{3,2},{4,3},{5,4},{6,5},{7,6},{9,8},{10,9},{11,10},{12... | collective-permute-start | bytes 2359304 | tf_op jit(solution)/shard_map/ppermute | solution.py:590
  64.3 8.5 %collective-permute-done.9.packed_ref = bf16[16,192,128]{2,1,0:T(8,128)(2,1)S(1)} collective-permute-done((bf16[16,192,128]{2,1,0:T(8,128)(2,1)S(1)}, bf16[16,192,128]{2,1,0:T(8,128)(2,1)S(1)}, u32[]{:S(2)}, u32[]{:S(2)}) %collective-permute-start.9) | collective-permute-done | bytes 786464 | tf_op jit(solution)/shard_map/ppermute | solution.py:590
  72.8 1.5 %merge.1 = bf16[32,128,128]{2,1,0:T(8,128)(2,1)} custom-call(bf16[32,128,128]{2,1,0:T(8,128)(2,1)S(1)} %get-tuple-element.68.skewed_ref, bf16[16,192,128]{2,1,0:T(8,128)(2,1)S(1)} %collective-permute-done.9.packed_ref), custom_call_target="tpu_custom_call" | custom-call | tf_op jit(solution)/shard_map/merge/pallas_call | solution.py:591
  (9 shorter events, 1.4 us)
Async XLA Ops:
  1.9 1.2 %copy-start = (bf16[32,128,128]{2,1,0:T(8,128)(2,1)S(1)}, bf16[32,128,128]{2,1,0:T(8,128)(2,1)}, u32[]{:S(2)}) copy-start(bf16[32,128,128]{2,1,0:T(8,128)(2,1)} %costs_ref.1) | copy-start | bytes 3145732
  9.3 3.8 %collective-permute-start = (bf16[128,128]{1,0:T(8,128)(2,1)S(1)}, bf16[128,128]{1,0:T(8,128)(2,1)S(1)}, u32[]{:S(2)}, u32[]{:S(2)}) collective-permute-start(bf16[128,128]{1,0:T(8,128)(2,1)S(1)} %get-tuple-element.40), channel_id=1, source_target_pairs={{0,1},{7,6},{8,9},{15,14},{16,17},{23,22},{24,25},{31,30},{2,10},{... | collective-permute-start | bytes 98312 | tf_op jit(solution)/shard_map/ppermute | solution.py:568
  15.8 4.1 %collective-permute-start.1 = (bf16[128,128]{1,0:T(8,128)(2,1)S(1)}, bf16[128,128]{1,0:T(8,128)(2,1)S(1)}, u32[]{:S(2)}, u32[]{:S(2)}) collective-permute-start(bf16[128,128]{1,0:T(8,128)(2,1)S(1)} %get-tuple-element.45), channel_id=1, source_target_pairs={{1,2},{6,5},{9,10},{14,13},{17,18},{22,21},{25,26},{30,29},{0,8},{... | collective-permute-start | bytes 98312 | tf_op jit(solution)/shard_map/ppermute | solution.py:568
  20.6 4.3 %collective-permute-start.2 = (bf16[128,128]{1,0:T(8,128)(2,1)S(1)}, bf16[128,128]{1,0:T(8,128)(2,1)S(1)}, u32[]{:S(2)}, u32[]{:S(2)}) collective-permute-start(bf16[128,128]{1,0:T(8,128)(2,1)S(1)} %get-tuple-element.48), channel_id=1, source_target_pairs={{2,3},{5,4},{10,11},{13,12},{18,19},{21,20},{26,27},{29,28},{8,16}... | collective-permute-start | bytes 98312 | tf_op jit(solution)/shard_map/ppermute | solution.py:568
  24.8 1.3 %collective-permute-start.3 = (bf16[128,128]{1,0:T(8,128)(2,1)S(1)}, bf16[128,128]{1,0:T(8,128)(2,1)S(1)}, u32[]{:S(2)}, u32[]{:S(2)}) collective-permute-start(bf16[128,128]{1,0:T(8,128)(2,1)S(1)} %get-tuple-element.53), channel_id=1, source_target_pairs={{3,4},{11,12},{19,20},{27,28},{16,24},{8,0},{9,17},{17,9},{10,18},... | collective-permute-start | bytes 98312 | tf_op jit(solution)/shard_map/ppermute | solution.py:568
  25.5 2.0 %collective-permute-start.5 = (bf16[128,128]{1,0:T(8,128)(2,1)S(1)}, bf16[128,128]{1,0:T(8,128)(2,1)S(1)}, u32[]{:S(2)}, u32[]{:S(2)}) collective-permute-start(bf16[128,128]{1,0:T(8,128)(2,1)S(1)} %get-tuple-element.53), channel_id=1, source_target_pairs={{4,3},{12,11},{20,19},{28,27}} | collective-permute-start | bytes 98312 | tf_op jit(solution)/shard_map/ppermute | solution.py:571
  26.2 9.9 %collective-permute-start.4 = (bf16[128,128]{1,0:T(8,128)(2,1)S(1)}, bf16[128,128]{1,0:T(8,128)(2,1)S(1)}, u32[]{:S(2)}, u32[]{:S(2)}) collective-permute-start(bf16[128,128]{1,0:T(8,128)(2,1)S(1)} %get-tuple-element.54), channel_id=1, source_target_pairs={{17,25},{9,1},{18,26},{10,2},{21,29},{13,5},{22,30},{14,6}} | collective-permute-start | bytes 98312 | tf_op jit(solution)/shard_map/ppermute | solution.py:568
  39.8 0.7 collective-permute-start.6
  40.6 8.7 %collective-permute-start.7 = (bf16[128,128]{1,0:T(8,128)(2,1)S(1)}, bf16[128,128]{1,0:T(8,128)(2,1)S(1)}, u32[]{:S(2)}, u32[]{:S(2)}) collective-permute-start(bf16[128,128]{1,0:T(8,128)(2,1)S(1)} %get-tuple-element.59), channel_id=1, source_target_pairs={{5,6},{2,1},{13,14},{10,9},{21,22},{18,17},{29,30},{26,25},{19,27}... | collective-permute-start | bytes 98312 | tf_op jit(solution)/shard_map/ppermute | solution.py:568
  51.9 2.1 %collective-permute-start.8 = (bf16[128,128]{1,0:T(8,128)(2,1)S(1)}, bf16[128,128]{1,0:T(8,128)(2,1)S(1)}, u32[]{:S(2)}, u32[]{:S(2)}) collective-permute-start(bf16[128,128]{1,0:T(8,128)(2,1)S(1)} %get-tuple-element.63), channel_id=1, source_target_pairs={{6,7},{1,0},{14,15},{9,8},{22,23},{17,16},{30,31},{25,24}} | collective-permute-start | bytes 98312 | tf_op jit(solution)/shard_map/ppermute | solution.py:568
  59.5 13.3 %collective-permute-start.9 = (bf16[16,192,128]{2,1,0:T(8,128)(2,1)S(1)}, bf16[16,192,128]{2,1,0:T(8,128)(2,1)S(1)}, u32[]{:S(2)}, u32[]{:S(2)}) collective-permute-start(bf16[16,192,128]{2,1,0:T(8,128)(2,1)S(1)} %get-tuple-element.69), channel_id=1, source_target_pairs={{1,0},{2,1},{3,2},{4,3},{5,4},{6,5},{7,6},{9,8},{10,9},{11,10},{12... | collective-permute-start | bytes 2359304 | tf_op jit(solution)/shard_map/ppermute | solution.py:590

commit v9 on v8

--- a/solution.py
+++ b/solution.py
@@ -102,7 +102,7 @@
             mixed_ref[2 * i + n] = flat.astype(jnp.bfloat16)
         return carry
 
-    lax.fori_loop(0, cols // SUB // 2, mixed, 0, unroll=2)
+    lax.fori_loop(0, cols // SUB // 2, mixed, 0, unroll=4)
     for j in range(0, SUB, 2):
         pick = spread(rows, cols, j)
 
@@ -114,7 +114,7 @@
                 low_ref[i * SUB + j + n] = fold_min(split(part))
             return carry
 
-        lax.fori_loop(0, cols // SUB, body, 0, unroll=4)
+        lax.fori_loop(0, cols // SUB, body, 0, unroll=8)
 
     for n, fetch in enumerate(fetches):
         fetch.wait()

time: 74.6 us -> 72.9 us (0.977)
  Pallas kernels: 22.9 us -> 21.2 us
    pallas_call x1, Pallas kernels: 5.16 us -> 3.5 us  [shards(): pl.pallas_call(prepare_kernel, out_shape=(jax.ShapeDtypeStruct((cols, dep...]
where the time goes in v9:
time: 72.9 us; the launch traced here: 72.6 us
  waiting for transfers between devices  29.7 us (41%)
  Pallas kernels  21.2 us (29%)
  starting transfers between devices  18.3 us (25%)
  between operations  2.09 us (3%)
  local copies, waits for them, and re-layouts  1.22 us (2%)
    ppermute x8, waiting for transfers between devices, shards(): lax.ppermute(buffers['sent'], ('row', 'col'), plan.route(s))  21.3 us
    pallas_call x9, Pallas kernels, run(): pl.pallas_call(functools.partial(body, names), out_shape=tuple([results[n...  16.3 us
    ppermute x8, starting transfers between devices, shards(): lax.ppermute(buffers['sent'], ('row', 'col'), plan.route(s))  12.8 us
    ppermute x1, waiting for transfers between devices, shards(): lax.ppermute(buffers['packed'], 'col', [(i, i - 1) for i in range(1, plan...  8.45 us
    ppermute x1, starting transfers between devices, shards(): lax.ppermute(buffers['packed'], 'col', [(i, i - 1) for i in range(1, plan...  4.84 us
    pallas_call x1, Pallas kernels, shards(): pl.pallas_call(prepare_kernel, out_shape=(jax.ShapeDtypeStruct((cols, dep...  3.5 us
    pallas_call x1, Pallas kernels, shards(): pl.pallas_call(merge_kernel, out_shape=tile, in_specs=in_vmem(2), out_spe...  1.47 us
  transfers between devices with their start and end apart: 10, of which 7 were waited for; matrix products, arithmetic and copies ran while one was open for 0% of the time, Pallas kernels for 0%

profile of v9, /device:TPU:1, one launch (start us, length us, event | category | flops | bytes accessed | tf_op | source)
XLA Modules:
  0.0 72.6 jit_solution(3459738764568356403)
XLA Ops:
  1.9 1.2 %copy-done = bf16[32,128,128]{2,1,0:T(8,128)(2,1)S(1)} copy-done((bf16[32,128,128]{2,1,0:T(8,128)(2,1)S(1)}, bf16[32,128,128]{2,1,0:T(8,128)(2,1)}, u32[]{:S(2)}) %copy-start) | copy-done | bytes 1048600
  3.1 3.5 %prepare.1 = (f32[128,128,128]{2,1,0:T(8,128)S(1)}, f32[128,8,128]{2,1,0:T(8,128)S(1)}, f32[2,8,128]{2,1,0:T(8,128)S(1)}, bf16[32,128,128]{2,1,0:T(8,128)(2,1)S(1)}) custom-call(bf16[32,128,128]{2,1,0:T(8,128)(2,1)S(1)} %copy-done, s32[1]{0:T(128)S(6)} %copy.37.small_ref, s32[1]{0:T(128)S(6)} %copy.38.large_ref), custom_call_target="tpu_custom_call" | custom-call | tf_op jit(solution)/shard_map/prepare/pallas_call | solution.py:512
  6.7 1.0 %stage0.1 = (bf16[128,128]{1,0:T(8,128)(2,1)S(1)}, f32[32,128,128]{2,1,0:T(8,128)S(1)}, f32[32,8,128]{2,1,0:T(8,128)S(1)}, bf16[32,128,128]{2,1,0:T(8,128)(2,1)S(1)}) custom-call(f32[2,8,128]{2,1,0:T(8,128)S(1)} %get-tuple-element.36.prices_ref, bf16[32,128,128]{2,1,0:T(8,128)(2,1)S(1)} %get-tuple-element.37.costs_ref, ...), custom_call_target="tpu_custom_call" | custom-call | tf_op jit(solution)/shard_map/stage0/pallas_call | solution.py:538
  7.6 1.3 %collective-permute-start = (bf16[128,128]{1,0:T(8,128)(2,1)S(1)}, bf16[128,128]{1,0:T(8,128)(2,1)S(1)}, u32[]{:S(2)}, u32[]{:S(2)}) collective-permute-start(bf16[128,128]{1,0:T(8,128)(2,1)S(1)} %get-tuple-element.40), channel_id=1, source_target_pairs={{0,1},{7,6},{8,9},{15,14},{16,17},{23,22},{24,25},{31,30},{2,10},{... | collective-permute-start | bytes 98312 | tf_op jit(solution)/shard_map/ppermute | solution.py:568
  8.9 2.5 %collective-permute-done.refs_2_.refs_3_.refs_5_ = bf16[128,128]{1,0:T(8,128)(2,1)S(1)} collective-permute-done((bf16[128,128]{1,0:T(8,128)(2,1)S(1)}, bf16[128,128]{1,0:T(8,128)(2,1)S(1)}, u32[]{:S(2)}, u32[]{:S(2)}) %collective-permute-start) | collective-permute-done | bytes 32800 | tf_op jit(solution)/shard_map/ppermute | solution.py:568
  11.4 2.7 %stage1.1 = (bf16[128,128]{1,0:T(8,128)(2,1)S(1)}, f32[32,128,128]{2,1,0:T(8,128)S(1)}, f32[32,8,128]{2,1,0:T(8,128)S(1)}, bf16[32,128,128]{2,1,0:T(8,128)(2,1)S(1)}) custom-call(f32[2,8,128]{2,1,0:T(8,128)S(1)} %get-tuple-element.36.prices_ref, ...), custom_call_target="tpu_custom_call", output_to_operand_aliasing={{1}: (5, {}), {2}: (6, {}), {3}: (7, {})} | custom-call | tf_op jit(solution)/shard_map/stage1/pallas_call | solution.py:538
  14.1 3.1 %collective-permute-start.1 = (bf16[128,128]{1,0:T(8,128)(2,1)S(1)}, bf16[128,128]{1,0:T(8,128)(2,1)S(1)}, u32[]{:S(2)}, u32[]{:S(2)}) collective-permute-start(bf16[128,128]{1,0:T(8,128)(2,1)S(1)} %get-tuple-element.45), channel_id=1, source_target_pairs={{1,2},{6,5},{9,10},{14,13},{17,18},{22,21},{25,26},{30,29},{0,8},{... | collective-permute-start | bytes 98312 | tf_op jit(solution)/shard_map/ppermute | solution.py:568
  17.2 1.0 %collective-permute-done.1.refs_4_.refs_6_ = bf16[128,128]{1,0:T(8,128)(2,1)S(1)} collective-permute-done((bf16[128,128]{1,0:T(8,128)(2,1)S(1)}, bf16[128,128]{1,0:T(8,128)(2,1)S(1)}, u32[]{:S(2)}, u32[]{:S(2)}) %collective-permute-start.1) | collective-permute-done | bytes 32800 | tf_op jit(solution)/shard_map/ppermute | solution.py:568
  18.2 0.7 stage2.1
  18.9 3.2 %collective-permute-start.2 = (bf16[128,128]{1,0:T(8,128)(2,1)S(1)}, bf16[128,128]{1,0:T(8,128)(2,1)S(1)}, u32[]{:S(2)}, u32[]{:S(2)}) collective-permute-start(bf16[128,128]{1,0:T(8,128)(2,1)S(1)} %get-tuple-element.48), channel_id=1, source_target_pairs={{2,3},{5,4},{10,11},{13,12},{18,19},{21,20},{26,27},{29,28},{8,16}... | collective-permute-start | bytes 98312 | tf_op jit(solution)/shard_map/ppermute | solution.py:568
  22.1 1.0 %collective-permute-done.2.refs_5_.refs_7_ = bf16[128,128]{1,0:T(8,128)(2,1)S(1)} collective-permute-done((bf16[128,128]{1,0:T(8,128)(2,1)S(1)}, bf16[128,128]{1,0:T(8,128)(2,1)S(1)}, u32[]{:S(2)}, u32[]{:S(2)}) %collective-permute-start.2) | collective-permute-done | bytes 32800 | tf_op jit(solution)/shard_map/ppermute | solution.py:568
  23.8 0.7 collective-permute-start.5
  24.5 1.3 %collective-permute-start.4 = (bf16[128,128]{1,0:T(8,128)(2,1)S(1)}, bf16[128,128]{1,0:T(8,128)(2,1)S(1)}, u32[]{:S(2)}, u32[]{:S(2)}) collective-permute-start(bf16[128,128]{1,0:T(8,128)(2,1)S(1)} %get-tuple-element.54), channel_id=1, source_target_pairs={{17,25},{9,1},{18,26},{10,2},{21,29},{13,5},{22,30},{14,6}} | collective-permute-start | bytes 98312 | tf_op jit(solution)/shard_map/ppermute | solution.py:568
  25.8 8.6 %collective-permute-done.4.refs_7_.refs_9_ = bf16[128,128]{1,0:T(8,128)(2,1)S(1)} collective-permute-done((bf16[128,128]{1,0:T(8,128)(2,1)S(1)}, bf16[128,128]{1,0:T(8,128)(2,1)S(1)}, u32[]{:S(2)}, u32[]{:S(2)}) %collective-permute-start.4) | collective-permute-done | bytes 32800 | tf_op jit(solution)/shard_map/ppermute | solution.py:568
  34.4 3.8 %stage5.1 = (bf16[128,128]{1,0:T(8,128)(2,1)S(1)}, f32[32,128,128]{2,1,0:T(8,128)S(1)}, f32[32,8,128]{2,1,0:T(8,128)S(1)}, f32[32,128,128]{2,1,0:T(8,128)S(1)}) custom-call(f32[2,8,128]{2,1,0:T(8,128)S(1)} %get-tuple-element.36.prices_ref, bf16[32,128,128]{2,1,0:T(8,128)(2,1)S(1)} %get-tuple-element.37.costs_ref, ...), custom_call_target="tpu_custom_call", output_to_operand_aliasing={{3}: (11, {})} | custom-call | tf_op jit(solution)/shard_map/stage5/pallas_call | solution.py:538
  38.9 1.3 %collective-permute-start.7 = (bf16[128,128]{1,0:T(8,128)(2,1)S(1)}, bf16[128,128]{1,0:T(8,128)(2,1)S(1)}, u32[]{:S(2)}, u32[]{:S(2)}) collective-permute-start(bf16[128,128]{1,0:T(8,128)(2,1)S(1)} %get-tuple-element.59), channel_id=1, source_target_pairs={{5,6},{2,1},{13,14},{10,9},{21,22},{18,17},{29,30},{26,25},{19,27}... | collective-permute-start | bytes 98312 | tf_op jit(solution)/shard_map/ppermute | solution.py:568
  40.2 7.4 %collective-permute-done.7.refs_9_.refs_11_ = bf16[128,128]{1,0:T(8,128)(2,1)S(1)} collective-permute-done((bf16[128,128]{1,0:T(8,128)(2,1)S(1)}, bf16[128,128]{1,0:T(8,128)(2,1)S(1)}, u32[]{:S(2)}, u32[]{:S(2)}) %collective-permute-start.7) | collective-permute-done | bytes 32800 | tf_op jit(solution)/shard_map/ppermute | solution.py:568
  47.6 2.7 %stage7.1 = (bf16[128,128]{1,0:T(8,128)(2,1)S(1)}, f32[32,128,128]{2,1,0:T(8,128)S(1)}, f32[32,8,128]{2,1,0:T(8,128)S(1)}, f32[32,128,128]{2,1,0:T(8,128)S(1)}) custom-call(f32[2,8,128]{2,1,0:T(8,128)S(1)} %get-tuple-element.36.prices_ref, ...), custom_call_target="tpu_custom_call", output_to_operand_aliasing={{1}: (12, {}), {2}: (13, {}), {3}: (14, {})} | custom-call | tf_op jit(solution)/shard_map/stage7/pallas_call | solution.py:538
  50.3 1.3 %collective-permute-start.8 = (bf16[128,128]{1,0:T(8,128)(2,1)S(1)}, bf16[128,128]{1,0:T(8,128)(2,1)S(1)}, u32[]{:S(2)}, u32[]{:S(2)}) collective-permute-start(bf16[128,128]{1,0:T(8,128)(2,1)S(1)} %get-tuple-element.63), channel_id=1, source_target_pairs={{6,7},{1,0},{14,15},{9,8},{22,23},{17,16},{30,31},{25,24}} | collective-permute-start | bytes 98312 | tf_op jit(solution)/shard_map/ppermute | solution.py:568
  51.6 0.8 %collective-permute-done.8.refs_12_ = bf16[128,128]{1,0:T(8,128)(2,1)S(1)} collective-permute-done((bf16[128,128]{1,0:T(8,128)(2,1)S(1)}, bf16[128,128]{1,0:T(8,128)(2,1)S(1)}, u32[]{:S(2)}, u32[]{:S(2)}) %collective-permute-start.8) | collective-permute-done | bytes 32800 | tf_op jit(solution)/shard_map/ppermute | solution.py:568
  52.4 5.4 %final.1 = (bf16[32,128,128]{2,1,0:T(8,128)(2,1)}, bf16[32,128,128]{2,1,0:T(8,128)(2,1)S(1)}, bf16[16,192,128]{2,1,0:T(8,128)(2,1)S(1)}, f32[32,128,128]{2,1,0:T...) custom-call(f32[2,8,128]{2,1,0:T(8,128)S(1)} %get-tuple-element.36.p, ...), custom_call_target="tpu_custom_call", output_to_operand_aliasing={{3}: (15, {}), {4}: (16, {}), {5}: (17, {})} | custom-call | tf_op jit(solution)/shard_map/final/pallas_call | solution.py:538
  57.8 4.8 %collective-permute-start.9 = (bf16[16,192,128]{2,1,0:T(8,128)(2,1)S(1)}, bf16[16,192,128]{2,1,0:T(8,128)(2,1)S(1)}, u32[]{:S(2)}, u32[]{:S(2)}) collective-permute-start(bf16[16,192,128]{2,1,0:T(8,128)(2,1)S(1)} %get-tuple-element.69), channel_id=1, source_target_pairs={{1,0},{2,1},{3,2},{4,3},{5,4},{6,5},{7,6},{9,8},{10,9},{11,10},{12... | collective-permute-start | bytes 2359304 | tf_op jit(solution)/shard_map/ppermute | solution.py:590
  62.6 8.5 %collective-permute-done.9.packed_ref = bf16[16,192,128]{2,1,0:T(8,128)(2,1)S(1)} collective-permute-done((bf16[16,192,128]{2,1,0:T(8,128)(2,1)S(1)}, bf16[16,192,128]{2,1,0:T(8,128)(2,1)S(1)}, u32[]{:S(2)}, u32[]{:S(2)}) %collective-permute-start.9) | collective-permute-done | bytes 786464 | tf_op jit(solution)/shard_map/ppermute | solution.py:590
  71.1 1.5 %merge.1 = bf16[32,128,128]{2,1,0:T(8,128)(2,1)} custom-call(bf16[32,128,128]{2,1,0:T(8,128)(2,1)S(1)} %get-tuple-element.68.skewed_ref, bf16[16,192,128]{2,1,0:T(8,128)(2,1)S(1)} %collective-permute-done.9.packed_ref), custom_call_target="tpu_custom_call" | custom-call | tf_op jit(solution)/shard_map/merge/pallas_call | solution.py:591
  (9 shorter events, 1.4 us)
Async XLA Ops:
  1.9 1.2 %copy-start = (bf16[32,128,128]{2,1,0:T(8,128)(2,1)S(1)}, bf16[32,128,128]{2,1,0:T(8,128)(2,1)}, u32[]{:S(2)}) copy-start(bf16[32,128,128]{2,1,0:T(8,128)(2,1)} %costs_ref.1) | copy-start | bytes 3145732
  7.6 3.8 %collective-permute-start = (bf16[128,128]{1,0:T(8,128)(2,1)S(1)}, bf16[128,128]{1,0:T(8,128)(2,1)S(1)}, u32[]{:S(2)}, u32[]{:S(2)}) collective-permute-start(bf16[128,128]{1,0:T(8,128)(2,1)S(1)} %get-tuple-element.40), channel_id=1, source_target_pairs={{0,1},{7,6},{8,9},{15,14},{16,17},{23,22},{24,25},{31,30},{2,10},{... | collective-permute-start | bytes 98312 | tf_op jit(solution)/shard_map/ppermute | solution.py:568
  14.1 4.1 %collective-permute-start.1 = (bf16[128,128]{1,0:T(8,128)(2,1)S(1)}, bf16[128,128]{1,0:T(8,128)(2,1)S(1)}, u32[]{:S(2)}, u32[]{:S(2)}) collective-permute-start(bf16[128,128]{1,0:T(8,128)(2,1)S(1)} %get-tuple-element.45), channel_id=1, source_target_pairs={{1,2},{6,5},{9,10},{14,13},{17,18},{22,21},{25,26},{30,29},{0,8},{... | collective-permute-start | bytes 98312 | tf_op jit(solution)/shard_map/ppermute | solution.py:568
  18.9 4.3 %collective-permute-start.2 = (bf16[128,128]{1,0:T(8,128)(2,1)S(1)}, bf16[128,128]{1,0:T(8,128)(2,1)S(1)}, u32[]{:S(2)}, u32[]{:S(2)}) collective-permute-start(bf16[128,128]{1,0:T(8,128)(2,1)S(1)} %get-tuple-element.48), channel_id=1, source_target_pairs={{2,3},{5,4},{10,11},{13,12},{18,19},{21,20},{26,27},{29,28},{8,16}... | collective-permute-start | bytes 98312 | tf_op jit(solution)/shard_map/ppermute | solution.py:568
  23.2 1.3 %collective-permute-start.3 = (bf16[128,128]{1,0:T(8,128)(2,1)S(1)}, bf16[128,128]{1,0:T(8,128)(2,1)S(1)}, u32[]{:S(2)}, u32[]{:S(2)}) collective-permute-start(bf16[128,128]{1,0:T(8,128)(2,1)S(1)} %get-tuple-element.53), channel_id=1, source_target_pairs={{3,4},{11,12},{19,20},{27,28},{16,24},{8,0},{9,17},{17,9},{10,18},... | collective-permute-start | bytes 98312 | tf_op jit(solution)/shard_map/ppermute | solution.py:568
  23.8 2.0 %collective-permute-start.5 = (bf16[128,128]{1,0:T(8,128)(2,1)S(1)}, bf16[128,128]{1,0:T(8,128)(2,1)S(1)}, u32[]{:S(2)}, u32[]{:S(2)}) collective-permute-start(bf16[128,128]{1,0:T(8,128)(2,1)S(1)} %get-tuple-element.53), channel_id=1, source_target_pairs={{4,3},{12,11},{20,19},{28,27}} | collective-permute-start | bytes 98312 | tf_op jit(solution)/shard_map/ppermute | solution.py:571
  24.5 9.9 %collective-permute-start.4 = (bf16[128,128]{1,0:T(8,128)(2,1)S(1)}, bf16[128,128]{1,0:T(8,128)(2,1)S(1)}, u32[]{:S(2)}, u32[]{:S(2)}) collective-permute-start(bf16[128,128]{1,0:T(8,128)(2,1)S(1)} %get-tuple-element.54), channel_id=1, source_target_pairs={{17,25},{9,1},{18,26},{10,2},{21,29},{13,5},{22,30},{14,6}} | collective-permute-start | bytes 98312 | tf_op jit(solution)/shard_map/ppermute | solution.py:568
  38.2 0.7 collective-permute-start.6
  38.9 8.7 %collective-permute-start.7 = (bf16[128,128]{1,0:T(8,128)(2,1)S(1)}, bf16[128,128]{1,0:T(8,128)(2,1)S(1)}, u32[]{:S(2)}, u32[]{:S(2)}) collective-permute-start(bf16[128,128]{1,0:T(8,128)(2,1)S(1)} %get-tuple-element.59), channel_id=1, source_target_pairs={{5,6},{2,1},{13,14},{10,9},{21,22},{18,17},{29,30},{26,25},{19,27}... | collective-permute-start | bytes 98312 | tf_op jit(solution)/shard_map/ppermute | solution.py:568
  50.3 2.1 %collective-permute-start.8 = (bf16[128,128]{1,0:T(8,128)(2,1)S(1)}, bf16[128,128]{1,0:T(8,128)(2,1)S(1)}, u32[]{:S(2)}, u32[]{:S(2)}) collective-permute-start(bf16[128,128]{1,0:T(8,128)(2,1)S(1)} %get-tuple-element.63), channel_id=1, source_target_pairs={{6,7},{1,0},{14,15},{9,8},{22,23},{17,16},{30,31},{25,24}} | collective-permute-start | bytes 98312 | tf_op jit(solution)/shard_map/ppermute | solution.py:568
  57.8 13.3 %collective-permute-start.9 = (bf16[16,192,128]{2,1,0:T(8,128)(2,1)S(1)}, bf16[16,192,128]{2,1,0:T(8,128)(2,1)S(1)}, u32[]{:S(2)}, u32[]{:S(2)}) collective-permute-start(bf16[16,192,128]{2,1,0:T(8,128)(2,1)S(1)} %get-tuple-element.69), channel_id=1, source_target_pairs={{1,0},{2,1},{3,2},{4,3},{5,4},{6,5},{7,6},{9,8},{10,9},{11,10},{12... | collective-permute-start | bytes 2359304 | tf_op jit(solution)/shard_map/ppermute | solution.py:590
